TPU v7x, 32 devices: a whole 2x2x4 slice. The times are simulated.
32 devices in a mesh: section: 2 (over x), ctx: 8 (over z, y), wshard: 2 (over core).
Axes of the slice: x: 2, y: 2, z: 4, core: 2. Of those that a mesh axis runs over, the one named last changes fastest.
Arguments:
- boundary: bfloat16 [2, 4, 2, 1024, 1024], P('section', None, 'wshard', 'ctx'), may hold values from -6 to 6
- segment_ids: int32 [4, 2, 1024], P(None, 'wshard', 'ctx'), may hold values from 0 to 1, never falling along the last dimension, each value on 1 to 768 neighbouring positions
- qkv_weight: bfloat16 [2, 1024, 3072], P('section', ('ctx', 'wshard')), may hold values from -0.1875 to 0.1875
- attn_out_weight: bfloat16 [2, 1024, 1024], P('section', ('ctx', 'wshard')), may hold values from -2 to 2
- ffn_in_weight: bfloat16 [2, 1024, 5248], P('section', ('ctx', 'wshard')), may hold values from -0.1875 to 0.1875
- ffn_out_weight: bfloat16 [2, 2624, 1024], P('section', None, ('ctx', 'wshard')), may hold values from -0.125 to 0.125
- norm_gains: bfloat16 [2, 2, 1024], P('section', None, ('ctx', 'wshard')), may hold values from 0.5 to 1.5
Outputs:
- boundary_out: bfloat16 [2, 4, 2, 1024, 1024], P('section', None, 'wshard', 'ctx')
- grad_qkv: float32 [2, 1024, 3072], P('section', ('ctx', 'wshard'))
- grad_attn_out: float32 [2, 1024, 1024], P('section', ('ctx', 'wshard'))
- grad_ffn_in: float32 [2, 1024, 5248], P('section', ('ctx', 'wshard'))
- grad_ffn_out: float32 [2, 2624, 1024], P('section', None, ('ctx', 'wshard'))
- grad_gains: float32 [2, 2, 1024], P('section', None, ('ctx', 'wshard'))
Inputs may be any that keep to these rules, and one draw needn't show every extreme that they name: `segment_ids`: within each sequence the ids never fall; every id of 0 to 1 holds 1 to 768 tokens.
All inputs are finite; a program needn't handle non-finite values.
Results may differ from a plain program's by a relative error of at most 0.034.
Values may be sent and summed in bfloat16 or wider, within the bound.
No kernel may reach another device: no remote copies, remote signals or barrier semaphores. Data moves between devices by JAX's collectives and lax.ppermute only.
A program may use at most 320 MiB of HBM per device.

v0:
```python
from functools import partial

import jax
import jax.numpy as jnp
from jax import lax
from jax.sharding import PartitionSpec as P

D = 1024
HEADS = 16
HEAD_DIM = 64
FF = 2624


EPSILON = 1e-05
ROPE_BASE = 160000.0
NEG_FILL = -1e30


def shifted(array, axis, by):
    count = lax.axis_size(axis)
    pairs = [(i, i + by) for i in range(count) if 0 <= i + by < count]
    return lax.ppermute(array, axis, pairs)


def norm_rows(values, gain_row):
    center = values - jnp.mean(values, axis=-1, keepdims=True)
    spread = jnp.mean(center * center, axis=-1, keepdims=True)
    return center * lax.rsqrt(spread + EPSILON) * gain_row


def positions_of(segment):
    places = jnp.arange(segment.shape[0], dtype=jnp.int32)
    begins = jnp.concatenate([jnp.ones((1,), dtype=jnp.bool_), segment[1:] != segment[:-1]])
    firsts = lax.cummax(jnp.where(begins, places, 0), axis=0)
    return places - firsts


def rotate(heads_in, position):
    half_width = heads_in.shape[-1] // 2
    exponent = jnp.arange(half_width, dtype=jnp.float32) * (-2.0 / heads_in.shape[-1])
    angles = position.astype(jnp.float32)[:, None] * (ROPE_BASE**exponent)[None, :]
    cosine = jnp.cos(angles)[:, None, :]
    sine_part = jnp.sin(angles)[:, None, :]
    first_half = heads_in[..., :half_width]
    second_half = heads_in[..., half_width:]
    return jnp.concatenate(
        [
            first_half * cosine - second_half * sine_part,
            second_half * cosine + first_half * sine_part,
        ],
        axis=-1,
    )


def rotate_pair(query_raw, key_raw, position):
    return (rotate(query_raw, position), rotate(key_raw, position))


def geglu(upward):
    split_at = upward.shape[-1] // 2
    return jax.nn.gelu(upward[:, :split_at], approximate=False) * upward[:, split_at:]


def take_slot(stack, index):
    return lax.dynamic_index_in_dim(stack, index, 0, keepdims=False)


def put_slot(stack, value, index):
    return lax.dynamic_update_index_in_dim(stack, value, index, 0)


def contract_rows(left, right):
    return lax.dot_general(
        left, right, (((0,), (0,)), ((), ())), preferred_element_type=jnp.float32
    )


def contract_cols(left, right):
    return lax.dot_general(
        left, right, (((1,), (1,)), ((), ())), preferred_element_type=jnp.float32
    )


def front_pass(inputs, position, weights):
    tok_rows = inputs.shape[0]
    gain_rows = weights[4].astype(jnp.float32)
    normed = norm_rows(inputs, gain_rows[0]).astype(jnp.bfloat16)
    mixed_rows = jnp.dot(normed, weights[0], preferred_element_type=jnp.float32)
    query_raw = mixed_rows[:, :D].reshape(tok_rows, HEADS, HEAD_DIM)
    key_raw = mixed_rows[:, D : 2 * D].reshape(tok_rows, HEADS, HEAD_DIM)
    queries = rotate(query_raw, position).astype(jnp.bfloat16)
    key_rot = rotate(key_raw, position).reshape(tok_rows, D).astype(jnp.bfloat16)
    value_rows = mixed_rows[:, 2 * D :].astype(jnp.bfloat16)
    return (normed, query_raw, key_raw, queries, key_rot, value_rows)


def fold_piece(queries, seg_query, seg_keys, running, key_piece, piece_start):
    row_top, row_total, weighted = running
    key_rows, value_rows = key_piece
    piece_rows = key_rows.shape[0]
    scores = jnp.einsum(
        "qhd,khd->hqk",
        queries,
        key_rows.reshape(piece_rows, HEADS, HEAD_DIM),
        preferred_element_type=jnp.float32,
    ) * HEAD_DIM ** (-0.5)
    allowed = (seg_query[:, None] == seg_keys[None, :])[None]
    scores = jnp.where(allowed, scores, NEG_FILL)
    new_top = jnp.maximum(row_top, jnp.max(scores, axis=-1))
    exp_terms = jnp.where(allowed, jnp.exp(scores - new_top[:, :, None]), 0.0)
    row_total = jnp.sum(exp_terms, axis=-1)
    part_sum = jnp.einsum(
        "hqk,khd->qhd",
        exp_terms.astype(jnp.bfloat16),
        value_rows.reshape(piece_rows, HEADS, HEAD_DIM),
        preferred_element_type=jnp.float32,
    )
    weighted = part_sum
    return (new_top, row_total, weighted)


def attend_back(
    queries, seg_query, seg_keys, key_whole, value_whole, row_top, row_total, grad_scaled, row_delta
):
    seq_length = key_whole.shape[0]
    key_block = max(min(512, seq_length), seq_length // 16)
    block_count = seq_length // key_block
    key_blocks = key_whole.reshape(block_count, key_block, HEADS, HEAD_DIM)
    value_blocks = value_whole.reshape(block_count, key_block, HEADS, HEAD_DIM)
    seg_blocks = seg_keys.reshape(block_count, key_block)
    scale = HEAD_DIM ** (-0.5)
    share = row_delta / row_total

    def one_block(grad_query_acc, block_item):
        key_rows, value_rows, seg_piece = block_item
        scores = (
            jnp.einsum("qhd,khd->hqk", queries, key_rows, preferred_element_type=jnp.float32)
            * scale
        )
        allowed = (seg_query[:, None] == seg_piece[None, :])[None]
        exp_terms = jnp.where(allowed, jnp.exp(scores - row_top[:, :, None]), 0.0)
        grad_exp = jnp.einsum(
            "qhd,khd->hqk", grad_scaled, value_rows, preferred_element_type=jnp.float32
        )
        grad_scores = (exp_terms * (grad_exp - share[:, :, None]) * scale).astype(jnp.bfloat16)
        grad_query_acc = grad_query_acc + jnp.einsum(
            "hqk,khd->qhd", grad_scores, key_rows, preferred_element_type=jnp.float32
        )
        key_terms = jnp.einsum(
            "hqk,qhd->khd", grad_scores, queries, preferred_element_type=jnp.float32
        )
        value_terms = jnp.einsum(
            "hqk,qhd->khd",
            exp_terms.astype(jnp.bfloat16),
            grad_scaled,
            preferred_element_type=jnp.float32,
        )
        return (
            grad_query_acc,
            (key_terms.reshape(key_block, D), value_terms.reshape(key_block, D)),
        )

    start_query = jnp.zeros(queries.shape, jnp.float32)
    grad_queries, block_terms = lax.scan(
        one_block, start_query, (key_blocks, value_blocks, seg_blocks)
    )
    return (
        grad_queries,
        block_terms[0].reshape(seq_length, D),
        block_terms[1].reshape(seq_length, D),
    )


def body(
    boundary, segment_ids, qkv_weight, attn_out_weight, ffn_in_weight, ffn_out_weight, norm_gains
):
    section_index = lax.axis_index("section")
    micro_count = boundary.shape[1]
    tok_rows = boundary.shape[3]
    local_rows = boundary[0, :, 0]
    seg_local = segment_ids[:, 0]
    seg_whole = lax.all_gather(seg_local, "ctx", axis=1, tiled=True)
    pos_whole = jax.vmap(positions_of)(seg_whole)
    pos_local = lax.dynamic_slice_in_dim(pos_whole, lax.axis_index("ctx") * tok_rows, tok_rows, 1)
    shards = (qkv_weight[0], attn_out_weight[0], ffn_in_weight[0], ffn_out_weight[0], norm_gains[0])
    weights = (
        lax.all_gather(shards[0], ("ctx", "wshard"), axis=0, tiled=True),
        lax.all_gather(shards[1], ("ctx", "wshard"), axis=0, tiled=True),
        lax.all_gather(shards[2], ("ctx", "wshard"), axis=0, tiled=True),
        lax.all_gather(shards[3], ("ctx", "wshard"), axis=1, tiled=True),
        lax.all_gather(shards[4], ("ctx", "wshard"), axis=1, tiled=True),
    )
    gain_rows = weights[4].astype(jnp.float32)
    empty_rows = jnp.zeros((tok_rows, D), jnp.bfloat16)
    kept_inputs = jnp.zeros((micro_count, tok_rows, D), jnp.bfloat16)
    kept_attn = jnp.zeros((micro_count, tok_rows, HEADS, HEAD_DIM), jnp.float32)
    kept_top = jnp.zeros((micro_count, HEADS, tok_rows), jnp.float32)
    kept_total = jnp.ones((micro_count, HEADS, tok_rows), jnp.float32)
    outputs = jnp.zeros((micro_count, tok_rows, D), jnp.bfloat16)
    received = empty_rows
    for timestep in range(micro_count + 1):
        slot_index = jnp.clip(timestep - section_index, 0, micro_count - 1)
        inputs_low = jnp.where(section_index == 0, take_slot(local_rows, slot_index), received)
        seg_query = take_slot(seg_local, slot_index)
        seg_keys = take_slot(seg_whole, slot_index)
        position = take_slot(pos_local, slot_index)
        inputs = inputs_low.astype(jnp.float32)
        normed, query_raw, key_raw, queries, key_rot, value_rows = front_pass(
            inputs, position, weights
        )
        start_carry = (
            jnp.full((HEADS, tok_rows), NEG_FILL, jnp.float32),
            jnp.zeros((HEADS, tok_rows), jnp.float32),
            jnp.zeros((tok_rows, HEADS, HEAD_DIM), jnp.float32),
        )
        folder = partial(fold_piece, queries, seg_query, seg_keys)
        row_top, row_total, weighted = folder(
            start_carry,
            (
                lax.all_gather(key_rot, "ctx", axis=0, tiled=True),
                lax.all_gather(value_rows, "ctx", axis=0, tiled=True),
            ),
            jnp.int32(0),
        )
        attended = weighted / jnp.transpose(row_total)[:, :, None]
        attn_low = attended.reshape(tok_rows, D).astype(jnp.bfloat16)
        hidden = inputs + jnp.dot(attn_low, weights[1], preferred_element_type=jnp.float32)
        second = norm_rows(hidden, gain_rows[1]).astype(jnp.bfloat16)
        upward = jnp.dot(second, weights[2], preferred_element_type=jnp.float32)
        activated = geglu(upward).astype(jnp.bfloat16)
        result = hidden + jnp.dot(activated, weights[3], preferred_element_type=jnp.float32)
        result_low = result.astype(jnp.bfloat16)
        kept_inputs = put_slot(kept_inputs, inputs_low, slot_index)
        kept_attn = put_slot(kept_attn, attended, slot_index)
        kept_top = put_slot(kept_top, row_top, slot_index)
        kept_total = put_slot(kept_total, row_total, slot_index)
        outputs = put_slot(outputs, result_low, slot_index)
        if timestep < micro_count:
            received = shifted(result_low, "section", 1)
    back_weights = (
        lax.all_gather(shards[0], ("ctx", "wshard"), axis=0, tiled=True),
        lax.all_gather(shards[1], ("ctx", "wshard"), axis=0, tiled=True),
        lax.all_gather(shards[2], ("ctx", "wshard"), axis=0, tiled=True),
        lax.all_gather(shards[3], ("ctx", "wshard"), axis=1, tiled=True),
        lax.all_gather(shards[4], ("ctx", "wshard"), axis=1, tiled=True),
    )
    back_gain = back_weights[4].astype(jnp.float32)
    grad_qkv = jnp.zeros((D, 3 * D), jnp.float32)
    grad_attn = jnp.zeros((D, D), jnp.float32)
    grad_in = jnp.zeros((D, 2 * FF), jnp.float32)
    grad_back = jnp.zeros((FF, D), jnp.float32)
    grad_gain = jnp.zeros((2, D), jnp.float32)
    input_grads = jnp.zeros((micro_count, tok_rows, D), jnp.bfloat16)
    received = empty_rows
    for timestep in range(micro_count + 1):
        order_index = timestep - 1 + section_index
        slot_index = jnp.clip(order_index, 0, micro_count - 1)
        live_turn = (order_index >= 0) & (order_index < micro_count)
        incoming = jnp.where(section_index == 1, take_slot(local_rows, slot_index), received)
        incoming = jnp.where(live_turn, incoming, jnp.zeros_like(incoming))
        seg_query = take_slot(seg_local, slot_index)
        seg_keys = take_slot(seg_whole, slot_index)
        position = take_slot(pos_local, slot_index)
        inputs = take_slot(kept_inputs, slot_index).astype(jnp.float32)
        normed, query_raw, key_raw, queries, key_rot, value_rows = front_pass(
            inputs, position, back_weights
        )
        attended = take_slot(kept_attn, slot_index)
        row_top = take_slot(kept_top, slot_index)
        row_total = take_slot(kept_total, slot_index)
        attn_low = attended.reshape(tok_rows, D).astype(jnp.bfloat16)
        hidden = inputs + jnp.dot(attn_low, back_weights[1], preferred_element_type=jnp.float32)
        second = norm_rows(hidden, back_gain[1]).astype(jnp.bfloat16)
        upward = jnp.dot(second, back_weights[2], preferred_element_type=jnp.float32)
        activated = geglu(upward).astype(jnp.bfloat16)
        grad_back = grad_back + contract_rows(activated, incoming)
        grad_act = contract_cols(incoming, back_weights[3])
        grad_up = jax.vjp(geglu, upward)[1](grad_act)[0].astype(jnp.bfloat16)
        grad_in = grad_in + contract_rows(second, grad_up)
        grad_second = contract_cols(grad_up, back_weights[2])
        pull_second = jax.vjp(norm_rows, hidden, back_gain[1])[1]
        grad_hidden_part, grad_gain_second = pull_second(grad_second)
        grad_hidden = incoming.astype(jnp.float32) + grad_hidden_part
        hidden_low = grad_hidden.astype(jnp.bfloat16)
        grad_attn = grad_attn + contract_rows(attn_low, hidden_low)
        grad_attended = contract_cols(hidden_low, back_weights[1]).reshape(
            tok_rows, HEADS, HEAD_DIM
        )
        row_delta = jnp.transpose(jnp.sum(grad_attended * attended, axis=-1))
        grad_scaled = (grad_attended / jnp.transpose(row_total)[:, :, None]).astype(jnp.bfloat16)
        key_whole, value_whole = (
            lax.all_gather(key_rot, "ctx", axis=0, tiled=True),
            lax.all_gather(value_rows, "ctx", axis=0, tiled=True),
        )
        grad_queries, key_terms, value_terms = attend_back(
            queries,
            seg_query,
            seg_keys,
            key_whole,
            value_whole,
            row_top,
            row_total,
            grad_scaled,
            row_delta,
        )
        grad_keys, grad_values = (
            lax.psum_scatter(
                key_terms.astype(jnp.bfloat16), "ctx", scatter_dimension=0, tiled=True
            ).astype(jnp.float32),
            lax.psum_scatter(
                value_terms.astype(jnp.bfloat16), "ctx", scatter_dimension=0, tiled=True
            ).astype(jnp.float32),
        )
        pull_rope = jax.vjp(partial(rotate_pair, position=position), query_raw, key_raw)[1]
        grad_query_raw, grad_key_raw = pull_rope(
            (grad_queries, grad_keys.reshape(tok_rows, HEADS, HEAD_DIM))
        )
        grad_mixed = jnp.concatenate(
            [grad_query_raw.reshape(tok_rows, D), grad_key_raw.reshape(tok_rows, D), grad_values],
            axis=1,
        ).astype(jnp.bfloat16)
        grad_qkv = grad_qkv + contract_rows(normed, grad_mixed)
        grad_normed = contract_cols(grad_mixed, back_weights[0])
        pull_first = jax.vjp(norm_rows, inputs, back_gain[0])[1]
        grad_inputs_part, grad_gain_first = pull_first(grad_normed)
        grad_inputs = grad_hidden + grad_inputs_part
        grad_gain = grad_gain + jnp.stack([grad_gain_first, grad_gain_second])
        grad_inputs_low = grad_inputs.astype(jnp.bfloat16)
        input_grads = put_slot(input_grads, grad_inputs_low, slot_index)
        if timestep < micro_count:
            received = shifted(grad_inputs_low, "section", -1)
    boundary_local = jnp.where(section_index == 0, input_grads, outputs)[None, :, None]
    grad_sums = (
        lax.psum_scatter(grad_qkv, ("ctx", "wshard"), scatter_dimension=0, tiled=True),
        lax.psum_scatter(grad_attn, ("ctx", "wshard"), scatter_dimension=0, tiled=True),
        lax.psum_scatter(grad_in, ("ctx", "wshard"), scatter_dimension=0, tiled=True),
        lax.psum_scatter(grad_back, ("ctx", "wshard"), scatter_dimension=1, tiled=True),
        lax.psum_scatter(grad_gain, ("ctx", "wshard"), scatter_dimension=1, tiled=True),
    )
    return (
        boundary_local,
        grad_sums[0][None],
        grad_sums[1][None],
        grad_sums[2][None],
        grad_sums[3][None],
        grad_sums[4][None],
    )


def solution(mesh):
    placed = (
        P("section", None, "wshard", "ctx", None),
        P(None, "wshard", "ctx"),
        P("section", ("ctx", "wshard"), None),
        P("section", ("ctx", "wshard"), None),
        P("section", ("ctx", "wshard"), None),
        P("section", None, ("ctx", "wshard")),
        P("section", None, ("ctx", "wshard")),
    )
    return jax.shard_map(
        body,
        mesh=mesh,
        in_specs=placed,
        out_specs=(
            P("section", None, "wshard", "ctx", None),
            P("section", ("ctx", "wshard"), None),
            P("section", ("ctx", "wshard"), None),
            P("section", ("ctx", "wshard"), None),
            P("section", None, ("ctx", "wshard")),
            P("section", None, ("ctx", "wshard")),
        ),
        check_vma=False,
    )
```

profile of v0, /device:TPU:13, one launch (start us, length us, event | category | flops | bytes accessed | tf_op | source)
XLA Modules:
  0.0 3121.5 jit_solution(7396680927561402097)
XLA Ops:
  128.0 48.3 %all-gather.33.cloned.1.call-done = bf16[1024,1024]{0,1:T(8,128)(2,1)} async-done(((bf16[128,1024]{0,1:T(8,128)(2,1)}), bf16[1024,1024]{0,1:T(8,128)(2,1)}) %all-gather.33.cloned.1.call-update) | async-done | bytes 2097168 | tf_op jit(solution)/shard_map/all_gather | solution.py:220
  221.8 87.9 %all-gather.75.cloned.1.call-done = bf16[1,1024,5248]{2,1,0:T(8,128)(2,1)} async-done(((bf16[1,64,5248]{2,1,0:T(8,128)(2,1)}), bf16[1,1024,5248]{2,1,0:T(8,128)(2,1)}) %all-gather.75.cloned.1.call-update) | async-done | bytes 10747920 | tf_op jit(solution)/shard_map/all_gather | solution.py:189
  316.9 51.6 %all-gather.77.cloned.1.call-done = bf16[1,2624,1024]{1,2,0:T(8,128)(2,1)} async-done(((bf16[1,2624,64]{1,2,0:T(8,128)(2,1)}), bf16[1,2624,1024]{1,2,0:T(8,128)(2,1)}) %all-gather.77.cloned.1.call-update) | async-done | bytes 5373968 | tf_op jit(solution)/shard_map/all_gather | solution.py:190
  395.7 47.8 %all-gather.37.cloned.1.call-done = bf16[1024,1024]{0,1:T(8,128)(2,1)} async-done(((bf16[128,1024]{0,1:T(8,128)(2,1)}), bf16[1024,1024]{0,1:T(8,128)(2,1)}) %all-gather.37.cloned.1.call-update) | async-done | bytes 2097168 | tf_op jit(solution)/shard_map/all_gather | solution.py:220
  452.7 42.2 %all-gather.35.cloned.1.call-done = bf16[1024,1024]{1,0:T(8,128)(2,1)} async-done(((bf16[128,1024]{1,0:T(8,128)(2,1)}), bf16[1024,1024]{1,0:T(8,128)(2,1)}) %all-gather.35.cloned.1.call-update) | async-done | bytes 2097168 | tf_op jit(solution)/shard_map/all_gather | solution.py:221
  534.7 49.1 %all-gather.41.cloned.1.call-done = bf16[1024,1024]{0,1:T(8,128)(2,1)} async-done(((bf16[128,1024]{0,1:T(8,128)(2,1)}), bf16[1024,1024]{0,1:T(8,128)(2,1)}) %all-gather.41.cloned.1.call-update) | async-done | bytes 2097168 | tf_op jit(solution)/shard_map/all_gather | solution.py:220
  593.1 41.8 %all-gather.39.cloned.1.call-done = bf16[1024,1024]{1,0:T(8,128)(2,1)} async-done(((bf16[128,1024]{1,0:T(8,128)(2,1)}), bf16[1024,1024]{1,0:T(8,128)(2,1)}) %all-gather.39.cloned.1.call-update) | async-done | bytes 2097168 | tf_op jit(solution)/shard_map/all_gather | solution.py:221
  674.6 49.3 %all-gather.45.cloned.1.call-done = bf16[1024,1024]{0,1:T(8,128)(2,1)} async-done(((bf16[128,1024]{0,1:T(8,128)(2,1)}), bf16[1024,1024]{0,1:T(8,128)(2,1)}) %all-gather.45.cloned.1.call-update) | async-done | bytes 2097168 | tf_op jit(solution)/shard_map/all_gather | solution.py:220
  818.8 43.5 %all-gather.49.cloned.1.call-done = bf16[1024,1024]{0,1:T(8,128)(2,1)} async-done(((bf16[128,1024]{0,1:T(8,128)(2,1)}), bf16[1024,1024]{0,1:T(8,128)(2,1)}) %all-gather.49.cloned.1.call-update) | async-done | bytes 2097168 | tf_op jit(solution)/shard_map/all_gather | solution.py:220
  1009.8 42.7 %all-gather.53.cloned.1.call-done = bf16[1024,1024]{1,0:T(8,128)(2,1)} async-done(((bf16[128,1024]{1,0:T(8,128)(2,1)}), bf16[1024,1024]{1,0:T(8,128)(2,1)}) %all-gather.53.cloned.1.call-update) | async-done | bytes 2097168 | tf_op jit(solution)/shard_map/all_gather | solution.py:293
  1067.7 42.2 %while.75 = (s32[]{:T(128)}, f32[128,16,64]{0,2,1:T(8,128)}, bf16[2,512,1024]{2,1,0:T(8,128)(2,1)}, bf16[2,512,1024]{2,1,0:T(8,128)(2,1)}, bf16[2,512,16,64]{1,3...) while((s32[]{:T(128)}, f32[128,16,64]{0,2,1:T(8,128)}, ...), condition=%wide.region_38.39_spmd.clone, body=%wide.region_37.38_spmd.clone.sunk | while | flops 682950656 | bytes 51608288 | solution.py:164
  1111.0 64.9 %reduce-scatter.18.cloned.1.call-done = bf16[128,1024]{1,0:T(8,128)(2,1)} async-done(((bf16[1024,1024]{1,0:T(8,128)(2,1)}), bf16[128,1024]{1,0:T(8,128)(2,1)}) %reduce-scatter.18.cloned.1.call-update) | async-done | bytes 262160 | tf_op jit(solution)/shard_map/reduce_scatter | solution.py:307
  1183.5 62.6 %reduce-scatter.20.cloned.1.call-done = bf16[128,1024]{1,0:T(8,128)(2,1)} async-done(((bf16[1024,1024]{1,0:T(8,128)(2,1)}), bf16[128,1024]{1,0:T(8,128)(2,1)}) %reduce-scatter.20.cloned.1.call-update) | async-done | bytes 262160 | tf_op jit(solution)/shard_map/reduce_scatter | solution.py:310
  1323.1 42.5 %all-gather.57.cloned.1.call-done = bf16[1024,1024]{1,0:T(8,128)(2,1)} async-done(((bf16[128,1024]{1,0:T(8,128)(2,1)}), bf16[1024,1024]{1,0:T(8,128)(2,1)}) %all-gather.57.cloned.1.call-update) | async-done | bytes 2097168 | tf_op jit(solution)/shard_map/all_gather | solution.py:293
  1380.8 42.2 %while.76 = (s32[]{:T(128)}, f32[128,16,64]{0,2,1:T(8,128)}, bf16[2,512,1024]{2,1,0:T(8,128)(2,1)}, bf16[2,512,1024]{2,1,0:T(8,128)(2,1)}, bf16[2,512,16,64]{1,3...) while((s32[]{:T(128)}, f32[128,16,64]{0,2,1:T(8,128)}, ...), condition=%wide.region_51.52_spmd.clone, body=%wide.region_50.51_spmd.clone.sunk | while | flops 682950656 | bytes 51608288 | solution.py:164
  1423.9 65.2 %reduce-scatter.22.cloned.1.call-done = bf16[128,1024]{1,0:T(8,128)(2,1)} async-done(((bf16[1024,1024]{1,0:T(8,128)(2,1)}), bf16[128,1024]{1,0:T(8,128)(2,1)}) %reduce-scatter.22.cloned.1.call-update) | async-done | bytes 262160 | tf_op jit(solution)/shard_map/reduce_scatter | solution.py:307
  1496.6 62.6 %reduce-scatter.24.cloned.1.call-done = bf16[128,1024]{1,0:T(8,128)(2,1)} async-done(((bf16[1024,1024]{1,0:T(8,128)(2,1)}), bf16[128,1024]{1,0:T(8,128)(2,1)}) %reduce-scatter.24.cloned.1.call-update) | async-done | bytes 262160 | tf_op jit(solution)/shard_map/reduce_scatter | solution.py:310
  1636.2 42.6 %all-gather.61.cloned.1.call-done = bf16[1024,1024]{1,0:T(8,128)(2,1)} async-done(((bf16[128,1024]{1,0:T(8,128)(2,1)}), bf16[1024,1024]{1,0:T(8,128)(2,1)}) %all-gather.61.cloned.1.call-update) | async-done | bytes 2097168 | tf_op jit(solution)/shard_map/all_gather | solution.py:293
  1693.9 42.2 %while.77 = (s32[]{:T(128)}, f32[128,16,64]{0,2,1:T(8,128)}, bf16[2,512,1024]{2,1,0:T(8,128)(2,1)}, bf16[2,512,1024]{2,1,0:T(8,128)(2,1)}, bf16[2,512,16,64]{1,3...) while((s32[]{:T(128)}, f32[128,16,64]{0,2,1:T(8,128)}, ...), condition=%wide.region_64.65_spmd.clone, body=%wide.region_63.64_spmd.clone.sunk | while | flops 682950656 | bytes 51608288 | solution.py:164
  1736.9 65.4 %reduce-scatter.26.cloned.1.call-done = bf16[128,1024]{1,0:T(8,128)(2,1)} async-done(((bf16[1024,1024]{1,0:T(8,128)(2,1)}), bf16[128,1024]{1,0:T(8,128)(2,1)}) %reduce-scatter.26.cloned.1.call-update) | async-done | bytes 262160 | tf_op jit(solution)/shard_map/reduce_scatter | solution.py:307
  1809.8 62.6 %reduce-scatter.28.cloned.1.call-done = bf16[128,1024]{1,0:T(8,128)(2,1)} async-done(((bf16[1024,1024]{1,0:T(8,128)(2,1)}), bf16[128,1024]{1,0:T(8,128)(2,1)}) %reduce-scatter.28.cloned.1.call-update) | async-done | bytes 262160 | tf_op jit(solution)/shard_map/reduce_scatter | solution.py:310
  1949.5 42.5 %all-gather.65.cloned.1.call-done = bf16[1024,1024]{1,0:T(8,128)(2,1)} async-done(((bf16[128,1024]{1,0:T(8,128)(2,1)}), bf16[1024,1024]{1,0:T(8,128)(2,1)}) %all-gather.65.cloned.1.call-update) | async-done | bytes 2097168 | tf_op jit(solution)/shard_map/all_gather | solution.py:293
  2007.1 42.2 %while.78 = (s32[]{:T(128)}, f32[128,16,64]{0,2,1:T(8,128)}, bf16[2,512,1024]{2,1,0:T(8,128)(2,1)}, bf16[2,512,1024]{2,1,0:T(8,128)(2,1)}, bf16[2,512,16,64]{1,3...) while((s32[]{:T(128)}, f32[128,16,64]{0,2,1:T(8,128)}, ...), condition=%wide.region_77.78_spmd.clone, body=%wide.region_76.77_spmd.clone.sunk | while | flops 682950656 | bytes 51608288 | solution.py:164
  2050.0 65.3 %reduce-scatter.30.cloned.1.call-done = bf16[128,1024]{1,0:T(8,128)(2,1)} async-done(((bf16[1024,1024]{1,0:T(8,128)(2,1)}), bf16[128,1024]{1,0:T(8,128)(2,1)}) %reduce-scatter.30.cloned.1.call-update) | async-done | bytes 262160 | tf_op jit(solution)/shard_map/reduce_scatter | solution.py:307
  2122.9 62.3 %reduce-scatter.32.cloned.1.call-done = bf16[128,1024]{1,0:T(8,128)(2,1)} async-done(((bf16[1024,1024]{1,0:T(8,128)(2,1)}), bf16[128,1024]{1,0:T(8,128)(2,1)}) %reduce-scatter.32.cloned.1.call-update) | async-done | bytes 262160 | tf_op jit(solution)/shard_map/reduce_scatter | solution.py:310
  2259.3 45.6 %all-gather.69.cloned.1.call-done = bf16[1024,1024]{1,0:T(8,128)(2,1)} async-done(((bf16[128,1024]{1,0:T(8,128)(2,1)}), bf16[1024,1024]{1,0:T(8,128)(2,1)}) %all-gather.69.cloned.1.call-update) | async-done | bytes 2097168 | tf_op jit(solution)/shard_map/all_gather | solution.py:293
  2366.2 53.7 %reduce-scatter.34.cloned.1.call-done = bf16[128,1024]{1,0:T(8,128)(2,1)} async-done(((bf16[1024,1024]{1,0:T(8,128)(2,1)}), bf16[128,1024]{1,0:T(8,128)(2,1)}) %reduce-scatter.34.cloned.1.call-update) | async-done | bytes 262160 | tf_op jit(solution)/shard_map/reduce_scatter | solution.py:307
  2424.1 66.0 %reduce-scatter.36.cloned.1.call-done = bf16[128,1024]{1,0:T(8,128)(2,1)} async-done(((bf16[1024,1024]{1,0:T(8,128)(2,1)}), bf16[128,1024]{1,0:T(8,128)(2,1)}) %reduce-scatter.36.cloned.1.call-update) | async-done | bytes 262160 | tf_op jit(solution)/shard_map/reduce_scatter | solution.py:310
  2642.4 41.5 %add_add_fusion = f32[1024,5248]{1,0:T(8,128)} fusion(f32[1024,5248]{1,0:T(8,128)} %fusion.767, f32[1024,5248]{1,0:T(8,128)} %fusion.766, f32[1024,5248]{1,0:T(8,128)} %fusion.764, f32[1024,5248]{1,0:T(8,128)} %fusion.765, f32[128,2624]{1,0:T(8,128)} %copy-done.60, f32[128,2624]{1,0:T(8,128)} %copy-done.81, f32[128,1024]{1,0:T(8,128)S(1)} %copy-done.24, ...), kind=kOutput, calls=%fused_computation.140 | convolution fusion | flops 1399095296 | bytes 110695424 | tf_op jit(solution)/shard_map/dot_general | solution.py:73
  2702.3 54.7 %reduce-scatter.44.cloned.1.call-done = f32[2624,64]{0,1:T(8,128)} async-done(((f32[2624,1024]{0,1:T(8,128)}), f32[2624,64]{0,1:T(8,128)}) %reduce-scatter.44.cloned.1.call-update) | async-done | bytes 671760 | tf_op jit(solution)/shard_map/reduce_scatter | solution.py:337
  2757.0 139.0 %reduce-scatter.38.cloned.1.call-done = f32[64,3072]{1,0:T(8,128)} async-done(((f32[1024,3072]{1,0:T(8,128)}), f32[64,3072]{1,0:T(8,128)}) %reduce-scatter.38.cloned.1.call-update) | async-done | bytes 786448 | tf_op jit(solution)/shard_map/reduce_scatter | solution.py:334
  2896.1 218.4 %reduce-scatter.42.cloned.1.call-done = f32[64,5248]{1,0:T(8,128)} async-done(((f32[1024,5248]{1,0:T(8,128)}), f32[64,5248]{1,0:T(8,128)}) %reduce-scatter.42.cloned.1.call-update) | async-done | bytes 1343504 | tf_op jit(solution)/shard_map/reduce_scatter | solution.py:336
  (1422 shorter events, 1373.6 us)
Async XLA Ops:
  7.9 117.2 %all-gather.31.cloned.1.call-start = ((), (), s32[]{:S(2)}) async-start(), calls=%async_computation.15 | async-start | bytes 2359296 | tf_op jit(solution)/shard_map/all_gather | solution.py:221
  96.8 122.5 %all-gather.73.cloned.1.call-start = ((), (), s32[]{:S(2)}) async-start(), calls=%async_computation.50 | async-start | bytes 2228224 | tf_op jit(solution)/shard_map/all_gather | solution.py:188
  97.4 212.3 %all-gather.75.cloned.1.call-start = ((), (), s32[]{:S(2)}) async-start(), calls=%async_computation.51 | async-start | bytes 11419648 | tf_op jit(solution)/shard_map/all_gather | solution.py:189
  98.0 270.5 %all-gather.77.cloned.1.call-start = ((), (), s32[]{:S(2)}) async-start(), calls=%async_computation.52 | async-start | bytes 5849088 | tf_op jit(solution)/shard_map/all_gather | solution.py:190
  98.5 345.0 %all-gather.37.cloned.1.call-start = ((), (), s32[]{:S(2)}) async-start(), calls=%async_computation.18 | async-start | bytes 2359296 | tf_op jit(solution)/shard_map/all_gather | solution.py:220
  394.3 100.6 %all-gather.35.cloned.1.call-start = ((), (), s32[]{:S(2)}) async-start(), calls=%async_computation.17 | async-start | bytes 2359296 | tf_op jit(solution)/shard_map/all_gather | solution.py:221
  395.1 188.6 %all-gather.41.cloned.1.call-start = ((), (), s32[]{:S(2)}) async-start(), calls=%async_computation.20 | async-start | bytes 2359296 | tf_op jit(solution)/shard_map/all_gather | solution.py:220
  532.4 102.5 %all-gather.39.cloned.1.call-start = ((), (), s32[]{:S(2)}) async-start(), calls=%async_computation.19 | async-start | bytes 2359296 | tf_op jit(solution)/shard_map/all_gather | solution.py:221
  534.3 189.6 %all-gather.45.cloned.1.call-start = ((), (), s32[]{:S(2)}) async-start(), calls=%async_computation.22 | async-start | bytes 2359296 | tf_op jit(solution)/shard_map/all_gather | solution.py:220
  672.5 102.5 %all-gather.43.cloned.1.call-start = ((), (), s32[]{:S(2)}) async-start(), calls=%async_computation.21 | async-start | bytes 2359296 | tf_op jit(solution)/shard_map/all_gather | solution.py:221
  674.4 187.9 %all-gather.49.cloned.1.call-start = ((), (), s32[]{:S(2)}) async-start(), calls=%async_computation.24 | async-start | bytes 2359296 | tf_op jit(solution)/shard_map/all_gather | solution.py:220
  811.0 101.9 %all-gather.47.cloned.1.call-start = ((), (), s32[]{:S(2)}) async-start(), calls=%async_computation.23 | async-start | bytes 2359296 | tf_op jit(solution)/shard_map/all_gather | solution.py:221
  812.8 189.1 %all-gather.51.cloned.1.call-start = ((), (), s32[]{:S(2)}) async-start(), calls=%async_computation.25 | async-start | bytes 2359296 | tf_op jit(solution)/shard_map/all_gather | solution.py:292
  955.2 220.7 %reduce-scatter.18.cloned.1.call-start = ((), (), s32[]{:S(2)}) async-start(), calls=%async_computation.27 | async-start | bytes 2359296 | tf_op jit(solution)/shard_map/reduce_scatter | solution.py:307
  1109.9 136.2 %reduce-scatter.20.cloned.1.call-start = ((), (), s32[]{:S(2)}) async-start(), calls=%async_computation.28 | async-start | bytes 2359296 | tf_op jit(solution)/shard_map/reduce_scatter | solution.py:310
  1110.5 204.6 %all-gather.55.cloned.1.call-start = ((), (), s32[]{:S(2)}) async-start(), calls=%async_computation.29 | async-start | bytes 2359296 | tf_op jit(solution)/shard_map/all_gather | solution.py:292
  1281.4 207.6 %reduce-scatter.22.cloned.1.call-start = ((), (), s32[]{:S(2)}) async-start(), calls=%async_computation.31 | async-start | bytes 2359296 | tf_op jit(solution)/shard_map/reduce_scatter | solution.py:307
  1423.0 136.2 %reduce-scatter.24.cloned.1.call-start = ((), (), s32[]{:S(2)}) async-start(), calls=%async_computation.32 | async-start | bytes 2359296 | tf_op jit(solution)/shard_map/reduce_scatter | solution.py:310
  1423.8 204.3 %all-gather.59.cloned.1.call-start = ((), (), s32[]{:S(2)}) async-start(), calls=%async_computation.33 | async-start | bytes 2359296 | tf_op jit(solution)/shard_map/all_gather | solution.py:292
  1593.4 208.8 %reduce-scatter.26.cloned.1.call-start = ((), (), s32[]{:S(2)}) async-start(), calls=%async_computation.35 | async-start | bytes 2359296 | tf_op jit(solution)/shard_map/reduce_scatter | solution.py:307
  1736.2 136.2 %reduce-scatter.28.cloned.1.call-start = ((), (), s32[]{:S(2)}) async-start(), calls=%async_computation.36 | async-start | bytes 2359296 | tf_op jit(solution)/shard_map/reduce_scatter | solution.py:310
  1736.8 204.4 %all-gather.63.cloned.1.call-start = ((), (), s32[]{:S(2)}) async-start(), calls=%async_computation.37 | async-start | bytes 2359296 | tf_op jit(solution)/shard_map/all_gather | solution.py:292
  1906.3 209.0 %reduce-scatter.30.cloned.1.call-start = ((), (), s32[]{:S(2)}) async-start(), calls=%async_computation.39 | async-start | bytes 2359296 | tf_op jit(solution)/shard_map/reduce_scatter | solution.py:307
  2049.3 136.0 %reduce-scatter.32.cloned.1.call-start = ((), (), s32[]{:S(2)}) async-start(), calls=%async_computation.40 | async-start | bytes 2359296 | tf_op jit(solution)/shard_map/reduce_scatter | solution.py:310
  2049.9 204.1 %all-gather.67.cloned.1.call-start = ((), (), s32[]{:S(2)}) async-start(), calls=%async_computation.41 | async-start | bytes 2359296 | tf_op jit(solution)/shard_map/all_gather | solution.py:292
  2219.9 199.9 %reduce-scatter.34.cloned.1.call-start = ((), (), s32[]{:S(2)}) async-start(), calls=%async_computation.43 | async-start | bytes 2359296 | tf_op jit(solution)/shard_map/reduce_scatter | solution.py:307
  2353.8 136.3 %reduce-scatter.36.cloned.1.call-start = ((), (), s32[]{:S(2)}) async-start(), calls=%async_computation.44 | async-start | bytes 2359296 | tf_op jit(solution)/shard_map/reduce_scatter | solution.py:310
  2354.6 346.3 %reduce-scatter.46.cloned.1.call-start = ((), (), s32[]{:S(2)}) async-start(), calls=%async_computation.53 | async-start | bytes 557056
  2497.4 204.9 %reduce-scatter.40.cloned.1.call-start = ((), (), s32[]{:S(2)}) async-start(), calls=%async_computation.46 | async-start | bytes 4456448 | tf_op jit(solution)/shard_map/reduce_scatter | solution.py:335
  2506.3 250.8 %reduce-scatter.44.cloned.1.call-start = ((), (), s32[]{:S(2)}) async-start(), calls=%async_computation.48 | async-start | bytes 11698176 | tf_op jit(solution)/shard_map/reduce_scatter | solution.py:337
  2553.3 342.8 %reduce-scatter.38.cloned.1.call-start = ((), (), s32[]{:S(2)}) async-start(), calls=%async_computation.45 | async-start | bytes 13369344 | tf_op jit(solution)/shard_map/reduce_scatter | solution.py:334
  2603.0 511.4 %reduce-scatter.42.cloned.1.call-start = ((), (), s32[]{:S(2)}) async-start(), calls=%async_computation.47 | async-start | bytes 22839296 | tf_op jit(solution)/shard_map/reduce_scatter | solution.py:336
  (410 other events, 8866.8 us)
Sparse Core Ops, SparseCore 0:
  10.3 63.3 all-gather.70
  221.4 88.1 all-gather.74
  311.8 56.6 all-gather.76
  394.4 49.0 all-gather.36
  446.3 48.5 all-gather.34
  532.5 51.1 all-gather.40
  672.6 51.1 all-gather.44
  726.4 48.5 all-gather.42
  811.1 51.2 all-gather.48
  1110.0 65.8 reduce-scatter.17
  1179.3 66.7 reduce-scatter.19
  1265.7 49.3 all-gather.54
  1317.0 48.5 all-gather.56
  1423.2 65.8 reduce-scatter.21
  1492.6 66.6 reduce-scatter.23
  1578.7 49.3 all-gather.58
  1630.1 48.6 all-gather.60
  1736.3 65.8 reduce-scatter.25
  1805.6 66.7 reduce-scatter.27
  1891.8 49.3 all-gather.62
  1943.3 48.5 all-gather.64
  2049.4 65.8 reduce-scatter.29
  2118.7 66.5 reduce-scatter.31
  2204.7 49.2 all-gather.66
  2256.2 48.6 all-gather.68
  2353.9 65.8 reduce-scatter.33
  2423.4 66.6 reduce-scatter.35
  2497.5 54.8 reduce-scatter.45
  2557.2 71.5 reduce-scatter.39
  2633.4 123.6 reduce-scatter.43
  2762.2 133.7 reduce-scatter.37
  2901.2 213.1 reduce-scatter.41
  (7 shorter events, 329.8 us)
where the time goes:
time: 3140 us; the launch traced here: 3120 us
  waiting for transfers between devices  2020 us (64%)
  matrix products  588 us (19%)
  local copies, waits for them, and re-layouts  338 us (11%)
  other arithmetic  102 us (3%)
    all_gather x10, waiting for transfers between devices, body(): lax.all_gather(value_rows, 'ctx', axis=0, tiled=True)  407 us
    all_gather x10, waiting for transfers between devices, body(): lax.all_gather(key_rot, 'ctx', axis=0, tiled=True)  335 us
    reduce_scatter x5, waiting for transfers between devices, body(): lax.psum_scatter(value_terms.astype(jnp.bfloat16), 'ctx', scatter_dimensi...  316 us
    reduce_scatter x5, waiting for transfers between devices, body(): lax.psum_scatter(key_terms.astype(jnp.bfloat16), 'ctx', scatter_dimension...  314 us
    reduce_scatter x1, waiting for transfers between devices, body(): lax.psum_scatter(grad_in, ('ctx', 'wshard'), scatter_dimension=0, tiled=T...  218 us
    dot_general x20, matrix products, contract_rows(): lax.dot_general(left, right, (((0,), (0,)), ((), ())), preferred_element_...  194 us
    reduce_scatter x1, waiting for transfers between devices, body(): lax.psum_scatter(grad_qkv, ('ctx', 'wshard'), scatter_dimension=0, tiled=...  139 us
    dot_general x20, matrix products, contract_cols(): lax.dot_general(left, right, (((1,), (1,)), ((), ())), preferred_element_...  91.5 us
  transfers between devices with their start and end apart: 47, of which 41 were waited for; matrix products, arithmetic and copies ran while one was open for 16% of the time, Pallas kernels for 0%

commit v1 on v0

v1 whole, which is shorter than its diff:
```python
from functools import partial

import jax
import jax.numpy as jnp
from jax import lax
from jax.experimental import pallas as pl
from jax.experimental.pallas import tpu as pltpu
from jax.sharding import PartitionSpec as P

D = 1024
HEADS = 16
HEAD_DIM = 64
FF = 2624
FFP = 2688
LANES = 128
PAIRS = D // LANES
EPSILON = 1e-05
ROPE_BASE = 160000.0
NEG_FILL = -1e30
BF = jnp.bfloat16
F32 = jnp.float32
BOTH = ("ctx", "wshard")
VMEM = 60 * 1024 * 1024


def dot(a, b, dims):
    return lax.dot_general(a, b, (dims, ((), ())), preferred_element_type=F32)


NN = ((1,), (0,))
NT = ((1,), (1,))
TN = ((0,), (0,))


def params(limit=VMEM):
    return pltpu.CompilerParams(vmem_limit_bytes=limit)


def rope_block(v, cosine, sine):
    lane = lax.broadcasted_iota(jnp.int32, v.shape, 1) % HEAD_DIM
    other = jnp.where(
        lane < HEAD_DIM // 2,
        pltpu.roll(v, LANES - HEAD_DIM // 2, 1),
        pltpu.roll(v, HEAD_DIM // 2, 1),
    )
    return v * cosine + other * sine


def rope_kernel(v_ref, cos_ref, sin_ref, out_ref, *, rotated):
    cosine, sine = cos_ref[...], sin_ref[...]
    for j in range(v_ref.shape[1] // LANES):
        at = slice(j * LANES, (j + 1) * LANES)
        v = v_ref[:, at].astype(F32)
        if j * LANES < rotated:
            v = rope_block(v, cosine, sine)
        out_ref[:, at] = v.astype(BF)


def rope_apply(v, cosine, sine, rotated):
    return pl.pallas_call(
        partial(rope_kernel, rotated=rotated),
        out_shape=jax.ShapeDtypeStruct(v.shape, BF),
        compiler_params=params(),
    )(v, cosine, sine)


def head_mask(shape, head):
    lane = lax.broadcasted_iota(jnp.int32, shape, 1)
    return (lane >= HEAD_DIM) if head else (lane < HEAD_DIM)


def pick(mask, v, other=0.0):
    return jnp.where(mask, v, jnp.full(v.shape, other, v.dtype))


def attend_kernel(q_ref, k_ref, v_ref, segq_ref, segk_ref, o_ref, lse_ref, bias_ref):
    @pl.when(pl.program_id(0) == 0)
    def _():
        bias_ref[...] = jnp.where(segk_ref[...] == segq_ref[...], 0.0, NEG_FILL)

    k, v = k_ref[...], v_ref[...]
    q = q_ref[...] * jnp.asarray(HEAD_DIM**-0.5, BF)
    qmask, vmask = head_mask(q.shape, 0), head_mask(v.shape, 0)
    parts, stats = [], []
    for head in range(2):
        qh = pick(qmask if head == 0 else ~qmask, q)
        vh = pick(vmask if head == 0 else ~vmask, v, 1.0)
        s = dot(k, qh, NT) + bias_ref[...]
        top = jnp.max(s, axis=0, keepdims=True)
        e = jnp.exp(s - top).astype(BF)
        u = dot(vh, e, TN)
        if head == 0:
            total, value = u[HEAD_DIM:], u[:HEAD_DIM]
        else:
            total, value = u[:HEAD_DIM], u[HEAD_DIM:]
        parts.append(value / total)
        stats.append(top + jnp.log(total[:1]))
    o_ref[...] = jnp.concatenate(parts, axis=0).T.astype(BF)
    lse_ref[0] = jnp.concatenate(stats, axis=0)


def attend(q, k, v, segq, segk):
    rows, keys = q.shape[0], k.shape[0]
    return pl.pallas_call(
        attend_kernel,
        grid=(PAIRS,),
        in_specs=[
            pl.BlockSpec((rows, LANES), lambda p: (0, p)),
            pl.BlockSpec((keys, LANES), lambda p: (0, p)),
            pl.BlockSpec((keys, LANES), lambda p: (0, p)),
            pl.BlockSpec((1, rows), lambda p: (0, 0)),
            pl.BlockSpec((keys, 1), lambda p: (0, 0)),
        ],
        out_specs=[
            pl.BlockSpec((rows, LANES), lambda p: (0, p)),
            pl.BlockSpec((1, 2, rows), lambda p: (p, 0, 0)),
        ],
        out_shape=[
            jax.ShapeDtypeStruct((rows, D), BF),
            jax.ShapeDtypeStruct((PAIRS, 2, rows), F32),
        ],
        scratch_shapes=[pltpu.VMEM((keys, rows), F32)],
        compiler_params=params(),
    )(q, k, v, segq, segk)


def attend_back_kernel(
    q_ref, k_ref, v_ref, do_ref, o_ref, lse_ref, segq_ref, segk_ref, dq_ref, dk_ref, dv_ref, bias_ref
):
    @pl.when(pl.program_id(0) == 0)
    def _():
        bias_ref[...] = jnp.where(segk_ref[...] == segq_ref[...], 0.0, NEG_FILL)

    scale = jnp.asarray(HEAD_DIM**-0.5, BF)
    k, v, do = k_ref[...], v_ref[...], do_ref[...]
    q = q_ref[...] * scale
    prod = (do.astype(F32) * o_ref[...].astype(F32)).T
    lse = lse_ref[0]
    qmask, kmask = head_mask(q.shape, 0), head_mask(k.shape, 0)
    dq = dk = dv = 0.0
    for head in range(2):
        qm = qmask if head == 0 else ~qmask
        km = kmask if head == 0 else ~kmask
        qh, doh, kh = pick(qm, q), pick(qm, do), pick(km, k)
        delta = jnp.sum(prod[head * HEAD_DIM : (head + 1) * HEAD_DIM], axis=0, keepdims=True)
        s = dot(k, qh, NT) + bias_ref[...]
        p = jnp.exp(s - lse[head : head + 1])
        dp = dot(v, doh, NT)
        ds = (p * (dp - delta)).astype(BF)
        dv += dot(p.astype(BF), doh, NN)
        dk += dot(ds, qh, NN)
        dq += dot(ds, kh, TN)
    dq_ref[...] = dq * HEAD_DIM**-0.5
    dk_ref[...] = dk.astype(BF)
    dv_ref[...] = dv.astype(BF)


def attend_back(q, k, v, do, o, lse, segq, segk):
    rows, keys = q.shape[0], k.shape[0]
    qspec = pl.BlockSpec((rows, LANES), lambda p: (0, p))
    kspec = pl.BlockSpec((keys, LANES), lambda p: (0, p))
    return pl.pallas_call(
        attend_back_kernel,
        grid=(PAIRS,),
        in_specs=[
            qspec,
            kspec,
            kspec,
            qspec,
            qspec,
            pl.BlockSpec((1, 2, rows), lambda p: (p, 0, 0)),
            pl.BlockSpec((1, rows), lambda p: (0, 0)),
            pl.BlockSpec((keys, 1), lambda p: (0, 0)),
        ],
        out_specs=[qspec, kspec, kspec],
        out_shape=[
            jax.ShapeDtypeStruct((rows, D), F32),
            jax.ShapeDtypeStruct((keys, D), BF),
            jax.ShapeDtypeStruct((keys, D), BF),
        ],
        scratch_shapes=[pltpu.VMEM((keys, rows), F32)],
        compiler_params=params(),
    )(q, k, v, do, o, lse, segq, segk)


def norm_parts(values):
    center = values - jnp.mean(values, axis=-1, keepdims=True)
    spread = jnp.mean(center * center, axis=-1, keepdims=True)
    inverse = lax.rsqrt(spread + EPSILON)
    return center * inverse, inverse


def norm_back(hat, inverse, gain_row, grad):
    scaled = grad * gain_row
    return inverse * (
        scaled
        - jnp.mean(scaled, axis=-1, keepdims=True)
        - hat * jnp.mean(scaled * hat, axis=-1, keepdims=True)
    )


def gelu_parts(t):
    phi = 0.5 * (1.0 + lax.erf(t * 0.7071067811865476))
    density = 0.3989422804014327 * jnp.exp(-0.5 * t * t)
    return t * phi, phi + t * density


class Plan:
    def __init__(self, boundary):
        self.micro = boundary.shape[1]
        self.tok_rows = boundary.shape[3]
        self.n_ctx = lax.axis_size("ctx")
        self.nw = lax.axis_size("wshard")
        self.g = self.n_ctx // (self.micro * self.nw)
        self.r = self.tok_rows // (self.g * self.nw)
        self.i = lax.axis_index("ctx")
        self.w = lax.axis_index("wshard")
        self.rows = self.n_ctx * self.r
        self.members = self.g * self.nw

    def to_sequences(self, local):
        parts = local.reshape(self.micro, self.g, self.nw, self.r, D)
        parts = lax.all_to_all(parts.transpose(2, 0, 1, 3, 4), "wshard", 0, 0, tiled=True)
        parts = parts.transpose(1, 0, 2, 3, 4).reshape(self.n_ctx, self.r, D)
        return lax.all_to_all(parts, "ctx", 0, 0, tiled=True).reshape(self.rows, D)

    def from_sequences(self, rows):
        parts = lax.all_to_all(rows.reshape(self.n_ctx, self.r, D), "ctx", 0, 0, tiled=True)
        parts = parts.reshape(self.micro, self.nw, self.g, self.r, D).transpose(1, 0, 2, 3, 4)
        parts = lax.all_to_all(parts, "wshard", 0, 0, tiled=True)
        return parts.transpose(1, 2, 0, 3, 4).reshape(self.micro, self.tok_rows, D)

    def rotation(self, by):
        pairs = []
        for flat in range(self.n_ctx * self.nw):
            group, place = divmod(flat, self.members)
            pairs.append((flat, group * self.members + (place + by) % self.members))
        return pairs

    def gather_rows(self, rows):
        pieces = [rows]
        for by in range(1, self.members):
            pieces.append(lax.ppermute(rows, BOTH, self.rotation(by)))
        return jnp.concatenate(pieces, axis=0)

    def scatter_rows(self, terms):
        count = self.rows
        total = terms[:count].astype(F32)
        for by in range(1, self.members):
            piece = terms[by * count : (by + 1) * count]
            total += lax.ppermute(piece, BOTH, self.rotation(-by)).astype(F32)
        return total


def body(
    boundary, segment_ids, qkv_weight, attn_out_weight, ffn_in_weight, ffn_out_weight, norm_gains
):
    section = lax.axis_index("section")
    sections = lax.axis_size("section")
    plan = Plan(boundary)
    rows = plan.rows
    own = plan.to_sequences(boundary[0, :, 0])

    whole = lax.all_gather(segment_ids[:, 0], BOTH, axis=0)
    whole = whole.reshape(plan.n_ctx, plan.nw, plan.micro, plan.tok_rows)
    mine = plan.i // plan.g
    line = lax.dynamic_index_in_dim(whole, mine // plan.nw, 2, keepdims=False)
    line = lax.dynamic_index_in_dim(line, mine % plan.nw, 1, keepdims=False).reshape(-1)
    grid = line.reshape(plan.n_ctx, plan.members, plan.r)
    place = (plan.i % plan.g) * plan.nw + plan.w
    seg_pieces = [
        lax.dynamic_index_in_dim(
            grid, (place - by) % plan.members, 1, keepdims=False
        ).reshape(rows)
        for by in range(plan.members)
    ]
    segq = seg_pieces[0]
    segk = jnp.concatenate(seg_pieces)
    token = (
        lax.broadcasted_iota(jnp.int32, (plan.n_ctx, plan.r), 0) * plan.tok_rows
        + place * plan.r
        + lax.broadcasted_iota(jnp.int32, (plan.n_ctx, plan.r), 1)
    ).reshape(rows)
    first = jnp.sum((line[None, :] < segq[:, None]).astype(jnp.int32), axis=1)
    position = (token - first).astype(F32)
    half = HEAD_DIM // 2
    exponent = jnp.arange(half, dtype=F32) * (-2.0 / HEAD_DIM)
    angles = position[:, None] * (ROPE_BASE**exponent)[None, :]
    cosine, sine = jnp.cos(angles), jnp.sin(angles)
    cos_rows = jnp.concatenate([cosine] * 4, axis=1)
    sin_rows = jnp.concatenate([-sine, sine] * 2, axis=1)
    segq_row, segk_col = segq[None, :], segk[:, None]

    gain_cols = jnp.pad(norm_gains[0].T, ((0, 0), (0, LANES - 2)))
    pad = FFP - FF
    first_shard = jnp.concatenate([qkv_weight[0], gain_cols], axis=1)
    in_shard = jnp.concatenate(
        [
            jnp.pad(ffn_in_weight[0][:, :FF], ((0, 0), (0, pad))),
            jnp.pad(ffn_in_weight[0][:, FF:], ((0, 0), (0, pad))),
        ],
        axis=1,
    )
    back_shard = jnp.pad(ffn_out_weight[0].T, ((0, 0), (0, pad)))
    w_first = lax.all_gather(first_shard, BOTH, axis=0, tiled=True)
    w_attn = lax.all_gather(attn_out_weight[0], BOTH, axis=0, tiled=True)
    w_in = lax.all_gather(in_shard, BOTH, axis=0, tiled=True)
    w_back = lax.all_gather(back_shard, BOTH, axis=0, tiled=True)
    w_qkv = w_first[:, : 3 * D]
    gains = w_first[:, 3 * D : 3 * D + 2].T.astype(F32)

    def forward(x_low):
        x = x_low.astype(F32)
        hat, _ = norm_parts(x)
        a = (hat * gains[0]).astype(BF)
        kv = rope_apply(dot(a, w_qkv[:, D:], NN), cos_rows, sin_rows, D)
        kv_all = plan.gather_rows(kv)
        q = rope_apply(dot(a, w_qkv[:, :D], NN), cos_rows, sin_rows, D)
        k_all, v_all = kv_all[:, :D], kv_all[:, D:]
        o, lse = attend(q, k_all, v_all, segq_row, segk_col)
        h = x + dot(o, w_attn, NN)
        hat2, inv2 = norm_parts(h)
        b = (hat2 * gains[1]).astype(BF)
        u = dot(b, w_in, NN)
        act, slope = gelu_parts(u[:, :FFP])
        gate = u[:, FFP:]
        z = (act * gate).astype(BF)
        out = (h + dot(z, w_back, NT)).astype(BF)
        return out, (x, a, q, k_all, v_all, o, lse, h, b, act.astype(BF), (slope * gate).astype(BF), z)

    def backward(stash, grad, with_weights):
        x, a, q, k_all, v_all, o, lse, h, b, act, slope, z = stash
        dz = dot(grad, w_back, NN)
        du = jnp.concatenate([dz * slope, dz * act], axis=1).astype(BF)
        db = dot(du, w_in, NT)
        hat2, inv2 = norm_parts(h)
        dh = grad.astype(F32) + norm_back(hat2, inv2, gains[1], db)
        dhb = dh.astype(BF)
        do = dot(dhb, w_attn, NT).astype(BF)
        dq, dk_terms, dv_terms = attend_back(q, k_all, v_all, do, o, lse, segq_row, segk_col)
        dkv = plan.scatter_rows(jnp.concatenate([dk_terms, dv_terms], axis=1))
        dm = rope_apply(jnp.concatenate([dq, dkv], axis=1), cos_rows, -sin_rows, 2 * D)
        da = dot(dm, w_qkv, NT)
        hat1, inv1 = norm_parts(x)
        dx = (dh + norm_back(hat1, inv1, gains[0], da)).astype(BF)
        if not with_weights:
            return dx, None
        g_back = dot(grad, z, TN).astype(BF)
        g_in = dot(b, du, TN).astype(BF)
        g_attn = dot(o, dhb, TN).astype(BF)
        g_qkv = dot(a, dm, TN).astype(BF)
        g_gain = jnp.stack([jnp.sum(da * hat1, axis=0), jnp.sum(db * hat2, axis=0)], axis=1)
        g_gain = jnp.pad(g_gain, ((0, 0), (0, LANES - 2))).astype(BF)
        return dx, (g_back, g_in, g_attn, jnp.concatenate([g_qkv, g_gain], axis=1))

    def handed(array, by):
        pairs = [(s, s + by) for s in range(sections) if 0 <= s + by < sections]
        return lax.ppermute(array, "section", pairs)

    first_out, _ = forward(own)
    x_in = jnp.where(section == 0, own, handed(first_out, 1))
    out, stash = forward(x_in)
    first_dx, _ = backward(stash, own, False)
    grad_in = jnp.where(section == sections - 1, own, handed(first_dx, -1))
    dx, grads = backward(stash, grad_in, True)
    g_back, g_in, g_attn, g_first = (
        lax.psum_scatter(t, BOTH, scatter_dimension=0, tiled=True).astype(F32) for t in grads
    )
    boundary_local = plan.from_sequences(jnp.where(section == 0, dx, out))
    return (
        boundary_local[None, :, None],
        g_first[None, :, : 3 * D],
        g_attn[None],
        jnp.concatenate([g_in[:, :FF], g_in[:, FFP : FFP + FF]], axis=1)[None],
        g_back[:, :FF].T[None],
        g_first[:, 3 * D : 3 * D + 2].T[None],
    )


def solution(mesh):
    placed = (
        P("section", None, "wshard", "ctx", None),
        P(None, "wshard", "ctx"),
        P("section", ("ctx", "wshard"), None),
        P("section", ("ctx", "wshard"), None),
        P("section", ("ctx", "wshard"), None),
        P("section", None, ("ctx", "wshard")),
        P("section", None, ("ctx", "wshard")),
    )
    return jax.shard_map(
        body,
        mesh=mesh,
        in_specs=placed,
        out_specs=(placed[0],) + placed[2:],
        check_vma=False,
    )
```

time: 3140 us -> 911 us (0.29)
  waiting for transfers between devices: 2020 us -> 455 us
  matrix products: 588 us -> 160 us
  local copies, waits for them, and re-layouts: 338 us -> 20.3 us
  Pallas kernels: 0 us -> 129 us
  other arithmetic: 102 us -> 46.6 us
    all_gather x24 -> x4, waiting for transfers between devices: 955 us -> 138 us  [the longest x1 84.5 us: body(): w_in = lax.all_gather(in_shard, BOTH, axis=0, tiled=True)]
    reduce_scatter x14 -> x4, waiting for transfers between devices: 1040 us -> 227 us  [body(): lax.psum_scatter(t, BOTH, scatter_dimension=0, tiled=True).astype(F32)]
    dot_general x135 -> x22, matrix products: 588 us -> 160 us  [dot(): return lax.dot_general(a, b, (dims, ((), ())), preferred_element_type=F32)]
    pallas_call x0 -> x10, Pallas kernels: none -> 129 us  [the longest x2 59.2 us: attend_back(): pl.pallas_call(attend_back_kernel, grid=(PAIRS,), in_specs=[qspec, kspec,...]
    unnamed x769 -> x47, local copies, waits for them, and re-layouts: 89.1 us -> 8.63 us
    reshape x30 -> x1, local copies, waits for them, and re-layouts: 73.6 us -> 0.08 us  [body(): seg_pieces = [lax.dynamic_index_in_dim(grid, (place - by) % plan.members,...]
    dynamic_update_slice x38 -> x0, local copies, waits for them, and re-layouts: 67.3 us -> none  [the longest x30 61.1 us: attend_back(): lax.scan(one_block, start_query, (key_blocks, value_blocks, seg_blocks))]
    slice x42 -> x5, local copies, waits for them, and re-layouts: 65.4 us -> 3.17 us  [the longest x1 1.23 us: body(): ffn_in_weight[0][:, FF:]]
  transfers between devices with their start and end apart: 47 -> 16, of which waited for: 41 -> 11; matrix products, arithmetic and copies ran while one was open for 16% -> 13% of each run, Pallas kernels for 0% -> 8%
where the time goes in v1:
time: 911 us; the launch traced here: 901 us
  waiting for transfers between devices  455 us (50%)
  matrix products  160 us (18%)
  Pallas kernels  129 us (14%)
  blocking collectives  58.4 us (6%)
  other arithmetic  46.6 us (5%)
  local copies, waits for them, and re-layouts  20.3 us (2%)
  starting transfers between devices  17.4 us (2%)
  between operations  14.8 us (2%)
    reduce_scatter x4, waiting for transfers between devices, body(): lax.psum_scatter(t, BOTH, scatter_dimension=0, tiled=True).astype(F32)  227 us
    dot_general x22, matrix products, dot(): return lax.dot_general(a, b, (dims, ((), ())), preferred_element_type=F32)  160 us
    all_gather x1, waiting for transfers between devices, body(): w_in = lax.all_gather(in_shard, BOTH, axis=0, tiled=True)  84.5 us
    pallas_call x2, Pallas kernels, attend_back(): pl.pallas_call(attend_back_kernel, grid=(PAIRS,), in_specs=[qspec, kspec,...  59.2 us
    all_gather x1, blocking collectives, body(): whole = lax.all_gather(segment_ids[:, 0], BOTH, axis=0)  48.9 us
    ppermute x2, waiting for transfers between devices, handed(): return lax.ppermute(array, 'section', pairs)  48.1 us
    all_gather x1, waiting for transfers between devices, body(): w_back = lax.all_gather(back_shard, BOTH, axis=0, tiled=True)  46 us
    pallas_call x2, Pallas kernels, attend(): pl.pallas_call(attend_kernel, grid=(PAIRS,), in_specs=[pl.BlockSpec((rows...  37.3 us
  transfers between devices with their start and end apart: 16, of which 11 were waited for; matrix products, arithmetic and copies ran while one was open for 13% of the time, Pallas kernels for 8%

profile of v1, /device:TPU:13, one launch (start us, length us, event | category | flops | bytes accessed | tf_op | source)
XLA Modules:
  0.0 901.5 jit_solution(16685775160115165776)
XLA Ops:
  25.6 48.9 %all-gather = s32[64,1,128]{2,1,0:T(1,128)S(1)} all-gather(s32[4,1,128]{2,1,0:T(1,128)S(1)} %copy-done.20), channel_id=2, replica_groups=mesh['section'=2,'ctx'=8,'wshard'=2] {'ctx','wshard'}, dimensions={0}, use_global_device_ids=true | all-gather | bytes 34816 | tf_op jit(solution)/shard_map/all_gather | solution.py:264
  80.1 7.7 all-gather.7.cloned.1.call-done
  89.6 6.5 fusion.23.v_ref
  115.0 18.7 %shard_map.120 = (bf16[512,1024]{1,0:T(8,128)(2,1)}, f32[8,2,512]{2,1,0:T(2,128)}) custom-call(bf16[512,1024]{1,0:T(8,128)(2,1)} %shard_map.118.q_ref, bf16[1024,1024]{1,0:T(8,128)(2,1)} %get-tuple-element.71.k_ref, bf16[1024,1024]{1,0:T(8,128)(2,1)} %get-tuple-element.70.v_ref, s32[1,512]{1,0:T(1,128)} %broadcast_in_dim_reshape.8.segq_ref, ...), custom_call_target="tpu_custom_call" | custom-call | tf_op jit(solution)/shard_map/pallas_call | solution.py:104
  137.3 84.5 %all-gather.9.cloned.1.call-done = bf16[1024,5376]{1,0:T(8,128)(2,1)} async-done(((bf16[64,5376]{1,0:T(8,128)(2,1)}), bf16[1024,5376]{1,0:T(8,128)(2,1)}) %all-gather.9.cloned.1.call-update) | async-done | bytes 11010064 | tf_op jit(solution)/shard_map/all_gather | solution.py:307
  221.8 12.9 %fusion.82 = f32[512,5376]{1,0:T(8,128)} fusion(bf16[1024,5376]{1,0:T(8,128)(2,1)} %all-gather.9.cloned.1.call-done, f32[512,1024]{1,0:T(8,128)S(1)} %get-tuple-element.79, f32[1024]{0:T(1024)S(1)} %get-tuple-element.52, f32[512]{0:T(512)S(1)} %add_rsqrt_fusion.3, f32[512]{0:T(512)S(1)} %broadcast_multiply_fusion.11), kind=kOutput, calls=%fused_computation.122 | convolution fusion | flops 5639241728 | bytes 24125440 | tf_op jit(solution)/shard_map/dot_general | solution.py:27
  234.7 46.0 %all-gather.11.cloned.1.call-done = bf16[1024,2688]{1,0:T(8,128)(2,1)} async-done(((bf16[64,2688]{1,0:T(8,128)(2,1)}), bf16[1024,2688]{1,0:T(8,128)(2,1)}) %all-gather.11.cloned.1.call-update) | async-done | bytes 5505040 | tf_op jit(solution)/shard_map/all_gather | solution.py:308
  280.7 8.4 add_convert_fusion.1
  292.3 22.5 %collective-permute-done.1 = bf16[512,1024]{1,0:T(8,128)(2,1)S(1)} collective-permute-done((bf16[512,1024]{1,0:T(8,128)(2,1)}, bf16[512,1024]{1,0:T(8,128)(2,1)S(1)}, u32[]{:S(2)}, u32[]{:S(2)}) %collective-permute-start.1) | collective-permute-done | bytes 1048608 | tf_op jit(solution)/shard_map/ppermute | solution.py:358
  315.6 6.6 fusion.21.v_ref
  340.4 18.7 %shard_map.123 = (bf16[512,1024]{1,0:T(8,128)(2,1)}, f32[8,2,512]{2,1,0:T(2,128)}) custom-call(bf16[512,1024]{1,0:T(8,128)(2,1)} %shard_map.121.q_ref, bf16[1024,1024]{1,0:T(8,128)(2,1)} %get-tuple-element.69.k_ref, bf16[1024,1024]{1,0:T(8,128)(2,1)} %get-tuple-element.68.v_ref, s32[1,512]{1,0:T(1,128)} %broadcast_in_dim_reshape.8.segq_ref, ...), custom_call_target="tpu_custom_call" | custom-call | tf_op jit(solution)/shard_map/pallas_call | solution.py:104
  362.9 8.5 fusion.93
  371.4 9.2 %fusion.6 = (bf16[512,2688]{1,0:T(8,128)(2,1)}, bf16[512,2688]{1,0:T(8,128)(2,1)}, f32[512,2688]{1,0:T(8,128)S(1)}, f32[2688,512]{0,1:T(8,128)}) fusion(f32[512,5376]{1,0:T(8,128)S(1)} %fusion.93, bf16[512,1024]{1,0:T(8,128)(2,1)S(1)} %bitcast.101, bf16[1024,2688]{1,0:T(8,128)(2,1)} %all-gather.11.cloned.1.call-done), kind=kOutput, calls=%fused_computation.17 | convolution fusion | flops 2836463616 | bytes 34078720 | tf_op jit(solution)/shard_map/dot_general | solution.py:27
  380.7 5.7 fusion.8
  386.3 11.6 %multiply_reduce_fusion.8 = (f32[512]{0:T(512)S(1)}, f32[512]{0:T(512)S(1)}, f32[512,1024]{1,0:T(8,128)S(1)}) fusion(f32[1024]{0:T(1024)S(1)} %get-tuple-element.52, f32[512]{0:T(512)S(1)} %add_rsqrt_fusion.1, f32[512,1024]{1,0:T(8,128)S(1)} %get-tuple-element.81, f32[512]{0:T(512)S(1)} %broadcast_multiply_fusion.9, ...), kind=kOutput, calls=%fused_computation.116 | convolution fusion | flops 5651299328 | bytes 20721664 | tf_op jit(solution)/shard_map/dot_general | solution.py:27
  401.8 29.4 %shard_map.124 = (f32[512,1024]{1,0:T(8,128)}, bf16[1024,1024]{1,0:T(8,128)(2,1)}, bf16[1024,1024]{1,0:T(8,128)(2,1)}) custom-call(bf16[512,1024]{1,0:T(8,128)(2,1)} %shard_map.121.q_ref, bf16[1024,1024]{1,0:T(8,128)(2,1)} %get-tuple-element.69.k_ref, bf16[1024,1024]{1,0:T(8,128)(2,1)} %get-tuple-element.68.v_ref, bf16[512,1024]{1,0:T(8,128)(2,1)} %fusion.75.do_ref, ...), custom_call_target="tpu_custom_call" | custom-call | tf_op jit(solution)/shard_map/pallas_call | solution.py:162
  442.3 7.0 shard_map.125
  449.3 7.7 multiply_reduce_fusion.7
  460.1 25.5 %collective-permute-done.4 = bf16[512,1024]{1,0:T(8,128)(2,1)} collective-permute-done((bf16[512,1024]{1,0:T(8,128)(2,1)}, bf16[512,1024]{1,0:T(8,128)(2,1)}, u32[]{:S(2)}, u32[]{:S(2)}) %collective-permute-start.4) | collective-permute-done | bytes 1048608 | tf_op jit(solution)/shard_map/ppermute | solution.py:358
  487.0 8.5 fusion.7
  495.5 12.3 %multiply_reduce_fusion = (bf16[1024]{0:T(1024)(128)(2,1)S(1)}, f32[512]{0:T(512)S(1)}, f32[512]{0:T(512)S(1)}, f32[512,1024]{1,0:T(8,128)}) fusion(f32[512]{0:T(512)S(1)} %add_rsqrt_fusion.1, f32[512,1024]{1,0:T(8,128)S(1)} %get-tuple-element.81, f32[512]{0:T(512)S(1)} %broadcast_multiply_fusion.9, f32[1024]{0:T(1024)S(1)} %get-tuple-element.52, ...), kind=kOutput, calls=%fused_computation.96 | convolution fusion | flops 5652346880 | bytes 20723712 | tf_op jit(solution)/shard_map/dot_general | solution.py:27
  515.5 6.8 convolution_convert_fusion.1
  526.9 29.9 %shard_map.126 = (f32[512,1024]{1,0:T(8,128)}, bf16[1024,1024]{1,0:T(8,128)(2,1)}, bf16[1024,1024]{1,0:T(8,128)(2,1)}) custom-call(bf16[512,1024]{1,0:T(8,128)(2,1)} %shard_map.121.q_ref, bf16[1024,1024]{1,0:T(8,128)(2,1)} %get-tuple-element.69.k_ref, bf16[1024,1024]{1,0:T(8,128)(2,1)} %get-tuple-element.68.v_ref, bf16[512,1024]{1,0:T(8,128)(2,1)} %fusion.78.do_ref, ...), custom_call_target="tpu_custom_call" | custom-call | tf_op jit(solution)/shard_map/pallas_call | solution.py:162
  568.3 7.1 shard_map.127
  575.4 8.9 fusion.48
  584.5 6.2 convolution_convert_fusion.2
  593.9 11.8 %convolution_convert_fusion = bf16[1024,5376]{1,0:T(8,128)(2,1)} fusion(bf16[512,2688]{1,0:T(8,128)(2,1)} %get-tuple-element.67, bf16[512,2688]{1,0:T(8,128)(2,1)} %get-tuple-element.66, f32[1024]{0:T(1024)S(1)} %get-tuple-element.52, f32[512,1024]{1,0:T(8,128)S(1)} %get-tuple-element.81, f32[512]{0:T(512)S(1)} %add_rsqrt_fusion.1, ...), kind=kOutput, calls=%fused_computation.2 | convolution fusion | flops 5655756800 | bytes 18620416 | tf_op jit(solution)/shard_map/dot_general | solution.py:27
  605.7 9.7 %fusion.83 = bf16[512,1024]{1,0:T(8,128)(2,1)} fusion(f32[512,1024]{1,0:T(8,128)} %copy-done.13, bf16[512,1024]{1,0:T(8,128)(2,1)S(1)} %copy-done.2, f32[512,1024]{1,0:T(8,128)} %get-tuple-element.86, f32[512]{0:T(512)S(1)} %broadcast_multiply_fusion.1, f32[512]{0:T(512)S(1)} %broadcast_multiply_fusion.2, f32[512]{0:T(512)S(1)} %add_rsqrt_fusion.2, ...), kind=kOutput, calls=%fused_computation.123 | convolution fusion | flops 2825388032 | bytes 16658433 | tf_op jit(solution)/shard_map/dot_general | solution.py:27
  621.7 32.7 %all-to-all-done.2 = bf16[8,64,1024]{2,1,0:T(8,128)(2,1)S(1)} async-done(((bf16[8,64,1024]{2,1,0:T(8,128)(2,1)}), bf16[8,64,1024]{2,1,0:T(8,128)(2,1)S(1)}, u32[]{:S(2)}, u32[]{:S(2)}) %all-to-all-start.2) | async-done | bytes 1048608 | tf_op jit(solution)/shard_map/all_to_all | solution.py:228
  660.1 13.7 %reduce-scatter.11.cloned.1.call-done = bf16[64,2688]{1,0:T(8,128)(2,1)} async-done(((bf16[1024,2688]{1,0:T(8,128)(2,1)}), bf16[64,2688]{1,0:T(8,128)(2,1)}) %reduce-scatter.11.cloned.1.call-update) | async-done | bytes 344080 | tf_op jit(solution)/shard_map/reduce_scatter | solution.py:367
  675.7 89.4 %reduce-scatter.5.cloned.1.call-done = bf16[64,3200]{1,0:T(8,128)(2,1)} async-done(((bf16[1024,3200]{1,0:T(8,128)(2,1)}), bf16[64,3200]{1,0:T(8,128)(2,1)}) %reduce-scatter.5.cloned.1.call-update) | async-done | bytes 409616 | tf_op jit(solution)/shard_map/reduce_scatter | solution.py:367
  767.8 124.2 %reduce-scatter.9.cloned.1.call-done = bf16[64,5376]{1,0:T(8,128)(2,1)} async-done(((bf16[1024,5376]{1,0:T(8,128)(2,1)}), bf16[64,5376]{1,0:T(8,128)(2,1)}) %reduce-scatter.9.cloned.1.call-update) | async-done | bytes 688144 | tf_op jit(solution)/shard_map/reduce_scatter | solution.py:367
  (171 shorter events, 139.7 us)
Async XLA Ops:
  7.2 4.7 copy-start.19
  7.2 4.7 copy-start.17
  7.2 80.5 %all-gather.7.cloned.1.call-start = ((), (), s32[]{:S(2)}) async-start(), calls=%async_computation.8 | async-start | bytes 6963200 | tf_op jit(solution)/shard_map/all_gather | solution.py:305
  9.8 3.1 copy-start.18
  9.9 123.9 %all-gather.13.cloned.1.call-start = ((), (), s32[]{:S(2)}) async-start(), calls=%async_computation.15 | async-start | bytes 2228224 | tf_op jit(solution)/shard_map/all_gather | solution.py:306
  10.6 211.2 %all-gather.9.cloned.1.call-start = ((), (), s32[]{:S(2)}) async-start(), calls=%async_computation.9 | async-start | bytes 11698176 | tf_op jit(solution)/shard_map/all_gather | solution.py:307
  10.7 3.1 copy-start.16
  12.9 267.8 %all-gather.11.cloned.1.call-start = ((), (), s32[]{:S(2)}) async-start(), calls=%async_computation.10 | async-start | bytes 5849088 | tf_op jit(solution)/shard_map/all_gather | solution.py:308
  18.7 6.9 copy-start.20
  19.7 59.5 %all-to-all-start.1 = ((bf16[8,64,1024]{2,1,0:T(8,128)(2,1)}), bf16[8,64,1024]{2,1,0:T(8,128)(2,1)S(1)}, u32[]{:S(2)}, u32[]{:S(2)}) async-start(bf16[8,64,1024]{2,1,0:T(8,128)(2,1)} %bitcast.3), calls=%async_computation.1 | async-start | bytes 2097152 | tf_op jit(solution)/shard_map/all_to_all | solution.py:225
  25.4 594.6 %reduce-scatter.7.cloned.1.call-start = ((), (), s32[]{:S(2)}) async-start(), calls=%async_computation.12 | async-start | bytes 2228224 | tf_op jit(solution)/shard_map/reduce_scatter | solution.py:367
  101.2 10.2 %collective-permute-start = (bf16[512,2048]{1,0:T(8,128)(2,1)}, bf16[512,2048]{1,0:T(8,128)(2,1)}, u32[]{:S(2)}, u32[]{:S(2)}) collective-permute-start(bf16[512,2048]{1,0:T(8,128)(2,1)} %shard_map.119), channel_id=1, source_target_pairs={{0,1},{1,0},{2,3},{3,2},{4,5},{5,4},{6,7},{7,6},{8,9},{9,8},{10,11... | collective-permute-start | bytes 6291464 | tf_op jit(solution)/shard_map/ppermute | solution.py:243
  107.4 3.9 copy-start.5
  289.1 25.7 %collective-permute-start.1 = (bf16[512,1024]{1,0:T(8,128)(2,1)}, bf16[512,1024]{1,0:T(8,128)(2,1)S(1)}, u32[]{:S(2)}, u32[]{:S(2)}) collective-permute-start(bf16[512,1024]{1,0:T(8,128)(2,1)} %add_convert_fusion.1), channel_id=1, source_target_pairs={{0,16},{1,17},{2,18},{3,19},{4,20},{5,21},{6,22},{7,23},{8,24},{9,... | collective-permute-start | bytes 3145736 | tf_op jit(solution)/shard_map/ppermute | solution.py:358
  315.2 13.1 %copy-start = (bf16[512,1024]{1,0:T(8,128)(2,1)}, bf16[512,1024]{1,0:T(8,128)(2,1)S(1)}, u32[]{:S(2)}) copy-start(bf16[512,1024]{1,0:T(8,128)(2,1)S(1)} %get-tuple-element.62) | copy-start | bytes 3145732
  327.2 9.2 %collective-permute-start.2 = (bf16[512,2048]{1,0:T(8,128)(2,1)}, bf16[512,2048]{1,0:T(8,128)(2,1)}, u32[]{:S(2)}, u32[]{:S(2)}) collective-permute-start(bf16[512,2048]{1,0:T(8,128)(2,1)} %shard_map.122), channel_id=1, source_target_pairs={{0,1},{1,0},{2,3},{3,2},{4,5},{5,4},{6,7},{7,6},{8,9},{9,8},{10,11... | collective-permute-start | bytes 6291464 | tf_op jit(solution)/shard_map/ppermute | solution.py:243
  332.5 3.9 copy-start.6
  433.8 5.0 copy-start.15
  433.8 4.2 collective-permute-start.3
  449.3 7.8 copy-start.1
  449.3 7.8 copy-start.4
  458.8 26.8 %collective-permute-start.4 = (bf16[512,1024]{1,0:T(8,128)(2,1)}, bf16[512,1024]{1,0:T(8,128)(2,1)}, u32[]{:S(2)}, u32[]{:S(2)}) collective-permute-start(bf16[512,1024]{1,0:T(8,128)(2,1)} %fusion.42), channel_id=1, source_target_pairs={{16,0},{17,1},{18,2},{19,3},{20,4},{21,5},{22,6},{23,7},{24,8},{25... | collective-permute-start | bytes 3145736 | tf_op jit(solution)/shard_map/ppermute | solution.py:358
  460.1 26.9 %copy-start.10 = (bf16[512,2688]{1,0:T(8,128)(2,1)S(1)}, bf16[512,2688]{1,0:T(8,128)(2,1)}, u32[]{:S(2)}) copy-start(bf16[512,2688]{1,0:T(8,128)(2,1)} %get-tuple-element.60) | copy-start | bytes 8257540
  487.0 20.9 %copy-start.8 = (bf16[512,1024]{1,0:T(8,128)(2,1)}, bf16[512,1024]{1,0:T(8,128)(2,1)S(1)}, u32[]{:S(2)}) copy-start(bf16[512,1024]{1,0:T(8,128)(2,1)S(1)} %broadcast_select_fusion) | copy-start | bytes 3145732
  507.8 3.8 copy-start.7
  514.3 159.5 %reduce-scatter.11.cloned.1.call-start = ((), (), s32[]{:S(2)}) async-start(), calls=%async_computation.14 | async-start | bytes 5849088 | tf_op jit(solution)/shard_map/reduce_scatter | solution.py:367
  522.3 242.9 %reduce-scatter.5.cloned.1.call-start = ((), (), s32[]{:S(2)}) async-start(), calls=%async_computation.11 | async-start | bytes 6963200 | tf_op jit(solution)/shard_map/reduce_scatter | solution.py:367
  559.3 4.8 collective-permute-start.5
  560.4 4.6 copy-start.14
  568.3 7.1 copy-start.2
  593.8 298.1 %reduce-scatter.9.cloned.1.call-start = ((), (), s32[]{:S(2)}) async-start(), calls=%async_computation.13 | async-start | bytes 11698176 | tf_op jit(solution)/shard_map/reduce_scatter | solution.py:367
  615.4 38.9 %all-to-all-start.2 = ((bf16[8,64,1024]{2,1,0:T(8,128)(2,1)}), bf16[8,64,1024]{2,1,0:T(8,128)(2,1)S(1)}, u32[]{:S(2)}, u32[]{:S(2)}) async-start(bf16[8,64,1024]{2,1,0:T(8,128)(2,1)} %bitcast.105), calls=%async_computation.2 | async-start | bytes 2097152 | tf_op jit(solution)/shard_map/all_to_all | solution.py:228
  (6 other events, 10.9 us)
Sparse Core Ops, SparseCore 0:
  10.9 76.7 all-gather.6
  89.9 39.2 all-gather.12
  132.0 89.7 all-gather.8
  224.0 56.6 all-gather.10
  514.4 58.3 reduce-scatter.6
  577.1 96.6 reduce-scatter.10
  677.8 87.3 reduce-scatter.4
  769.8 122.0 reduce-scatter.8

commit v2 on v1

v2 whole, which is shorter than its diff:
```python
from functools import partial

import jax
import jax.numpy as jnp
from jax import lax
from jax.experimental import pallas as pl
from jax.experimental.pallas import tpu as pltpu
from jax.sharding import PartitionSpec as P

D = 1024
HEADS = 16
HEAD_DIM = 64
FF = 2624
FFP = 2688
FFB = 896
LANES = 128
PAIRS = D // LANES
WIDE = 4 * D + LANES
EPSILON = 1e-05
ROPE_BASE = 160000.0
NEG_FILL = -1e30
BF = jnp.bfloat16
F32 = jnp.float32
BOTH = ("ctx", "wshard")
VMEM = 60 * 1024 * 1024
NN = ((1,), (0,))
NT = ((1,), (1,))
TN = ((0,), (0,))
SMEM_SPEC = pl.BlockSpec(memory_space=pltpu.SMEM)


def dot(a, b, dims):
    return lax.dot_general(a, b, (dims, ((), ())), preferred_element_type=F32)


def after(value, *others):
    return lax.optimization_barrier((value,) + others)[0]


def shaped(shape, kind=BF):
    return jax.ShapeDtypeStruct(shape, kind)


def call(kernel, name, flops=0, moved=0, exps=0, **more):
    return pl.pallas_call(
        kernel,
        name=name,
        compiler_params=pltpu.CompilerParams(vmem_limit_bytes=VMEM),
        cost_estimate=pl.CostEstimate(
            flops=int(flops), bytes_accessed=int(moved), transcendentals=int(exps)
        ),
        **more,
    )


def whole(shape):
    return pl.BlockSpec(shape, lambda *_: (0,) * len(shape))


def rope_block(v, cosine, sine):
    lane = lax.broadcasted_iota(jnp.int32, v.shape, 1) % HEAD_DIM
    other = jnp.where(
        lane < HEAD_DIM // 2,
        pltpu.roll(v, LANES - HEAD_DIM // 2, 1),
        pltpu.roll(v, HEAD_DIM // 2, 1),
    )
    return v * cosine + other * sine


def norm_parts(values):
    center = values - jnp.mean(values, axis=-1, keepdims=True)
    spread = jnp.mean(center * center, axis=-1, keepdims=True)
    inverse = lax.rsqrt(spread + EPSILON)
    return center * inverse, inverse


def norm_back(values, gain_row, grad):
    hat, inverse = norm_parts(values)
    scaled = grad * gain_row
    back = inverse * (
        scaled
        - jnp.mean(scaled, axis=-1, keepdims=True)
        - hat * jnp.mean(scaled * hat, axis=-1, keepdims=True)
    )
    return back, jnp.sum(grad * hat, axis=0, keepdims=True)


def head_mask(shape, head):
    lane = lax.broadcasted_iota(jnp.int32, shape, 1)
    return (lane >= HEAD_DIM) if head else (lane < HEAD_DIM)


def pick(mask, v, other=0.0):
    return jnp.where(mask, v, jnp.full(v.shape, other, v.dtype))


def gains_of(wide):
    def kernel(w_ref, out_ref):
        out_ref[...] = w_ref[...].astype(F32).T[:8]

    return call(
        kernel,
        "gains",
        grid=(1,),
        in_specs=[pl.BlockSpec((D, LANES), lambda j: (0, 4 * D // LANES))],
        out_specs=whole((8, D)),
        out_shape=shaped((8, D), F32),
    )(wide)


def keys_values(x, gains, wide, cosine, sine):
    rows = x.shape[0]
    block = 512

    def kernel(x_ref, gain_ref, w_ref, cos_ref, sin_ref, a_ref, out_ref):
        @pl.when(pl.program_id(0) == 0)
        def _():
            hat, _ = norm_parts(x_ref[...].astype(F32))
            a_ref[...] = (hat * gain_ref[0:1]).astype(BF)

        m = dot(a_ref[...], w_ref[...], NN)
        for j in range(block // LANES):
            at = slice(j * LANES, (j + 1) * LANES)
            v = m[:, at]
            if j % 2 == 0:
                v = rope_block(v, cos_ref[...], sin_ref[...])
            out_ref[:, at] = v.astype(BF)

    return call(
        kernel,
        "keys_values",
        flops=2 * rows * D * 2 * D,
        moved=2 * (2 * D * D + 4 * rows * D),
        grid=(2 * D // block,),
        in_specs=[
            whole((rows, D)),
            whole((8, D)),
            pl.BlockSpec((D, block), lambda j: (0, j)),
            whole((rows, LANES)),
            whole((rows, LANES)),
        ],
        out_specs=[whole((rows, D)), pl.BlockSpec((rows, block), lambda j: (0, j))],
        out_shape=[shaped((rows, D)), shaped((rows, 2 * D))],
    )(x, gains, wide, cosine, sine)


def queries_of(a, wide, cosine, sine):
    rows = a.shape[0]
    block = 512

    def kernel(a_ref, w_ref, cos_ref, sin_ref, out_ref):
        m = dot(a_ref[...], w_ref[...], NN)
        for j in range(block // LANES):
            at = slice(j * LANES, (j + 1) * LANES)
            out_ref[:, at] = rope_block(m[:, at], cos_ref[...], sin_ref[...]).astype(BF)

    return call(
        kernel,
        "queries",
        flops=2 * rows * D * D,
        moved=2 * (D * D + 2 * rows * D),
        grid=(D // block,),
        in_specs=[
            whole((rows, D)),
            pl.BlockSpec((D, block), lambda j: (0, 2 * D // block + j)),
            whole((rows, LANES)),
            whole((rows, LANES)),
        ],
        out_specs=pl.BlockSpec((rows, block), lambda j: (0, j)),
        out_shape=shaped((rows, D)),
    )(a, wide, cosine, sine)


def attend(q, kv_list, segq, segk):
    rows = q.shape[0]
    members = len(kv_list)
    keys = members * rows

    def kernel(q_ref, segq_ref, segk_ref, *refs):
        kv_refs, (o_ref, lse_ref, bias_ref) = refs[:members], refs[members:]

        @pl.when(pl.program_id(0) == 0)
        def _():
            bias_ref[...] = jnp.where(segk_ref[...] == segq_ref[...], 0.0, NEG_FILL)

        k = jnp.concatenate([r[:, :LANES] for r in kv_refs], axis=0)
        v = jnp.concatenate([r[:, LANES:] for r in kv_refs], axis=0)
        q = q_ref[...] * jnp.asarray(HEAD_DIM**-0.5, BF)
        parts, stats = [], []
        for head in range(2):
            qh = pick(head_mask(q.shape, head), q)
            vh = pick(head_mask(v.shape, head), v, 1.0)
            s = dot(k, qh, NT) + bias_ref[...]
            top = jnp.max(s, axis=0, keepdims=True)
            e = jnp.exp(s - top).astype(BF)
            u = dot(vh, e, TN)
            low, high = u[:HEAD_DIM], u[HEAD_DIM:]
            value, total = (high, low) if head else (low, high)
            parts.append(value / total)
            stats.append(top + jnp.log(total[:1]))
        o_ref[...] = jnp.concatenate(parts, axis=0).T.astype(BF)
        lse_ref[0] = jnp.concatenate(stats, axis=0)

    return call(
        kernel,
        "attend",
        flops=8 * rows * keys * D,
        moved=2 * (2 * rows * D + 2 * keys * D),
        exps=rows * keys * HEADS,
        grid=(PAIRS,),
        in_specs=[
            pl.BlockSpec((rows, LANES), lambda p: (0, p)),
            whole((1, rows)),
            whole((keys, 1)),
        ]
        + [pl.BlockSpec((rows, 2 * LANES), lambda p: (0, p))] * members,
        out_specs=[
            pl.BlockSpec((rows, LANES), lambda p: (0, p)),
            pl.BlockSpec((1, 2, rows), lambda p: (p, 0, 0)),
        ],
        out_shape=[shaped((rows, D)), shaped((PAIRS, 2, rows), F32)],
        scratch_shapes=[pltpu.VMEM((keys, rows), F32)],
    )(q, segq, segk, *kv_list)


def project(x, o, gains, wide):
    rows = x.shape[0]
    block = 512
    steps = D // block

    def kernel(x_ref, o_ref, gain_ref, w_ref, h_ref, b_ref):
        j = pl.program_id(0)
        at = pl.ds(pl.multiple_of(j * block, block), block)
        h_ref[:, at] = x_ref[:, at].astype(F32) + dot(o_ref[...], w_ref[...], NN)

        @pl.when(j == steps - 1)
        def _():
            hat, _ = norm_parts(h_ref[...])
            b_ref[...] = (hat * gain_ref[1:2]).astype(BF)

    return call(
        kernel,
        "project",
        flops=2 * rows * D * D,
        moved=2 * D * D + 10 * rows * D,
        grid=(steps,),
        in_specs=[
            whole((rows, D)),
            whole((rows, D)),
            whole((8, D)),
            pl.BlockSpec((D, block), lambda j: (0, 3 * D // block + j)),
        ],
        out_specs=[whole((rows, D)), whole((rows, D))],
        out_shape=[shaped((rows, D), F32), shaped((rows, D))],
    )(x, o, gains, wide)


def ffn_in(b, w_in, keep):
    rows = b.shape[0]
    steps = FFP // FFB

    def kernel(b_ref, wa_ref, wg_ref, z_ref, *kept):
        a = dot(b_ref[...], wa_ref[...], NN)
        g = dot(b_ref[...], wg_ref[...], NN)
        phi = 0.5 * (1.0 + lax.erf(a * 0.7071067811865476))
        act = a * phi
        z_ref[...] = (act * g).astype(BF)
        if keep:
            density = 0.3989422804014327 * jnp.exp(-0.5 * a * a)
            kept[0][...] = act.astype(BF)
            kept[1][...] = ((phi + a * density) * g).astype(BF)

    out_spec = pl.BlockSpec((rows, FFB), lambda j: (0, j))
    count = 3 if keep else 1
    return call(
        kernel,
        "ffn_in",
        flops=4 * rows * D * FFP,
        moved=2 * (2 * D * FFP + rows * D + count * rows * FFP),
        grid=(steps,),
        in_specs=[
            whole((rows, D)),
            pl.BlockSpec((D, FFB), lambda j: (0, j)),
            pl.BlockSpec((D, FFB), lambda j: (0, steps + j)),
        ],
        out_specs=[out_spec] * count,
        out_shape=[shaped((rows, FFP))] * count,
    )(b, w_in, w_in)


def ffn_out(h, z, w_back):
    rows = h.shape[0]
    block = 256

    def kernel(h_ref, z_ref, w_ref, out_ref):
        out_ref[...] = (h_ref[...] + dot(z_ref[...], w_ref[...], NT)).astype(BF)

    return call(
        kernel,
        "ffn_out",
        flops=2 * rows * D * FFP,
        moved=2 * (D * FFP + rows * FFP + 3 * rows * D),
        grid=(D // block,),
        in_specs=[
            pl.BlockSpec((rows, block), lambda j: (0, j)),
            whole((rows, FFP)),
            pl.BlockSpec((block, FFP), lambda j: (j, 0)),
        ],
        out_specs=pl.BlockSpec((rows, block), lambda j: (0, j)),
        out_shape=shaped((rows, D)),
    )(h, z, w_back)


def ffn_back(grad, act, slope, w_back):
    rows = grad.shape[0]

    def kernel(g_ref, act_ref, slope_ref, w_ref, da_ref, dg_ref):
        dz = dot(g_ref[...], w_ref[...], NN)
        da_ref[...] = (dz * slope_ref[...].astype(F32)).astype(BF)
        dg_ref[...] = (dz * act_ref[...].astype(F32)).astype(BF)

    spec = pl.BlockSpec((rows, FFB), lambda j: (0, j))
    return call(
        kernel,
        "ffn_back",
        flops=2 * rows * D * FFP,
        moved=2 * (D * FFP + 4 * rows * FFP + rows * D),
        grid=(FFP // FFB,),
        in_specs=[whole((rows, D)), spec, spec, pl.BlockSpec((D, FFB), lambda j: (0, j))],
        out_specs=[spec, spec],
        out_shape=[shaped((rows, FFP))] * 2,
    )(grad, act, slope, w_back)


def hidden_back(grad, da, dg, h, gains, w_in):
    rows = grad.shape[0]
    block = 256
    steps = D // block

    def kernel(g_ref, da_ref, dg_ref, h_ref, gain_ref, w_ref, dh_ref, low_ref, sum_ref):
        j = pl.program_id(0)
        at = pl.ds(pl.multiple_of(j * block, block), block)
        dh_ref[:, at] = dot(da_ref[...], w_ref[:, :FFP], NT) + dot(dg_ref[...], w_ref[:, FFP:], NT)

        @pl.when(j == steps - 1)
        def _():
            back, total = norm_back(h_ref[...], gain_ref[1:2], dh_ref[...])
            dh = g_ref[...].astype(F32) + back
            dh_ref[...] = dh
            low_ref[...] = dh.astype(BF)
            sum_ref[...] = total

    return call(
        kernel,
        "hidden_back",
        flops=4 * rows * D * FFP,
        moved=2 * (2 * D * FFP + 2 * rows * FFP + 6 * rows * D),
        grid=(steps,),
        in_specs=[
            whole((rows, D)),
            whole((rows, FFP)),
            whole((rows, FFP)),
            whole((rows, D)),
            whole((8, D)),
            pl.BlockSpec((block, 2 * FFP), lambda j: (j, 0)),
        ],
        out_specs=[whole((rows, D)), whole((rows, D)), whole((1, D))],
        out_shape=[shaped((rows, D), F32), shaped((rows, D)), shaped((1, D), F32)],
    )(grad, da, dg, h, gains, w_in)


def attend_back(q, kv_list, dh_low, o, lse, segq, segk, wide, cosine, sine):
    rows = q.shape[0]
    members = len(kv_list)
    keys = members * rows

    def kernel(q_ref, dh_ref, w_ref, o_ref, lse_ref, segq_ref, segk_ref, cos_ref, sin_ref, *refs):
        kv_refs, (dq_ref, *dkv_refs, bias_ref) = refs[:members], refs[members:]

        @pl.when(pl.program_id(0) == 0)
        def _():
            bias_ref[...] = jnp.where(segk_ref[...] == segq_ref[...], 0.0, NEG_FILL)

        k = jnp.concatenate([r[:, :LANES] for r in kv_refs], axis=0)
        v = jnp.concatenate([r[:, LANES:] for r in kv_refs], axis=0)
        do = dot(dh_ref[...], w_ref[...], NT).astype(BF)
        q = q_ref[...] * jnp.asarray(HEAD_DIM**-0.5, BF)
        prod = (do.astype(F32) * o_ref[...].astype(F32)).T
        lse = lse_ref[0]
        dq = dk = dv = 0.0
        for head in range(2):
            mask = head_mask(q.shape, head)
            qh, doh = pick(mask, q), pick(mask, do)
            kh = pick(head_mask(k.shape, head), k)
            delta = jnp.sum(prod[head * HEAD_DIM : (head + 1) * HEAD_DIM], axis=0, keepdims=True)
            s = dot(k, qh, NT) + bias_ref[...]
            p = jnp.exp(s - lse[head : head + 1])
            ds = (p * (dot(v, doh, NT) - delta)).astype(BF)
            dv += dot(p.astype(BF), doh, NN)
            dk += dot(ds, qh, NN)
            dq += dot(ds, kh, TN)
        dq = rope_block(dq * HEAD_DIM**-0.5, cos_ref[...], -sin_ref[...])
        dq_ref[...] = dq.astype(BF)
        for m, out in enumerate(dkv_refs):
            out[:, :LANES] = dk[m * rows : (m + 1) * rows].astype(BF)
            out[:, LANES:] = dv[m * rows : (m + 1) * rows].astype(BF)

    spec = pl.BlockSpec((rows, LANES), lambda p: (0, p))
    kv_spec = pl.BlockSpec((rows, 2 * LANES), lambda p: (0, p))
    results = call(
        kernel,
        "attend_back",
        flops=20 * rows * keys * D,
        moved=2 * (6 * rows * D + 4 * keys * D),
        exps=rows * keys * HEADS,
        grid=(PAIRS,),
        in_specs=[
            spec,
            whole((rows, D)),
            pl.BlockSpec((LANES, D), lambda p: (p, 3)),
            spec,
            pl.BlockSpec((1, 2, rows), lambda p: (p, 0, 0)),
            whole((1, rows)),
            whole((keys, 1)),
            whole((rows, LANES)),
            whole((rows, LANES)),
        ]
        + [kv_spec] * members,
        out_specs=[spec] + [kv_spec] * members,
        out_shape=[shaped((rows, D))] + [shaped((rows, 2 * D))] * members,
        scratch_shapes=[pltpu.VMEM((keys, rows), F32)],
    )(q, dh_low, wide, o, lse, segq, segk, cosine, sine, *kv_list)
    return results[0], results[1:]


def input_back(x, dh, dq, dkv_list, gains, wide, cosine, sine):
    rows = x.shape[0]
    members = len(dkv_list)
    block = 256
    steps = D // block

    def kernel(x_ref, dh_ref, dq_ref, gain_ref, w_ref, cos_ref, sin_ref, *refs):
        dkv_refs, (dx_ref, dm_ref, sum_ref, da_ref) = refs[:members], refs[members:]
        j = pl.program_id(0)

        @pl.when(j == 0)
        def _():
            for b in range(2 * PAIRS):
                at = slice(b * LANES, (b + 1) * LANES)
                v = dkv_refs[0][:, at].astype(F32)
                for r in dkv_refs[1:]:
                    v += r[:, at].astype(F32)
                if b % 2 == 0:
                    v = rope_block(v, cos_ref[...], -sin_ref[...])
                dm_ref[:, at] = v.astype(BF)

        at = pl.ds(pl.multiple_of(j * block, block), block)
        da_ref[:, at] = dot(dm_ref[...], w_ref[:, : 2 * D], NT) + dot(
            dq_ref[...], w_ref[:, 2 * D :], NT
        )

        @pl.when(j == steps - 1)
        def _():
            back, total = norm_back(x_ref[...].astype(F32), gain_ref[0:1], da_ref[...])
            dx_ref[...] = (dh_ref[...] + back).astype(BF)
            sum_ref[...] = total

    return call(
        kernel,
        "input_back",
        flops=6 * rows * D * D,
        moved=2 * (3 * D * D + (2 * members + 7) * rows * D),
        grid=(steps,),
        in_specs=[
            whole((rows, D)),
            whole((rows, D)),
            whole((rows, D)),
            whole((8, D)),
            pl.BlockSpec((block, 3 * D), lambda j: (j, 0)),
            whole((rows, LANES)),
            whole((rows, LANES)),
        ]
        + [whole((rows, 2 * D))] * members,
        out_specs=[whole((rows, D)), whole((rows, 2 * D)), whole((1, D))],
        out_shape=[shaped((rows, D)), shaped((rows, 2 * D)), shaped((1, D), F32)],
        scratch_shapes=[pltpu.VMEM((rows, D), F32)],
    )(x, dh, dq, gains, wide, cosine, sine, *dkv_list)


def weight_rows(order, rows, pairs, extra=None):
    count = order.shape[0]
    tokens = pairs[0][0].shape[0]
    flat, columns = [], 0
    for left, rights in pairs:
        flat += [left] + list(rights)
        columns += sum(r.shape[1] for r in rights)
    if extra is not None:
        flat.append(extra)
        columns += LANES

    def kernel(order_ref, *refs):
        ins, out_ref, turned_ref, left_ref = refs[:-3], refs[-3], refs[-2], refs[-1]
        at = where = 0
        for left, rights in pairs:
            turned_ref[...] = ins[where][...].T
            where += 1
            for n in range(count):
                start = pl.multiple_of(order_ref[n] * rows, rows)
                left_ref[n * rows : (n + 1) * rows] = turned_ref[pl.ds(start, rows)]
            for right in rights:
                width = right.shape[1]
                for begin in range(0, width, 512):
                    end = min(begin + 512, width)
                    out_ref[:, at + begin : at + end] = dot(
                        left_ref[...], ins[where][:, begin:end], NN
                    ).astype(BF)
                at += width
                where += 1
        if extra is not None:
            for n in range(count):
                start = pl.multiple_of(order_ref[n] * rows, rows)
                out_ref[n * rows : (n + 1) * rows, at:] = ins[where][pl.ds(start, rows)]

    return call(
        kernel,
        "weight_rows",
        flops=2 * count * rows * tokens * columns,
        moved=2 * (count * rows * columns + sum(v.size for v in flat)),
        in_specs=[SMEM_SPEC] + [pl.BlockSpec(memory_space=pltpu.VMEM)] * len(flat),
        out_specs=pl.BlockSpec(memory_space=pltpu.VMEM),
        out_shape=shaped((count * rows, columns)),
        scratch_shapes=[
            pltpu.VMEM((D, tokens), BF),
            pltpu.VMEM((count * rows, tokens), BF),
        ],
    )(order, *flat)


def ring_add(core, mine, other, moving, rows, first, blocks, partial_moving):
    columns = mine.shape[1]

    def kernel(core_ref, mine_ref, other_ref, *refs):
        total = mine_ref[...].astype(F32) + other_ref[...].astype(F32)
        if moving is None:
            refs[0][...] = total.astype(BF)
            return
        moved = refs[0][...].astype(F32)
        if partial_moving:
            moved = jnp.where(core_ref[0] == pl.program_id(0), moved, 0.0)
        refs[1][...] = (total + moved).astype(BF)

    spec = pl.BlockSpec((rows, columns), lambda j: (first + j, 0))
    ins, specs = [core, mine, other], [SMEM_SPEC, spec, spec]
    if moving is not None:
        ins.append(moving)
        specs.append(
            pl.BlockSpec((rows, columns), (lambda j: (0, 0)) if partial_moving else (lambda j: (j, 0)))
        )
    return call(
        kernel,
        "ring_add",
        flops=2 * blocks * rows * columns,
        moved=8 * blocks * rows * columns,
        grid=(blocks,),
        in_specs=specs,
        out_specs=pl.BlockSpec((rows, columns), lambda j: (j, 0)),
        out_shape=shaped((blocks * rows, columns)),
    )(*ins)


class Plan:
    def __init__(self, boundary):
        self.micro = boundary.shape[1]
        self.tok_rows = boundary.shape[3]
        self.n_ctx = lax.axis_size("ctx")
        self.nw = lax.axis_size("wshard")
        self.g = self.n_ctx // (self.micro * self.nw)
        self.r = self.tok_rows // (self.g * self.nw)
        self.i = lax.axis_index("ctx")
        self.w = lax.axis_index("wshard")
        self.rows = self.n_ctx * self.r
        self.members = self.g * self.nw
        count = self.n_ctx
        chips = [2 * p if p < count // 2 else 2 * (count - 1 - p) + 1 for p in range(count)]
        self.half = count // 2
        self.way = 1 - 2 * self.w
        self.ring_pairs = []
        for p in range(count):
            self.ring_pairs.append((chips[p] * 2, chips[(p + 1) % count] * 2))
            self.ring_pairs.append((chips[p] * 2 + 1, chips[(p - 1) % count] * 2 + 1))
        place = jnp.where(self.i % 2 == 0, self.i // 2, count - 1 - self.i // 2)

        def chip(at):
            at = at % count
            return jnp.where(at < count // 2, 2 * at, 2 * (count - 1 - at) + 1)

        self.behind = [chip(place - self.way * k) for k in range(self.half + 1)]
        self.ahead = [chip(place + self.way * k) for k in range(self.half + 1)]
        self.wrows = D // (self.n_ctx * self.nw)
        near = range(self.half - 1, 0, -1)
        theirs = [2 * self.ahead[self.half] + 1 - self.w]
        mine = [2 * self.ahead[self.half] + self.w]
        for k in near:
            theirs += [2 * self.behind[k], 2 * self.behind[k] + 1]
            mine += [2 * self.ahead[k], 2 * self.ahead[k] + 1]
        mine += [2 * self.i, 2 * self.i + 1]
        self.theirs = jnp.stack(theirs).astype(jnp.int32)
        self.mine = jnp.stack(mine).astype(jnp.int32)
        self.core = self.w[None].astype(jnp.int32)

    def swap(self, array):
        return lax.ppermute(array, "wshard", [(0, 1), (1, 0)])

    def step(self, array):
        return lax.ppermute(array, BOTH, self.ring_pairs)

    def in_order(self, own, other):
        first = self.w == 0
        return jnp.concatenate(
            [jnp.where(first, own, other), jnp.where(first, other, own)], axis=0
        )

    def to_sequences(self, local):
        parts = local.reshape(self.micro, self.g, self.nw, self.r, D)
        parts = lax.all_to_all(parts.transpose(2, 0, 1, 3, 4), "wshard", 0, 0, tiled=True)
        parts = parts.transpose(1, 0, 2, 3, 4).reshape(self.n_ctx, self.r, D)
        return lax.all_to_all(parts, "ctx", 0, 0, tiled=True).reshape(self.rows, D)

    def from_sequences(self, rows):
        parts = lax.all_to_all(rows.reshape(self.n_ctx, self.r, D), "ctx", 0, 0, tiled=True)
        parts = parts.reshape(self.micro, self.nw, self.g, self.r, D).transpose(1, 0, 2, 3, 4)
        parts = lax.all_to_all(parts, "wshard", 0, 0, tiled=True)
        return parts.transpose(1, 2, 0, 3, 4).reshape(self.micro, self.tok_rows, D)

    def gather_weights(self, streams):
        whole_of, token = {}, {}
        rows = self.wrows

        def put(name, block, chip):
            whole_of[name] = lax.dynamic_update_index_in_dim(whole_of[name], block, chip, 0)

        def travel(name, shard, dep):
            whole_of[name] = jnp.zeros((self.n_ctx, self.nw * rows, shard.shape[1]), BF)
            current = self.in_order(shard, self.swap(shard))
            put(name, current, self.i)
            if dep is not None:
                current = after(current, dep)
            for k in range(1, self.half):
                current = self.step(current)
                yield current
                put(name, current, self.behind[k])
                put(name, self.swap(current), self.ahead[k])
            part = lax.dynamic_slice_in_dim(current, self.w * rows, rows, 0)
            part = self.step(part)
            yield part
            put(name, self.in_order(part, self.swap(part)), self.behind[self.half])

        def lane(items):
            dep = None
            for name, shard in items:
                for dep in travel(name, shard, dep):
                    yield dep

        lanes = [lane(items) for items in streams]
        while lanes:
            for one in list(lanes):
                if next(one, None) is None:
                    lanes.remove(one)
        return {n: v.reshape(D, v.shape[2]) for n, v in whole_of.items()}

    def reduce_weights(self, pairs, extra=None):
        rows = self.wrows
        other = self.swap(weight_rows(self.theirs, rows, pairs, extra))
        mine = weight_rows(self.mine, rows, pairs, extra)
        moving = self.step(ring_add(self.core, mine, other, None, rows, 0, 1, False))
        at = 1
        for k in range(self.half - 1, 0, -1):
            moving = self.step(
                ring_add(self.core, mine, other, moving, rows, at, 2, k == self.half - 1)
            )
            at += 2
        final = moving.astype(F32) + mine[at * rows :].astype(F32)
        keep = lax.dynamic_slice_in_dim(final, self.w * rows, rows, 0)
        give = lax.dynamic_slice_in_dim(final, (1 - self.w) * rows, rows, 0)
        return keep + self.swap(give.astype(BF)).astype(F32)

    def rotation(self, by):
        pairs = []
        for flat in range(self.n_ctx * self.nw):
            group, place = divmod(flat, self.members)
            pairs.append((flat, group * self.members + (place + by) % self.members))
        return pairs

    def gather_rows(self, rows):
        return [rows] + [
            lax.ppermute(rows, BOTH, self.rotation(by)) for by in range(1, self.members)
        ]

    def scatter_rows(self, terms):
        return [terms[0]] + [
            lax.ppermute(terms[by], BOTH, self.rotation(-by)) for by in range(1, self.members)
        ]


def interleave(keys, values):
    lead = keys.shape[0]
    both = jnp.stack([keys.reshape(lead, PAIRS, LANES), values.reshape(lead, PAIRS, LANES)], axis=2)
    return both.reshape(lead, 2 * D)


def apart(both):
    lead = both.shape[0]
    both = both.reshape(lead, PAIRS, 2, LANES)
    return both[:, :, 0].reshape(lead, D), both[:, :, 1].reshape(lead, D)


def body(
    boundary, segment_ids, qkv_weight, attn_out_weight, ffn_in_weight, ffn_out_weight, norm_gains
):
    section = lax.axis_index("section")
    sections = lax.axis_size("section")
    plan = Plan(boundary)
    rows = plan.rows
    own = plan.to_sequences(boundary[0, :, 0])

    pad = FFP - FF
    wide_shard = jnp.concatenate(
        [
            interleave(qkv_weight[0][:, D : 2 * D], qkv_weight[0][:, 2 * D :]),
            qkv_weight[0][:, :D],
            attn_out_weight[0],
            jnp.pad(norm_gains[0].T, ((0, 0), (0, LANES - 2))),
        ],
        axis=1,
    )
    in_shard = jnp.concatenate(
        [
            jnp.pad(ffn_in_weight[0][:, :FF], ((0, 0), (0, pad))),
            jnp.pad(ffn_in_weight[0][:, FF:], ((0, 0), (0, pad))),
        ],
        axis=1,
    )
    back_shard = jnp.pad(ffn_out_weight[0].T, ((0, 0), (0, pad)))
    weights = plan.gather_weights(
        [[("wide", wide_shard), ("back", back_shard)], [("in", in_shard)]]
    )
    wide, w_in, w_back = weights["wide"], weights["in"], weights["back"]
    gains = gains_of(wide)

    ids = segment_ids[:, 0]
    ids = plan.in_order(ids[None], plan.swap(ids[None])).transpose(1, 0, 2)
    ids = jnp.repeat(ids.reshape(plan.micro * plan.nw, plan.tok_rows), plan.g, axis=0)
    line = lax.all_to_all(ids, "ctx", 0, 0, tiled=True).reshape(-1)
    grid = line.reshape(plan.n_ctx, plan.members, plan.r)
    place = (plan.i % plan.g) * plan.nw + plan.w
    seg_pieces = [
        lax.dynamic_index_in_dim(grid, (place - by) % plan.members, 1, keepdims=False).reshape(rows)
        for by in range(plan.members)
    ]
    segq = seg_pieces[0]
    segk = jnp.concatenate(seg_pieces)
    token = (
        lax.broadcasted_iota(jnp.int32, (plan.n_ctx, plan.r), 0) * plan.tok_rows
        + place * plan.r
        + lax.broadcasted_iota(jnp.int32, (plan.n_ctx, plan.r), 1)
    ).reshape(rows)
    first = jnp.sum((line[None, :] < segq[:, None]).astype(jnp.int32), axis=1)
    position = (token - first).astype(F32)
    exponent = jnp.arange(HEAD_DIM // 2, dtype=F32) * (-2.0 / HEAD_DIM)
    angles = position[:, None] * (ROPE_BASE**exponent)[None, :]
    cosine, sine = jnp.cos(angles), jnp.sin(angles)
    cos_rows = jnp.concatenate([cosine] * 4, axis=1)
    sin_rows = jnp.concatenate([-sine, sine] * 2, axis=1)
    segq_row, segk_col = segq[None, :], segk[:, None]

    def forward(x, keep):
        a, kv = keys_values(x, gains, wide, cos_rows, sin_rows)
        kv_list = plan.gather_rows(kv)
        q = queries_of(a, wide, cos_rows, sin_rows)
        o, lse = attend(q, kv_list, segq_row, segk_col)
        h, b = project(x, o, gains, wide)
        z, *kept = ffn_in(b, w_in, keep)
        out = ffn_out(h, z, w_back)
        return out, (x, a, q, kv_list, o, lse, h, b, z, kept)

    def backward(stash, grad, with_weights):
        x, a, q, kv_list, o, lse, h, b, z, (act, slope) = stash
        sums = []
        if with_weights:
            sums.append(plan.reduce_weights([(grad, [z])]))
        da, dg = ffn_back(grad, act, slope, w_back)
        if with_weights:
            sums.append(plan.reduce_weights([(b, [da, dg])]))
        dh, dh_low, gain_second = hidden_back(grad, da, dg, h, gains, w_in)
        dq, terms = attend_back(
            q, kv_list, dh_low, o, lse, segq_row, segk_col, wide, cos_rows, sin_rows
        )
        dkv_list = plan.scatter_rows(terms)
        dx, dkv, gain_first = input_back(x, dh, dq, dkv_list, gains, wide, cos_rows, sin_rows)
        if with_weights:
            cols = jnp.concatenate([gain_first, gain_second], axis=0).T
            cols = jnp.pad(cols, ((0, 0), (0, LANES - 2))).astype(BF)
            sums.append(plan.reduce_weights([(a, [dkv, dq]), (o, [dh_low])], cols))
        return dx, sums

    def handed(array, by):
        pairs = [(s, s + by) for s in range(sections) if 0 <= s + by < sections]
        return lax.ppermute(array, "section", pairs)

    first_out, _ = forward(own, False)
    x_in = jnp.where(section == 0, own, handed(first_out, 1))
    out, stash = forward(x_in, True)
    first_dx, _ = backward(stash, own, False)
    grad_in = jnp.where(section == sections - 1, own, handed(first_dx, -1))
    dx, (g_back, g_in, g_wide) = backward(stash, grad_in, True)
    boundary_local = plan.from_sequences(jnp.where(section == 0, dx, out))
    g_key, g_value = apart(g_wide[:, : 2 * D])
    return (
        boundary_local[None, :, None],
        jnp.concatenate([g_wide[:, 2 * D : 3 * D], g_key, g_value], axis=1)[None],
        g_wide[None, :, 3 * D : 4 * D],
        jnp.concatenate([g_in[:, :FF], g_in[:, FFP : FFP + FF]], axis=1)[None],
        g_back[:, :FF].T[None],
        g_wide[:, 4 * D : 4 * D + 2].T[None],
    )


def solution(mesh):
    placed = (
        P("section", None, "wshard", "ctx", None),
        P(None, "wshard", "ctx"),
        P("section", ("ctx", "wshard"), None),
        P("section", ("ctx", "wshard"), None),
        P("section", ("ctx", "wshard"), None),
        P("section", None, ("ctx", "wshard")),
        P("section", None, ("ctx", "wshard")),
    )
    return jax.shard_map(
        body,
        mesh=mesh,
        in_specs=placed,
        out_specs=(placed[0],) + placed[2:],
        check_vma=False,
    )
```

time: 911 us -> 715 us (0.78)
  waiting for transfers between devices: 455 us -> 196 us
  Pallas kernels: 129 us -> 334 us
  matrix products: 160 us -> 0 us
  starting transfers between devices: 17.4 us -> 72.5 us
  blocking collectives: 58.4 us -> 4.21 us
  local copies, waits for them, and re-layouts: 20.3 us -> 67.5 us
  other arithmetic: 46.6 us -> 29.9 us
  between operations: 14.8 us -> 1.6 us
    reduce_scatter x4 -> x0, waiting for transfers between devices: 227 us -> none  [body(): lax.psum_scatter(t, BOTH, scatter_dimension=0, tiled=True).astype(F32)]
    pallas_call x10 -> x39, Pallas kernels: 129 us -> 334 us  [the longest x2 69.7 us: attend_back(): call(kernel, 'attend_back', flops=20 * rows * keys * D, moved=2 * (6 * ro...]
    dot_general x22 -> x0, matrix products: 160 us -> none  [dot(): return lax.dot_general(a, b, (dims, ((), ())), preferred_element_type=F32)]
    ppermute x4 -> x50, waiting for transfers between devices: 7.93 us -> 147 us  [the longest x24 142 us: step(): return lax.ppermute(array, BOTH, self.ring_pairs)]
    all_gather x4 -> x0, waiting for transfers between devices: 138 us -> none  [the longest x1 84.5 us: body(): w_in = lax.all_gather(in_shard, BOTH, axis=0, tiled=True)]
    all_gather x1 -> x0, blocking collectives: 48.9 us -> none  [body(): whole = lax.all_gather(segment_ids[:, 0], BOTH, axis=0)]
    ppermute x4 -> x50, starting transfers between devices: 2.41 us -> 47.4 us  [the longest x22 26.7 us: swap(): return lax.ppermute(array, 'wshard', [(0, 1), (1, 0)])]
    all_to_all x1, waiting for transfers between devices: 32.7 us -> 0.01 us  [from_sequences(): lax.all_to_all(rows.reshape(self.n_ctx, self.r, D), 'ctx', 0, 0, tiled=True)]
  transfers between devices with their start and end apart: 16 -> 56, of which waited for: 11 -> 19; matrix products, arithmetic and copies ran while one was open for 13% -> 11% of each run, Pallas kernels for 8% -> 25%
where the time goes in v2:
time: 715 us; the launch traced here: 706 us
  Pallas kernels  334 us (47%)
  waiting for transfers between devices  196 us (27%)
  starting transfers between devices  72.5 us (10%)
  local copies, waits for them, and re-layouts  67.5 us (9%)
  other arithmetic  29.9 us (4%)
    ppermute x24, waiting for transfers between devices, step(): return lax.ppermute(array, BOTH, self.ring_pairs)  142 us
    pallas_call x2, Pallas kernels, attend_back(): call(kernel, 'attend_back', flops=20 * rows * keys * D, moved=2 * (6 * ro...  69.7 us
    ppermute x2, waiting for transfers between devices, handed(): return lax.ppermute(array, 'section', pairs)  47.3 us
    pallas_call x6, Pallas kernels, weight_rows(): call(kernel, 'weight_rows', flops=2 * count * rows * tokens * columns, mo...  43.6 us
    pallas_call x2, Pallas kernels, attend(): call(kernel, 'attend', flops=8 * rows * keys * D, moved=2 * (2 * rows * D...  37.2 us
    pallas_call x12, Pallas kernels, ring_add(): call(kernel, 'ring_add', flops=2 * blocks * rows * columns, moved=8 * blo...  31.4 us
    pallas_call x2, Pallas kernels, hidden_back(): call(kernel, 'hidden_back', flops=4 * rows * D * FFP, moved=2 * (2 * D *...  28.6 us
    pallas_call x2, Pallas kernels, input_back(): call(kernel, 'input_back', flops=6 * rows * D * D, moved=2 * (3 * D * D +...  28.5 us
  transfers between devices with their start and end apart: 56, of which 19 were waited for; matrix products, arithmetic and copies ran while one was open for 11% of the time, Pallas kernels for 25%

profile of v2, /device:TPU:13, one launch (start us, length us, event | category | flops | bytes accessed | tf_op | source)
XLA Modules:
  0.0 706.0 jit_solution(11676894759778189960)
XLA Ops:
  54.9 6.9 collective-permute-done.1
  65.2 11.3 %collective-permute-done.12 = bf16[128,5376]{1,0:T(8,128)(2,1)S(1)} collective-permute-done((bf16[128,5376]{1,0:T(8,128)(2,1)S(1)}, bf16[128,5376]{1,0:T(8,128)(2,1)S(1)}, u32[]{:S(2)}, u32[]{:S(2)}) %collective-permute-start.12) | collective-permute-done | bytes 1376288 | tf_op jit(solution)/shard_map/ppermute | solution.py:615
  80.0 8.0 %collective-permute-done.3 = bf16[128,4224]{1,0:T(8,128)(2,1)S(1)} collective-permute-done((bf16[128,4224]{1,0:T(8,128)(2,1)S(1)}, bf16[128,4224]{1,0:T(8,128)(2,1)S(1)}, u32[]{:S(2)}, u32[]{:S(2)}) %collective-permute-start.3) | collective-permute-done | bytes 1081376 | tf_op jit(solution)/shard_map/ppermute | solution.py:615
  92.6 10.2 %collective-permute-done.14 = bf16[128,5376]{1,0:T(8,128)(2,1)S(1)} collective-permute-done((bf16[128,5376]{1,0:T(8,128)(2,1)S(1)}, bf16[128,5376]{1,0:T(8,128)(2,1)S(1)}, u32[]{:S(2)}, u32[]{:S(2)}) %collective-permute-start.14) | collective-permute-done | bytes 1376288 | tf_op jit(solution)/shard_map/ppermute | solution.py:615
  107.5 6.9 collective-permute-done.5
  119.0 15.9 %collective-permute-done.7 = bf16[64,4224]{1,0:T(8,128)(2,1)S(1)} collective-permute-done((bf16[64,4224]{1,0:T(8,128)(2,1)S(1)}, bf16[64,4224]{1,0:T(8,128)(2,1)S(1)}, u32[]{:S(2)}, u32[]{:S(2)}) %collective-permute-start.7) | collective-permute-done | bytes 540704 | tf_op jit(solution)/shard_map/ppermute | solution.py:615
  147.4 7.5 %keys_values.2 = (bf16[512,1024]{1,0:T(8,128)(2,1)}, bf16[512,2048]{1,0:T(8,128)(2,1)}) custom-call(bf16[512,1024]{1,0:T(8,128)(2,1)} %bitcast.142, f32[8,1024]{1,0:T(8,128)} %gains.1.gain_ref, bf16[1024,4224]{1,0:T(8,128)(2,1)} %bitcast.17.w_ref, f32[512,128]{1,0:T(8,128)} %get-tuple-element.121.cos_ref, f32[512,128]{1,0:T(8,128)} %get-tuple-element.122.sin_ref), custom_call_target="tpu_custom_call" | custom-call | flops 2147483648 | bytes 8388608 | tf_op jit(solution)/shard_map/keys_values/pallas_call | solution.py:129
  162.9 7.8 %collective-permute-done.23 = bf16[128,2688]{1,0:T(8,128)(2,1)S(1)} collective-permute-done((bf16[128,2688]{1,0:T(8,128)(2,1)}, bf16[128,2688]{1,0:T(8,128)(2,1)S(1)}, u32[]{:S(2)}, u32[]{:S(2)}) %collective-permute-start.23) | collective-permute-done | bytes 688160 | tf_op jit(solution)/shard_map/ppermute | solution.py:615
  190.3 18.6 %attend.2 = (bf16[512,1024]{1,0:T(8,128)(2,1)}, f32[8,2,512]{2,1,0:T(2,128)}) custom-call(bf16[512,1024]{1,0:T(8,128)(2,1)} %queries.2.q_ref, s32[1,512]{1,0:T(1,128)} %broadcast_in_dim_reshape.8.segq_ref, s32[1024,1]{1,0:T(8,128)} %copy.75.segk_ref, bf16[512,2048]{1,0:T(8,128)(2,1)} %get-tuple-element.41.refs_0_, ...), custom_call_target="tpu_custom_call" | custom-call | flops 4294967296 | bytes 6291456 | tf_op jit(solution)/shard_map/attend/pallas_call | solution.py:204
  214.4 10.5 %ffn_in.2.z_ref = bf16[512,2688]{1,0:T(8,128)(2,1)} custom-call(bf16[512,1024]{1,0:T(8,128)(2,1)} %get-tuple-element.44.b_ref, bf16[1024,5376]{1,0:T(8,128)(2,1)} %bitcast.33.wa_ref.wg_ref.w_ref, bf16[1024,5376]{1,0:T(8,128)(2,1)} %bitcast.33.wa_ref.wg_ref.w_ref), custom_call_target="tpu_custom_call" | custom-call | flops 5637144576 | bytes 14811136 | tf_op jit(solution)/shard_map/ffn_in/pallas_call | solution.py:275
  226.9 7.9 %ffn_out.2 = bf16[512,1024]{1,0:T(8,128)(2,1)} custom-call(f32[512,1024]{1,0:T(8,128)} %get-tuple-element.43.h_ref, bf16[512,2688]{1,0:T(8,128)(2,1)} %ffn_in.2.z_ref, bf16[1024,2688]{1,0:T(8,128)(2,1)} %bitcast.44.w_ref), custom_call_target="tpu_custom_call" | custom-call | flops 2818572288 | bytes 11403264 | tf_op jit(solution)/shard_map/ffn_out/pallas_call | solution.py:298
  238.2 22.6 %collective-permute-done.29 = bf16[512,1024]{1,0:T(8,128)(2,1)S(1)} collective-permute-done((bf16[512,1024]{1,0:T(8,128)(2,1)}, bf16[512,1024]{1,0:T(8,128)(2,1)S(1)}, u32[]{:S(2)}, u32[]{:S(2)}) %collective-permute-start.29) | collective-permute-done | bytes 1048608 | tf_op jit(solution)/shard_map/ppermute | solution.py:808
  261.9 7.5 %keys_values.3 = (bf16[512,1024]{1,0:T(8,128)(2,1)}, bf16[512,2048]{1,0:T(8,128)(2,1)}) custom-call(bf16[512,1024]{1,0:T(8,128)(2,1)} %broadcast_select_fusion.2.x_ref, f32[8,1024]{1,0:T(8,128)} %gains.1.gain_ref, bf16[1024,4224]{1,0:T(8,128)(2,1)} %bitcast.17.w_ref, f32[512,128]{1,0:T(8,128)} %get-tuple-element.121.cos_ref, ...), custom_call_target="tpu_custom_call" | custom-call | flops 2147483648 | bytes 8388608 | tf_op jit(solution)/shard_map/keys_values/pallas_call | solution.py:129
  276.4 18.6 %attend.3 = (bf16[512,1024]{1,0:T(8,128)(2,1)}, f32[8,2,512]{2,1,0:T(2,128)}) custom-call(bf16[512,1024]{1,0:T(8,128)(2,1)} %queries.3.q_ref, s32[1,512]{1,0:T(1,128)} %broadcast_in_dim_reshape.8.segq_ref, s32[1024,1]{1,0:T(8,128)} %copy.75.segk_ref, bf16[512,2048]{1,0:T(8,128)(2,1)} %get-tuple-element.47.refs_0_, bf16[512,2048]{1,0:T(8,128)(2,1)} %copy-done.24), custom_call_target="tpu_custom_call" | custom-call | flops 4294967296 | bytes 6291456 | tf_op jit(solution)/shard_map/attend/pallas_call | solution.py:204
  300.6 11.1 %ffn_in.3 = (bf16[512,2688]{1,0:T(8,128)(2,1)}, bf16[512,2688]{1,0:T(8,128)(2,1)}, bf16[512,2688]{1,0:T(8,128)(2,1)}) custom-call(bf16[512,1024]{1,0:T(8,128)(2,1)} %get-tuple-element.49.b_ref.refs_0_, bf16[1024,5376]{1,0:T(8,128)(2,1)} %bitcast.33.wa_ref.wg_ref.w_ref, bf16[1024,5376]{1,0:T(8,128)(2,1)} %bitcast.33.wa_ref.wg_ref.w_ref), custom_call_target="tpu_custom_call" | custom-call | flops 5637144576 | bytes 20316160 | tf_op jit(solution)/shard_map/ffn_in/pallas_call | solution.py:275
  311.7 10.0 %ffn_back.2 = (bf16[512,2688]{1,0:T(8,128)(2,1)}, bf16[512,2688]{1,0:T(8,128)(2,1)}) custom-call(bf16[512,1024]{1,0:T(8,128)(2,1)} %bitcast.144, bf16[512,2688]{1,0:T(8,128)(2,1)} %get-tuple-element.50.act_ref, bf16[512,2688]{1,0:T(8,128)(2,1)} %get-tuple-element.51.slope_ref, bf16[1024,2688]{1,0:T(8,128)(2,1)} %bitcast.44.w_ref), custom_call_target="tpu_custom_call" | custom-call | flops 2818572288 | bytes 17563648 | tf_op jit(solution)/shard_map/ffn_back/pallas_call | solution.py:323
  321.7 14.3 %hidden_back.2 = (f32[512,1024]{1,0:T(8,128)}, bf16[512,1024]{1,0:T(8,128)(2,1)}, f32[1,1024]{1,0:T(1,128)}) custom-call(bf16[512,1024]{1,0:T(8,128)(2,1)} %bitcast.145, bf16[512,2688]{1,0:T(8,128)(2,1)} %get-tuple-element.52.da_ref, bf16[512,2688]{1,0:T(8,128)(2,1)} %get-tuple-element.53.dg_ref, f32[512,1024]{1,0:T(8,128)} %get-tuple-element.54.h_ref, ...), custom_call_target="tpu_custom_call" | custom-call | flops 5637144576 | bytes 22806528 | tf_op jit(solution)/shard_map/hidden_back/pallas_call | solution.py:353
  335.9 35.1 %attend_back.2 = (bf16[512,1024]{1,0:T(8,128)(2,1)}, bf16[512,2048]{1,0:T(8,128)(2,1)}, bf16[512,2048]{1,0:T(8,128)(2,1)}) custom-call(bf16[512,1024]{1,0:T(8,128)(2,1)} %queries.3.q_ref, bf16[512,1024]{1,0:T(8,128)(2,1)} %get-tuple-element.56.dh_ref, bf16[1024,4224]{1,0:T(8,128)(2,1)} %bitcast.17.w_ref, bf16[512,1024]{1,0:T(8,128)(2,1)} %get-tuple-element.48.o_ref.refs_3_, ...), custom_call_target="tpu_custom_call" | custom-call | flops 10737418240 | bytes 14680064 | tf_op jit(solution)/shard_map/attend_back/pallas_call | solution.py:410
  376.8 14.0 %input_back.2 = (bf16[512,1024]{1,0:T(8,128)(2,1)}, bf16[512,2048]{1,0:T(8,128)(2,1)}, f32[1,1024]{1,0:T(1,128)}) custom-call(bf16[512,1024]{1,0:T(8,128)(2,1)} %broadcast_select_fusion.2.x_ref, f32[512,1024]{1,0:T(8,128)} %get-tuple-element.55.dh_ref, bf16[512,1024]{1,0:T(8,128)(2,1)} %get-tuple-element.58.dq_ref, f32[8,1024]{1,0:T(8,128)} %gains.1.gain_ref, ...), custom_call_target="tpu_custom_call" | custom-call | flops 3221225472 | bytes 17825792 | tf_op jit(solution)/shard_map/input_back/pallas_call | solution.py:468
  392.9 24.7 %collective-permute-done.32 = bf16[512,1024]{1,0:T(8,128)(2,1)S(1)} collective-permute-done((bf16[512,1024]{1,0:T(8,128)(2,1)}, bf16[512,1024]{1,0:T(8,128)(2,1)S(1)}, u32[]{:S(2)}, u32[]{:S(2)}) %collective-permute-start.32) | collective-permute-done | bytes 1048608 | tf_op jit(solution)/shard_map/ppermute | solution.py:808
  418.8 10.2 %ffn_back.3 = (bf16[512,2688]{1,0:T(8,128)(2,1)}, bf16[512,2688]{1,0:T(8,128)(2,1)}) custom-call(bf16[512,1024]{1,0:T(8,128)(2,1)} %broadcast_select_fusion.g_ref.refs_0_, bf16[512,2688]{1,0:T(8,128)(2,1)} %get-tuple-element.50.act_ref, bf16[512,2688]{1,0:T(8,128)(2,1)} %get-tuple-element.51.slope_ref, bf16[1024,2688]{1,0:T(8,128)(2,1)} %bitcast.44.w_ref), custom_call_target="tpu_custom_call" | custom-call | flops 2818572288 | bytes 17563648 | tf_op jit(solution)/shard_map/ffn_back/pallas_call | solution.py:323
  428.9 14.3 %hidden_back.3 = (f32[512,1024]{1,0:T(8,128)}, bf16[512,1024]{1,0:T(8,128)(2,1)}, f32[1,1024]{1,0:T(1,128)}) custom-call(bf16[512,1024]{1,0:T(8,128)(2,1)} %broadcast_select_fusion.g_ref.refs_0_, bf16[512,2688]{1,0:T(8,128)(2,1)} %get-tuple-element.62.da_ref.refs_1_, bf16[512,2688]{1,0:T(8,128)(2,1)} %get-tuple-element.63.dg_ref.refs_2_, ...), custom_call_target="tpu_custom_call" | custom-call | flops 5637144576 | bytes 22806528 | tf_op jit(solution)/shard_map/hidden_back/pallas_call | solution.py:353
  443.2 8.2 %weight_rows.9 = bf16[448,5376]{1,0:T(8,128)(2,1)} custom-call(s32[7]{0:T(128)} %stack.75.order_ref, bf16[512,1024]{1,0:T(8,128)(2,1)} %get-tuple-element.49.b_ref.refs_0_, bf16[512,2688]{1,0:T(8,128)(2,1)} %get-tuple-element.62.da_ref.refs_1_, bf16[512,2688]{1,0:T(8,128)(2,1)} %get-tuple-element.63.dg_ref.refs_2_), custom_call_target="tpu_custom_call" | custom-call | flops 2466250752 | bytes 11370496 | tf_op jit(solution)/shard_map/weight_rows/pallas_call | solution.py:524
  452.3 34.7 %attend_back.3 = (bf16[512,1024]{1,0:T(8,128)(2,1)}, bf16[512,2048]{1,0:T(8,128)(2,1)}, bf16[512,2048]{1,0:T(8,128)(2,1)}) custom-call(bf16[512,1024]{1,0:T(8,128)(2,1)} %queries.3.q_ref, bf16[512,1024]{1,0:T(8,128)(2,1)} %get-tuple-element.65.dh_ref.refs_4_, bf16[1024,4224]{1,0:T(8,128)(2,1)} %bitcast.17.w_ref, ...), custom_call_target="tpu_custom_call" | custom-call | flops 10737418240 | bytes 14680064 | tf_op jit(solution)/shard_map/attend_back/pallas_call | solution.py:410
  492.8 14.4 %input_back.3 = (bf16[512,1024]{1,0:T(8,128)(2,1)}, bf16[512,2048]{1,0:T(8,128)(2,1)}, f32[1,1024]{1,0:T(1,128)}) custom-call(bf16[512,1024]{1,0:T(8,128)(2,1)} %broadcast_select_fusion.2.x_ref, f32[512,1024]{1,0:T(8,128)} %get-tuple-element.64.dh_ref, bf16[512,1024]{1,0:T(8,128)(2,1)} %get-tuple-element.66.dq_ref.refs_2_, f32[8,1024]{1,0:T(8,128)} %gains.1.gain_ref, ...), custom_call_target="tpu_custom_call" | custom-call | flops 3221225472 | bytes 17825792 | tf_op jit(solution)/shard_map/input_back/pallas_call | solution.py:468
  509.0 7.0 weight_rows.7
  516.7 9.4 %weight_rows.8.mine_ref = bf16[576,5376]{1,0:T(8,128)(2,1)} custom-call(s32[9]{0:T(128)} %stack.67.order_ref, bf16[512,1024]{1,0:T(8,128)(2,1)} %get-tuple-element.49.b_ref.refs_0_, bf16[512,2688]{1,0:T(8,128)(2,1)} %get-tuple-element.62.da_ref.refs_1_, bf16[512,2688]{1,0:T(8,128)(2,1)} %get-tuple-element.63.dg_ref.refs_2_), custom_call_target="tpu_custom_call" | custom-call | flops 3170893824 | bytes 12746752 | tf_op jit(solution)/shard_map/weight_rows/pallas_call | solution.py:524
  562.2 7.9 %weight_rows.6.mine_ref = bf16[576,4224]{1,0:T(8,128)(2,1)} custom-call(s32[9]{0:T(128)} %stack.67.order_ref, bf16[512,1024]{1,0:T(8,128)(2,1)} %get-tuple-element.46.a_ref.refs_0_, bf16[512,2048]{1,0:T(8,128)(2,1)} %get-tuple-element.71.refs_1_, bf16[512,1024]{1,0:T(8,128)(2,1)} %get-tuple-element.66.dq_ref.refs_2_, ...), custom_call_target="tpu_custom_call" | custom-call | flops 2491416576 | bytes 11419648 | tf_op jit(solution)/shard_map/weight_rows/pallas_call | solution.py:524
  572.3 7.9 %ffn_out.3 = bf16[512,1024]{1,0:T(8,128)(2,1)} custom-call(f32[512,1024]{1,0:T(8,128)} %get-tuple-element.54.h_ref, bf16[512,2688]{1,0:T(8,128)(2,1)} %get-tuple-element.70.z_ref.refs_1_, bf16[1024,2688]{1,0:T(8,128)(2,1)} %bitcast.44.w_ref), custom_call_target="tpu_custom_call" | custom-call | flops 2818572288 | bytes 11403264 | tf_op jit(solution)/shard_map/ffn_out/pallas_call | solution.py:298
  601.4 39.8 %collective-permute-done.36.refs_0_ = bf16[128,4224]{1,0:T(8,128)(2,1)S(1)} collective-permute-done((bf16[128,4224]{1,0:T(8,128)(2,1)}, bf16[128,4224]{1,0:T(8,128)(2,1)S(1)}, u32[]{:S(2)}, u32[]{:S(2)}) %collective-permute-start.36) | collective-permute-done | bytes 1081376 | tf_op jit(solution)/shard_map/ppermute | solution.py:615
  667.3 7.1 %collective-permute-done.44 = bf16[128,5376]{1,0:T(8,128)(2,1)} collective-permute-done((bf16[128,5376]{1,0:T(8,128)(2,1)}, bf16[128,5376]{1,0:T(8,128)(2,1)}, u32[]{:S(2)}, u32[]{:S(2)}) %collective-permute-start.44) | collective-permute-done | bytes 1376288 | tf_op jit(solution)/shard_map/ppermute | solution.py:615
  676.4 9.5 %collective-permute-done.38 = bf16[128,4224]{1,0:T(8,128)(2,1)S(1)} collective-permute-done((bf16[128,4224]{1,0:T(8,128)(2,1)}, bf16[128,4224]{1,0:T(8,128)(2,1)S(1)}, u32[]{:S(2)}, u32[]{:S(2)}) %collective-permute-start.38) | collective-permute-done | bytes 1081376 | tf_op jit(solution)/shard_map/ppermute | solution.py:615
  (275 shorter events, 264.7 us)
Async XLA Ops:
  8.9 30.2 %collective-permute-start = (bf16[64,4224]{1,0:T(8,128)(2,1)}, bf16[64,4224]{1,0:T(8,128)(2,1)}, u32[]{:S(2)}, u32[]{:S(2)}) collective-permute-start(bf16[64,4224]{1,0:T(8,128)(2,1)} %fusion.7), channel_id=1, source_target_pairs={{0,1},{1,0},{2,3},{3,2},{4,5},{5,4},{6,7},{7,6},{8,9},{9,8},{10,11... | collective-permute-start | bytes 1622024 | tf_op jit(solution)/shard_map/ppermute | solution.py:612
  10.6 36.6 %collective-permute-start.11 = (bf16[64,5376]{1,0:T(8,128)(2,1)}, bf16[64,5376]{1,0:T(8,128)(2,1)S(1)}, u32[]{:S(2)}, u32[]{:S(2)}) collective-permute-start(bf16[64,5376]{1,0:T(8,128)(2,1)} %fusion.4), channel_id=1, source_target_pairs={{0,1},{1,0},{2,3},{3,2},{4,5},{5,4},{6,7},{7,6},{8,9},{9,8},{10,11... | collective-permute-start | bytes 2064392 | tf_op jit(solution)/shard_map/ppermute | solution.py:612
  11.4 22.0 %collective-permute-start.20 = (bf16[64,2688]{1,0:T(8,128)(2,1)}, bf16[64,2688]{1,0:T(8,128)(2,1)}, u32[]{:S(2)}, u32[]{:S(2)}) collective-permute-start(bf16[64,2688]{1,0:T(8,128)(2,1)} %pad.22), channel_id=1, source_target_pairs={{0,1},{1,0},{2,3},{3,2},{4,5},{5,4},{6,7},{7,6},{8,9},{9,8},{10,11... | collective-permute-start | bytes 1032200 | tf_op jit(solution)/shard_map/ppermute | solution.py:612
  21.4 125.0 %all-to-all-start.1 = ((bf16[8,64,1024]{2,1,0:T(8,128)(2,1)}), bf16[8,64,1024]{2,1,0:T(8,128)(2,1)S(1)}, u32[]{:S(2)}, u32[]{:S(2)}) async-start(bf16[8,64,1024]{2,1,0:T(8,128)(2,1)} %bitcast.3), calls=%async_computation.1 | async-start | bytes 2097152 | tf_op jit(solution)/shard_map/all_to_all | solution.py:627
  40.4 21.3 %collective-permute-start.1 = (bf16[128,4224]{1,0:T(8,128)(2,1)S(1)}, bf16[128,4224]{1,0:T(8,128)(2,1)S(1)}, u32[]{:S(2)}, u32[]{:S(2)}) collective-permute-start(bf16[128,4224]{1,0:T(8,128)(2,1)S(1)} %pad_maximum_fusion.1), channel_id=1, source_target_pairs={{0,4},{1,3},{4,8},{5,1},{8,12},{9,5},{12,14},{13,9},{14,10},{15,13... | collective-permute-start | bytes 3244040 | tf_op jit(solution)/shard_map/ppermute | solution.py:615
  47.5 29.0 %collective-permute-start.12 = (bf16[128,5376]{1,0:T(8,128)(2,1)S(1)}, bf16[128,5376]{1,0:T(8,128)(2,1)S(1)}, u32[]{:S(2)}, u32[]{:S(2)}) collective-permute-start(bf16[128,5376]{1,0:T(8,128)(2,1)S(1)} %pad_maximum_fusion), channel_id=1, source_target_pairs={{0,4},{1,3},{4,8},{5,1},{8,12},{9,5},{12,14},{13,9},{14,10},{15,13... | collective-permute-start | bytes 4128776 | tf_op jit(solution)/shard_map/ppermute | solution.py:615
  61.7 28.7 %collective-permute-start.2 = (bf16[128,4224]{1,0:T(8,128)(2,1)S(1)}, bf16[128,4224]{1,0:T(8,128)(2,1)S(1)}, u32[]{:S(2)}, u32[]{:S(2)}) collective-permute-start(bf16[128,4224]{1,0:T(8,128)(2,1)S(1)} %collective-permute-done.1), channel_id=1, source_target_pairs={{0,1},{1,0},{2,3},{3,2},{4,5},{5,4},{6,7},{7,6},{8,9},{9,8},{10,11... | collective-permute-start | bytes 3244040 | tf_op jit(solution)/shard_map/ppermute | solution.py:612
  64.1 24.0 %collective-permute-start.3 = (bf16[128,4224]{1,0:T(8,128)(2,1)S(1)}, bf16[128,4224]{1,0:T(8,128)(2,1)S(1)}, u32[]{:S(2)}, u32[]{:S(2)}) collective-permute-start(bf16[128,4224]{1,0:T(8,128)(2,1)S(1)} %collective-permute-done.1), channel_id=1, source_target_pairs={{0,4},{1,3},{4,8},{5,1},{8,12},{9,5},{12,14},{13,9},{14,10},{15,13... | collective-permute-start | bytes 3244040 | tf_op jit(solution)/shard_map/ppermute | solution.py:615
  76.5 28.7 %collective-permute-start.13 = (bf16[128,5376]{1,0:T(8,128)(2,1)S(1)}, bf16[128,5376]{1,0:T(8,128)(2,1)S(1)}, u32[]{:S(2)}, u32[]{:S(2)}) collective-permute-start(bf16[128,5376]{1,0:T(8,128)(2,1)S(1)} %collective-permute-done.12), channel_id=1, source_target_pairs={{0,1},{1,0},{2,3},{3,2},{4,5},{5,4},{6,7},{7,6},{8,9},{9,8},{10,11... | collective-permute-start | bytes 4128776 | tf_op jit(solution)/shard_map/ppermute | solution.py:612
  78.8 24.0 %collective-permute-start.14 = (bf16[128,5376]{1,0:T(8,128)(2,1)S(1)}, bf16[128,5376]{1,0:T(8,128)(2,1)S(1)}, u32[]{:S(2)}, u32[]{:S(2)}) collective-permute-start(bf16[128,5376]{1,0:T(8,128)(2,1)S(1)} %collective-permute-done.12), channel_id=1, source_target_pairs={{0,4},{1,3},{4,8},{5,1},{8,12},{9,5},{12,14},{13,9},{14,10},{15,13... | collective-permute-start | bytes 4128776 | tf_op jit(solution)/shard_map/ppermute | solution.py:615
  88.1 28.8 %collective-permute-start.4 = (bf16[128,4224]{1,0:T(8,128)(2,1)S(1)}, bf16[128,4224]{1,0:T(8,128)(2,1)S(1)}, u32[]{:S(2)}, u32[]{:S(2)}) collective-permute-start(bf16[128,4224]{1,0:T(8,128)(2,1)S(1)} %collective-permute-done.3), channel_id=1, source_target_pairs={{0,1},{1,0},{2,3},{3,2},{4,5},{5,4},{6,7},{7,6},{8,9},{9,8},{10,11... | collective-permute-start | bytes 3244040 | tf_op jit(solution)/shard_map/ppermute | solution.py:612
  90.4 24.0 %collective-permute-start.5 = (bf16[128,4224]{1,0:T(8,128)(2,1)S(1)}, bf16[128,4224]{1,0:T(8,128)(2,1)S(1)}, u32[]{:S(2)}, u32[]{:S(2)}) collective-permute-start(bf16[128,4224]{1,0:T(8,128)(2,1)S(1)} %collective-permute-done.3), channel_id=1, source_target_pairs={{0,4},{1,3},{4,8},{5,1},{8,12},{9,5},{12,14},{13,9},{14,10},{15,13... | collective-permute-start | bytes 3244040 | tf_op jit(solution)/shard_map/ppermute | solution.py:615
  102.8 37.3 %collective-permute-start.15 = (bf16[128,5376]{1,0:T(8,128)(2,1)S(1)}, bf16[128,5376]{1,0:T(8,128)(2,1)S(1)}, u32[]{:S(2)}, u32[]{:S(2)}) collective-permute-start(bf16[128,5376]{1,0:T(8,128)(2,1)S(1)} %collective-permute-done.14), channel_id=1, source_target_pairs={{0,1},{1,0},{2,3},{3,2},{4,5},{5,4},{6,7},{7,6},{8,9},{9,8},{10,11... | collective-permute-start | bytes 4128776 | tf_op jit(solution)/shard_map/ppermute | solution.py:612
  105.2 32.1 %collective-permute-start.16 = (bf16[128,5376]{1,0:T(8,128)(2,1)S(1)}, bf16[128,5376]{1,0:T(8,128)(2,1)S(1)}, u32[]{:S(2)}, u32[]{:S(2)}) collective-permute-start(bf16[128,5376]{1,0:T(8,128)(2,1)S(1)} %collective-permute-done.14), channel_id=1, source_target_pairs={{0,4},{1,3},{4,8},{5,1},{8,12},{9,5},{12,14},{13,9},{14,10},{15,13... | collective-permute-start | bytes 4128776 | tf_op jit(solution)/shard_map/ppermute | solution.py:615
  116.7 25.9 %collective-permute-start.6 = (bf16[128,4224]{1,0:T(8,128)(2,1)S(1)}, bf16[128,4224]{1,0:T(8,128)(2,1)S(1)}, u32[]{:S(2)}, u32[]{:S(2)}) collective-permute-start(bf16[128,4224]{1,0:T(8,128)(2,1)S(1)} %collective-permute-done.5), channel_id=1, source_target_pairs={{0,1},{1,0},{2,3},{3,2},{4,5},{5,4},{6,7},{7,6},{8,9},{9,8},{10,11... | collective-permute-start | bytes 3244040 | tf_op jit(solution)/shard_map/ppermute | solution.py:612
  135.0 25.4 %collective-permute-start.21 = (bf16[128,2688]{1,0:T(8,128)(2,1)}, bf16[128,2688]{1,0:T(8,128)(2,1)}, u32[]{:S(2)}, u32[]{:S(2)}) collective-permute-start(bf16[128,2688]{1,0:T(8,128)(2,1)} %pad_maximum_fusion.2), channel_id=1, source_target_pairs={{0,4},{1,3},{4,8},{5,1},{8,12},{9,5},{12,14},{13,9},{14,10},{15,13... | collective-permute-start | bytes 2064392 | tf_op jit(solution)/shard_map/ppermute | solution.py:615
  138.2 24.3 %collective-permute-start.18 = (bf16[64,5376]{1,0:T(8,128)(2,1)}, bf16[64,5376]{1,0:T(8,128)(2,1)S(1)}, u32[]{:S(2)}, u32[]{:S(2)}) collective-permute-start(bf16[64,5376]{1,0:T(8,128)(2,1)} %constant_dynamic-slice_fusion.1), channel_id=1, source_target_pairs={{0,4},{1,3},{4,8},{5,1},{8,12},{9,5},{12,14},{13,9},{14,10},{15,13... | collective-permute-start | bytes 2064392 | tf_op jit(solution)/shard_map/ppermute | solution.py:615
  140.1 33.9 %collective-permute-start.17 = (bf16[128,5376]{1,0:T(8,128)(2,1)S(1)}, bf16[128,5376]{1,0:T(8,128)(2,1)}, u32[]{:S(2)}, u32[]{:S(2)}) collective-permute-start(bf16[128,5376]{1,0:T(8,128)(2,1)S(1)} %collective-permute-done.16), channel_id=1, source_target_pairs={{0,1},{1,0},{2,3},{3,2},{4,5},{5,4},{6,7},{7,6},{8,9},{9,8},{10,11... | collective-permute-start | bytes 4128776 | tf_op jit(solution)/shard_map/ppermute | solution.py:612
  154.9 35.4 %collective-permute-start.10 = (bf16[512,2048]{1,0:T(8,128)(2,1)}, bf16[512,2048]{1,0:T(8,128)(2,1)}, u32[]{:S(2)}, u32[]{:S(2)}) collective-permute-start(bf16[512,2048]{1,0:T(8,128)(2,1)} %get-tuple-element.41.refs_0_), channel_id=1, source_target_pairs={{0,1},{1,0},{2,3},{3,2},{4,5},{5,4},{6,7},{7,6},{8,9},{9,8},{10,11... | collective-permute-start | bytes 6291464 | tf_op jit(solution)/shard_map/ppermute | solution.py:696
  182.2 42.8 %collective-permute-start.26 = (bf16[128,2688]{1,0:T(8,128)(2,1)S(1)}, bf16[128,2688]{1,0:T(8,128)(2,1)S(1)}, u32[]{:S(2)}, u32[]{:S(2)}) collective-permute-start(bf16[128,2688]{1,0:T(8,128)(2,1)S(1)} %collective-permute-done.25), channel_id=1, source_target_pairs={{0,1},{1,0},{2,3},{3,2},{4,5},{5,4},{6,7},{7,6},{8,9},{9,8},{10,11... | collective-permute-start | bytes 2064392 | tf_op jit(solution)/shard_map/ppermute | solution.py:612
  188.6 36.4 %collective-permute-start.28 = (bf16[64,2688]{1,0:T(8,128)(2,1)S(1)}, bf16[64,2688]{1,0:T(8,128)(2,1)S(1)}, u32[]{:S(2)}, u32[]{:S(2)}) collective-permute-start(bf16[64,2688]{1,0:T(8,128)(2,1)S(1)} %collective-permute-done.27), channel_id=1, source_target_pairs={{0,1},{1,0},{2,3},{3,2},{4,5},{5,4},{6,7},{7,6},{8,9},{9,8},{10,11... | collective-permute-start | bytes 1032200 | tf_op jit(solution)/shard_map/ppermute | solution.py:612
  234.8 26.0 %collective-permute-start.29 = (bf16[512,1024]{1,0:T(8,128)(2,1)}, bf16[512,1024]{1,0:T(8,128)(2,1)S(1)}, u32[]{:S(2)}, u32[]{:S(2)}) collective-permute-start(bf16[512,1024]{1,0:T(8,128)(2,1)} %ffn_out.2), channel_id=1, source_target_pairs={{0,16},{1,17},{2,18},{3,19},{4,20},{5,21},{6,22},{7,23},{8,24},{9,... | collective-permute-start | bytes 3145736 | tf_op jit(solution)/shard_map/ppermute | solution.py:808
  390.9 26.7 %collective-permute-start.32 = (bf16[512,1024]{1,0:T(8,128)(2,1)}, bf16[512,1024]{1,0:T(8,128)(2,1)S(1)}, u32[]{:S(2)}, u32[]{:S(2)}) collective-permute-start(bf16[512,1024]{1,0:T(8,128)(2,1)} %get-tuple-element.61), channel_id=1, source_target_pairs={{16,0},{17,1},{18,2},{19,3},{20,4},{21,5},{22,6},{23,7},{24,8},{25... | collective-permute-start | bytes 3145736 | tf_op jit(solution)/shard_map/ppermute | solution.py:808
  451.4 74.7 %collective-permute-start.40 = (bf16[448,5376]{1,0:T(8,128)(2,1)}, bf16[448,5376]{1,0:T(8,128)(2,1)}, u32[]{:S(2)}, u32[]{:S(2)}) collective-permute-start(bf16[448,5376]{1,0:T(8,128)(2,1)} %weight_rows.9), channel_id=1, source_target_pairs={{0,1},{1,0},{2,3},{3,2},{4,5},{5,4},{6,7},{7,6},{8,9},{9,8},{10,11... | collective-permute-start | bytes 14450696 | tf_op jit(solution)/shard_map/ppermute | solution.py:612
  492.4 41.9 %collective-permute-start.46 = (bf16[448,2688]{1,0:T(8,128)(2,1)}, bf16[448,2688]{1,0:T(8,128)(2,1)S(1)}, u32[]{:S(2)}, u32[]{:S(2)}) collective-permute-start(bf16[448,2688]{1,0:T(8,128)(2,1)} %weight_rows.11), channel_id=1, source_target_pairs={{0,1},{1,0},{2,3},{3,2},{4,5},{5,4},{6,7},{7,6},{8,9},{9,8},{10,11... | collective-permute-start | bytes 7225352 | tf_op jit(solution)/shard_map/ppermute | solution.py:612
  516.0 54.1 %collective-permute-start.34 = (bf16[448,4224]{1,0:T(8,128)(2,1)}, bf16[448,4224]{1,0:T(8,128)(2,1)}, u32[]{:S(2)}, u32[]{:S(2)}) collective-permute-start(bf16[448,4224]{1,0:T(8,128)(2,1)} %weight_rows.7), channel_id=1, source_target_pairs={{0,1},{1,0},{2,3},{3,2},{4,5},{5,4},{6,7},{7,6},{8,9},{9,8},{10,11... | collective-permute-start | bytes 11354120 | tf_op jit(solution)/shard_map/ppermute | solution.py:612
  552.5 31.7 %collective-permute-start.42 = (bf16[128,5376]{1,0:T(8,128)(2,1)}, bf16[128,5376]{1,0:T(8,128)(2,1)S(1)}, u32[]{:S(2)}, u32[]{:S(2)}) collective-permute-start(bf16[128,5376]{1,0:T(8,128)(2,1)} %ring_add.17), channel_id=1, source_target_pairs={{0,4},{1,3},{4,8},{5,1},{8,12},{9,5},{12,14},{13,9},{14,10},{15,13... | collective-permute-start | bytes 4128776 | tf_op jit(solution)/shard_map/ppermute | solution.py:615
  572.3 22.9 %collective-permute-start.35 = (bf16[64,4224]{1,0:T(8,128)(2,1)}, bf16[64,4224]{1,0:T(8,128)(2,1)S(1)}, u32[]{:S(2)}, u32[]{:S(2)}) collective-permute-start(bf16[64,4224]{1,0:T(8,128)(2,1)} %ring_add.12), channel_id=1, source_target_pairs={{0,4},{1,3},{4,8},{5,1},{8,12},{9,5},{12,14},{13,9},{14,10},{15,13... | collective-permute-start | bytes 1622024 | tf_op jit(solution)/shard_map/ppermute | solution.py:615
  588.4 58.4 %collective-permute-start.43 = (bf16[128,5376]{1,0:T(8,128)(2,1)}, bf16[128,5376]{1,0:T(8,128)(2,1)}, u32[]{:S(2)}, u32[]{:S(2)}) collective-permute-start(bf16[128,5376]{1,0:T(8,128)(2,1)} %ring_add.18), channel_id=1, source_target_pairs={{0,4},{1,3},{4,8},{5,1},{8,12},{9,5},{12,14},{13,9},{14,10},{15,13... | collective-permute-start | bytes 4128776 | tf_op jit(solution)/shard_map/ppermute | solution.py:615
  590.3 64.2 %all-to-all-start.3 = ((bf16[8,64,1024]{2,1,0:T(8,128)(2,1)}), bf16[8,64,1024]{2,1,0:T(8,128)(2,1)S(1)}, u32[]{:S(2)}, u32[]{:S(2)}) async-start(bf16[8,64,1024]{2,1,0:T(8,128)(2,1)} %bitcast.45), calls=%async_computation.3 | async-start | bytes 2097152 | tf_op jit(solution)/shard_map/all_to_all | solution.py:630
  598.7 42.5 %collective-permute-start.36 = (bf16[128,4224]{1,0:T(8,128)(2,1)}, bf16[128,4224]{1,0:T(8,128)(2,1)S(1)}, u32[]{:S(2)}, u32[]{:S(2)}) collective-permute-start(bf16[128,4224]{1,0:T(8,128)(2,1)} %ring_add.13), channel_id=1, source_target_pairs={{0,4},{1,3},{4,8},{5,1},{8,12},{9,5},{12,14},{13,9},{14,10},{15,13... | collective-permute-start | bytes 3244040 | tf_op jit(solution)/shard_map/ppermute | solution.py:615
  650.1 24.3 %collective-permute-start.44 = (bf16[128,5376]{1,0:T(8,128)(2,1)}, bf16[128,5376]{1,0:T(8,128)(2,1)}, u32[]{:S(2)}, u32[]{:S(2)}) collective-permute-start(bf16[128,5376]{1,0:T(8,128)(2,1)} %ring_add.19), channel_id=1, source_target_pairs={{0,4},{1,3},{4,8},{5,1},{8,12},{9,5},{12,14},{13,9},{14,10},{15,13... | collective-permute-start | bytes 4128776 | tf_op jit(solution)/shard_map/ppermute | solution.py:615
  (49 other events, 422.6 us)

commit v3 on v2

v3 whole, which is shorter than its diff:
```python
from functools import partial

import jax
import jax.numpy as jnp
from jax import lax
from jax.experimental import pallas as pl
from jax.experimental.pallas import tpu as pltpu
from jax.sharding import PartitionSpec as P

D = 1024
HEADS = 16
HEAD_DIM = 64
FF = 2624
FFP = 2688
FFB = 896
LANES = 128
PAIRS = D // LANES
EPSILON = 1e-05
ROPE_BASE = 160000.0
NEG_FILL = -1e30
BF = jnp.bfloat16
F32 = jnp.float32
BOTH = ("ctx", "wshard")
IDS = 16
PENALTY = -(2.0**100)
NN = ((1,), (0,))
NT = ((1,), (1,))
TN = ((0,), (0,))
SMEM_SPEC = pl.BlockSpec(memory_space=pltpu.SMEM)


def dot(a, b, dims):
    return lax.dot_general(a, b, (dims, ((), ())), preferred_element_type=F32)


def after(value, *others):
    return lax.optimization_barrier((value,) + others)[0]


def shaped(shape, kind=BF):
    return jax.ShapeDtypeStruct(shape, kind)


def call(kernel, name, limit=20, flops=0, moved=0, exps=0, **more):
    return pl.pallas_call(
        kernel,
        name=name,
        compiler_params=pltpu.CompilerParams(vmem_limit_bytes=limit * 1024 * 1024),
        cost_estimate=pl.CostEstimate(
            flops=int(flops), bytes_accessed=int(moved), transcendentals=int(exps)
        ),
        **more,
    )


def whole(shape):
    return pl.BlockSpec(shape, lambda *_: (0,) * len(shape))


def rope_block(v, cosine, sine):
    lane = lax.broadcasted_iota(jnp.int32, v.shape, 1) % HEAD_DIM
    other = jnp.where(
        lane < HEAD_DIM // 2,
        pltpu.roll(v, LANES - HEAD_DIM // 2, 1),
        pltpu.roll(v, HEAD_DIM // 2, 1),
    )
    return v * cosine + other * sine


def norm_parts(values):
    center = values - jnp.mean(values, axis=-1, keepdims=True)
    spread = jnp.mean(center * center, axis=-1, keepdims=True)
    inverse = lax.rsqrt(spread + EPSILON)
    return center * inverse, inverse


def norm_back(values, gain_row, grad):
    hat, inverse = norm_parts(values)
    scaled = grad * gain_row
    back = inverse * (
        scaled
        - jnp.mean(scaled, axis=-1, keepdims=True)
        - hat * jnp.mean(scaled * hat, axis=-1, keepdims=True)
    )
    return back, jnp.sum(grad * hat, axis=0, keepdims=True)


def head_mask(shape, head):
    lane = lax.broadcasted_iota(jnp.int32, shape, 1)
    return (lane >= HEAD_DIM) if head else (lane < HEAD_DIM)


def pick(mask, v, other=0.0):
    return jnp.where(mask, v, jnp.full(v.shape, other, v.dtype))


def gains_of(w_mix):
    def kernel(w_ref, out_ref):
        out_ref[...] = w_ref[...].astype(F32).T[:8]

    return call(
        kernel,
        "gains",
        grid=(1,),
        in_specs=[pl.BlockSpec((D, LANES), lambda j: (0, 4 * D // LANES))],
        out_specs=whole((8, D)),
        out_shape=shaped((8, D), F32),
    )(w_mix)


def keys_values(x, gains, w_kv, cosine, sine):
    rows = x.shape[0]
    block = 512

    def kernel(x_ref, gain_ref, w_ref, cos_ref, sin_ref, a_ref, out_ref):
        @pl.when(pl.program_id(0) == 0)
        def _():
            hat, _ = norm_parts(x_ref[...].astype(F32))
            a_ref[...] = (hat * gain_ref[0:1]).astype(BF)

        m = dot(a_ref[...], w_ref[...], NN)
        for j in range(block // LANES):
            at = slice(j * LANES, (j + 1) * LANES)
            v = m[:, at]
            if j % 2 == 0:
                v = rope_block(v, cos_ref[...], sin_ref[...])
            out_ref[:, at] = v.astype(BF)

    return call(
        kernel,
        "keys_values",
        flops=2 * rows * D * 2 * D,
        moved=2 * (2 * D * D + 4 * rows * D),
        grid=(2 * D // block,),
        in_specs=[
            whole((rows, D)),
            whole((8, D)),
            pl.BlockSpec((D, block), lambda j: (0, j)),
            whole((rows, LANES)),
            whole((rows, LANES)),
        ],
        out_specs=[whole((rows, D)), pl.BlockSpec((rows, block), lambda j: (0, j))],
        out_shape=[shaped((rows, D)), shaped((rows, 2 * D))],
    )(x, gains, w_kv, cosine, sine)


def queries_of(a, w_mix, cosine, sine):
    rows = a.shape[0]
    block = 512

    def kernel(a_ref, w_ref, cos_ref, sin_ref, out_ref):
        m = dot(a_ref[...], w_ref[...], NN)
        for j in range(block // LANES):
            at = slice(j * LANES, (j + 1) * LANES)
            out_ref[:, at] = rope_block(m[:, at], cos_ref[...], sin_ref[...]).astype(BF)

    return call(
        kernel,
        "queries",
        flops=2 * rows * D * D,
        moved=2 * (D * D + 2 * rows * D),
        grid=(D // block,),
        in_specs=[
            whole((rows, D)),
            pl.BlockSpec((D, block), lambda j: (0, 2 * D // block + j)),
            whole((rows, LANES)),
            whole((rows, LANES)),
        ],
        out_specs=pl.BlockSpec((rows, block), lambda j: (0, j)),
        out_shape=shaped((rows, D)),
    )(a, w_mix, cosine, sine)


def key_marks(seg):
    lane = jnp.arange(LANES) % HEAD_DIM
    return jnp.where(lane < IDS, (seg[:, None] == lane), lane < IDS + 3).astype(BF)
def query_marks(seg):
    lane = jnp.arange(LANES) % HEAD_DIM
    return jnp.where((lane < IDS) & (seg[:, None] != lane), PENALTY, 0.0).astype(BF)

def split3(v):
    a = v.astype(BF).astype(F32)
    b = (v - a).astype(BF).astype(F32)
    return a, b, v - a - b


def attend(q, kv_list, qmarks, kmarks, begin, count):
    rows = q.shape[0]
    members = len(kv_list)
    keys = members * rows

    def kernel(q_ref, qm_ref, km_ref, *refs):
        kv_refs, (o_ref, lse_ref) = refs[:members], refs[members:]
        k = jnp.concatenate([r[:, :LANES] for r in kv_refs], axis=0)
        v = jnp.concatenate([r[:, LANES:] for r in kv_refs], axis=0)
        q = q_ref[...] * jnp.asarray(HEAD_DIM**-0.5, BF)
        parts, stats = [], []
        for head in range(2):
            mine = head_mask((rows, LANES), head)
            theirs = head_mask((keys, LANES), head)
            s = dot(jnp.where(theirs, k, km_ref[...]), jnp.where(mine, q, qm_ref[...]), NT)
            top = jnp.max(s, axis=0, keepdims=True)
            e = jnp.exp(s - top).astype(BF)
            u = dot(pick(theirs, v, 1.0), e, TN)
            low, high = u[:HEAD_DIM], u[HEAD_DIM:]
            value, total = (high, low) if head else (low, high)
            parts.append(value / total)
            stats.append(top + jnp.log(total[:1]))
        o_ref[...] = jnp.concatenate(parts, axis=0).T.astype(BF)
        lse_ref[0] = jnp.concatenate(stats, axis=0)

    return call(
        kernel,
        "attend",
        flops=8 * rows * keys * count * LANES,
        moved=2 * (2 * rows + 2 * keys) * count * LANES,
        exps=rows * keys * count * 2,
        grid=(count,),
        in_specs=[
            pl.BlockSpec((rows, LANES), lambda p: (0, begin + p)),
            whole((rows, LANES)),
            whole((keys, LANES)),
        ]
        + [pl.BlockSpec((rows, 2 * LANES), lambda p: (0, begin + p))] * members,
        out_specs=[
            pl.BlockSpec((rows, LANES), lambda p: (0, p)),
            pl.BlockSpec((1, 2, rows), lambda p: (p, 0, 0)),
        ],
        out_shape=[shaped((rows, count * LANES)), shaped((count, 2, rows), F32)],
    )(q, qmarks, kmarks, *kv_list)

def project(x, o_list, gains, w_mix):
    rows = x.shape[0]
    block = 512
    steps = D // block

    def kernel(x_ref, gain_ref, w_ref, *refs):
        o_refs, (h_ref, b_ref) = refs[:-2], refs[-2:]
        j = pl.program_id(0)
        at = pl.ds(pl.multiple_of(j * block, block), block)
        total = x_ref[:, at].astype(F32)
        begin = 0
        for o_ref in o_refs:
            end = begin + o_ref.shape[1]
            total += dot(o_ref[...], w_ref[begin:end], NN)
            begin = end
        h_ref[:, at] = total

        @pl.when(j == steps - 1)
        def _():
            hat, _ = norm_parts(h_ref[...])
            b_ref[...] = (hat * gain_ref[1:2]).astype(BF)

    return call(
        kernel,
        "project",
        flops=2 * rows * D * D,
        moved=2 * D * D + 10 * rows * D,
        grid=(steps,),
        in_specs=[
            whole((rows, D)),
            whole((8, D)),
            pl.BlockSpec((D, block), lambda j: (0, 3 * D // block + j)),
        ]
        + [whole(o.shape) for o in o_list],
        out_specs=[whole((rows, D)), whole((rows, D))],
        out_shape=[shaped((rows, D), F32), shaped((rows, D))],
    )(x, gains, w_mix, *o_list)


def ffn_in(b, w_in, w_gate, keep):
    rows = b.shape[0]
    steps = FFP // FFB

    def kernel(b_ref, wa_ref, wg_ref, z_ref, *kept):
        a = dot(b_ref[...], wa_ref[...], NN)
        g = dot(b_ref[...], wg_ref[...], NN)
        phi = 0.5 * (1.0 + lax.erf(a * 0.7071067811865476))
        act = a * phi
        z_ref[...] = (act * g).astype(BF)
        if keep:
            density = 0.3989422804014327 * jnp.exp(-0.5 * a * a)
            kept[0][...] = act.astype(BF)
            kept[1][...] = ((phi + a * density) * g).astype(BF)

    out_spec = pl.BlockSpec((rows, FFB), lambda j: (0, j))
    count = 3 if keep else 1
    return call(
        kernel,
        "ffn_in",
        flops=4 * rows * D * FFP,
        moved=2 * (2 * D * FFP + rows * D + count * rows * FFP),
        grid=(steps,),
        in_specs=[whole((rows, D))] + [pl.BlockSpec((D, FFB), lambda j: (0, j))] * 2,
        out_specs=[out_spec] * count,
        out_shape=[shaped((rows, FFP))] * count,
    )(b, w_in, w_gate)


def ffn_out(h, z, w_back):
    rows = h.shape[0]
    block = 256

    def kernel(h_ref, z_ref, w_ref, out_ref):
        out_ref[...] = (h_ref[...] + dot(z_ref[...], w_ref[...], NT)).astype(BF)

    return call(
        kernel,
        "ffn_out",
        flops=2 * rows * D * FFP,
        moved=2 * (D * FFP + rows * FFP + 3 * rows * D),
        grid=(D // block,),
        in_specs=[
            pl.BlockSpec((rows, block), lambda j: (0, j)),
            whole((rows, FFP)),
            pl.BlockSpec((block, FFP), lambda j: (j, 0)),
        ],
        out_specs=pl.BlockSpec((rows, block), lambda j: (0, j)),
        out_shape=shaped((rows, D)),
    )(h, z, w_back)


def ffn_back(grad, act, slope, w_back):
    rows = grad.shape[0]

    def kernel(g_ref, act_ref, slope_ref, w_ref, da_ref, dg_ref):
        dz = dot(g_ref[...], w_ref[...], NN)
        da_ref[...] = (dz * slope_ref[...].astype(F32)).astype(BF)
        dg_ref[...] = (dz * act_ref[...].astype(F32)).astype(BF)

    spec = pl.BlockSpec((rows, FFB), lambda j: (0, j))
    return call(
        kernel,
        "ffn_back",
        flops=2 * rows * D * FFP,
        moved=2 * (D * FFP + 4 * rows * FFP + rows * D),
        grid=(FFP // FFB,),
        in_specs=[whole((rows, D)), spec, spec, pl.BlockSpec((D, FFB), lambda j: (0, j))],
        out_specs=[spec, spec],
        out_shape=[shaped((rows, FFP))] * 2,
    )(grad, act, slope, w_back)


def hidden_back(grad, da, dg, h, gains, w_in, w_gate):
    rows = grad.shape[0]
    block = 256
    steps = D // block

    def kernel(g_ref, da_ref, dg_ref, h_ref, gain_ref, wa_ref, wg_ref, dh_ref, low_ref, sum_ref):
        j = pl.program_id(0)
        at = pl.ds(pl.multiple_of(j * block, block), block)
        dh_ref[:, at] = dot(da_ref[...], wa_ref[...], NT) + dot(dg_ref[...], wg_ref[...], NT)

        @pl.when(j == steps - 1)
        def _():
            back, total = norm_back(h_ref[...], gain_ref[1:2], dh_ref[...])
            dh = g_ref[...].astype(F32) + back
            dh_ref[...] = dh
            low_ref[...] = dh.astype(BF)
            sum_ref[...] = total

    return call(
        kernel,
        "hidden_back",
        flops=4 * rows * D * FFP,
        moved=2 * (2 * D * FFP + 2 * rows * FFP + 6 * rows * D),
        grid=(steps,),
        in_specs=[
            whole((rows, D)),
            whole((rows, FFP)),
            whole((rows, FFP)),
            whole((rows, D)),
            whole((8, D)),
        ]
        + [pl.BlockSpec((block, FFP), lambda j: (j, 0))] * 2,
        out_specs=[whole((rows, D)), whole((rows, D)), whole((1, D))],
        out_shape=[shaped((rows, D), F32), shaped((rows, D)), shaped((1, D), F32)],
    )(grad, da, dg, h, gains, w_in, w_gate)


def attend_back(q, kv_list, dh_low, o, lse, qmarks, kmarks, w_mix, cosine, sine, begin):
    count = o.shape[1] // LANES
    rows = q.shape[0]
    members = len(kv_list)
    keys = members * rows

    def kernel(q_ref, dh_ref, w_ref, o_ref, lse_ref, qm_ref, km_ref, cos_ref, sin_ref, *refs):
        kv_refs, (dq_ref, *dkv_refs) = refs[:members], refs[members:]
        k = jnp.concatenate([r[:, :LANES] for r in kv_refs], axis=0)
        v = jnp.concatenate([r[:, LANES:] for r in kv_refs], axis=0)
        do = dot(dh_ref[...], w_ref[...], NT).astype(BF)
        q = q_ref[...] * jnp.asarray(HEAD_DIM**-0.5, BF)
        prod = do.astype(F32) * o_ref[...].astype(F32)
        lse = lse_ref[0]
        row = lax.broadcasted_iota(jnp.int32, (LANES, rows), 0)
        beside = jnp.zeros((LANES, rows), F32)
        for head in range(2):
            for n, part in enumerate(split3(-lse[head : head + 1])):
                beside = jnp.where(row == IDS + n + (HEAD_DIM if head == 0 else 0), part, beside)
        beside = beside.T.astype(BF) + qm_ref[...]
        lane = lax.broadcasted_iota(jnp.int32, (rows, LANES), 1)
        dks, dvs, dqs = [], [], []
        for head in range(2):
            mine = head_mask((rows, LANES), head)
            theirs = head_mask((keys, LANES), head)
            delta = jnp.sum(jnp.where(mine, prod, 0.0), axis=1, keepdims=True)
            there = jnp.zeros((rows, LANES), F32)
            for n, part in enumerate(split3(-delta)):
                there = jnp.where(lane == IDS + n + (HEAD_DIM if head == 0 else 0), part, there)
            qh = jnp.where(mine, q, beside)
            doh = jnp.where(mine, do, there.astype(BF))
            kh = jnp.where(theirs, k, km_ref[...])
            vh = jnp.where(theirs, v, km_ref[...])
            p = jnp.exp(dot(kh, qh, NT))
            ds = (p * dot(vh, doh, NT)).astype(BF)
            dvs.append(dot(p.astype(BF), do, NN))
            dks.append(dot(ds, q, NN))
            dqs.append(dot(ds, k, TN))
        first = head_mask((rows, LANES), 0)
        dq = jnp.where(first, dqs[0], dqs[1])
        dq = rope_block(dq * HEAD_DIM**-0.5, cos_ref[...], -sin_ref[...])
        dq_ref[...] = dq.astype(BF)
        for m, out in enumerate(dkv_refs):
            cut = slice(m * rows, (m + 1) * rows)
            out[:, :LANES] = jnp.where(first, dks[0][cut], dks[1][cut]).astype(BF)
            out[:, LANES:] = jnp.where(first, dvs[0][cut], dvs[1][cut]).astype(BF)

    spec = pl.BlockSpec((rows, LANES), lambda p: (0, p))
    kv_spec = pl.BlockSpec((rows, 2 * LANES), lambda p: (0, p))
    results = call(
        kernel,
        "attend_back",
        flops=20 * rows * keys * count * LANES,
        moved=2 * (6 * rows + 4 * keys) * count * LANES,
        exps=rows * keys * 2 * count,
        grid=(count,),
        in_specs=[
            pl.BlockSpec((rows, LANES), lambda p: (0, begin + p)),
            whole((rows, D)),
            pl.BlockSpec((LANES, D), lambda p: (begin + p, 3)),
            spec,
            pl.BlockSpec((1, 2, rows), lambda p: (p, 0, 0)),
            whole((rows, LANES)),
            whole((keys, LANES)),
            whole((rows, LANES)),
            whole((rows, LANES)),
        ]
        + [pl.BlockSpec((rows, 2 * LANES), lambda p: (0, begin + p))] * members,
        out_specs=[spec] + [kv_spec] * members,
        out_shape=[shaped((rows, count * LANES))] + [shaped((rows, 2 * count * LANES))] * members,
    )(q, dh_low, w_mix, o, lse, qmarks, kmarks, cosine, sine, *kv_list)
    return results[0], results[1:]


def keys_back(terms, cosine, sine):
    rows, columns = terms[0].shape

    def kernel(cos_ref, sin_ref, *refs):
        for b in range(columns // LANES):
            at = slice(b * LANES, (b + 1) * LANES)
            v = refs[0][:, at].astype(F32)
            for r in refs[1:-1]:
                v += r[:, at].astype(F32)
            if b % 2 == 0:
                v = rope_block(v, cos_ref[...], -sin_ref[...])
            refs[-1][:, at] = v.astype(BF)

    return call(
        kernel,
        "keys_back",
        flops=10 * rows * columns,
        moved=2 * (len(terms) + 1) * rows * columns,
        grid=(1,),
        in_specs=[whole((rows, LANES))] * 2 + [whole((rows, columns))] * len(terms),
        out_specs=whole((rows, columns)),
        out_shape=shaped((rows, columns)),
    )(cosine, sine, *terms)


def input_back(x, dh, dq_list, dkv_list, gains, w_kv, w_mix):
    rows = x.shape[0]
    block = 256
    steps = D // block
    grads = list(dkv_list) + list(dq_list)

    def kernel(x_ref, dh_ref, gain_ref, wkv_ref, wq_ref, *refs):
        grad_refs, (dx_ref, sum_ref, da_ref) = refs[:-3], refs[-3:]
        j = pl.program_id(0)
        total = 0.0
        begin = 0
        for n, ref in enumerate(grad_refs):
            if n == len(dkv_list):
                begin = 0
            end = begin + ref.shape[1]
            w_ref = wkv_ref if n < len(dkv_list) else wq_ref
            total += dot(ref[...], w_ref[:, begin:end], NT)
            begin = end
        da_ref[:, pl.ds(pl.multiple_of(j * block, block), block)] = total

        @pl.when(j == steps - 1)
        def _():
            back, total = norm_back(x_ref[...].astype(F32), gain_ref[0:1], da_ref[...])
            dx_ref[...] = (dh_ref[...] + back).astype(BF)
            sum_ref[...] = total

    return call(
        kernel,
        "input_back",
        flops=6 * rows * D * D,
        moved=2 * (3 * D * D + 10 * rows * D),
        grid=(steps,),
        in_specs=[
            whole((rows, D)),
            whole((rows, D)),
            whole((8, D)),
            pl.BlockSpec((block, 2 * D), lambda j: (j, 0)),
            pl.BlockSpec((block, D), lambda j: (j, 2)),
        ]
        + [whole(g.shape) for g in grads],
        out_specs=[whole((rows, D)), whole((1, D))],
        out_shape=[shaped((rows, D)), shaped((1, D), F32)],
        scratch_shapes=[pltpu.VMEM((rows, D), F32)],
    )(x, dh, gains, w_kv, w_mix, *grads)


def weight_rows(order, rows, lefts, rights, other=None):
    count = order.shape[0]
    tokens = lefts[0].shape[0]
    columns = sum(r.shape[1] for r in rights)
    flat = list(lefts) + list(rights) + ([] if other is None else [other])
    added = 0 if other is None else other.shape[0]
    outs = 1 if other is None else 2

    def kernel(order_ref, *refs):
        left_refs, right_refs = refs[: len(lefts)], refs[len(lefts) : len(lefts) + len(rights)]
        out_refs, (turned_ref, left_ref) = refs[len(flat) : len(flat) + outs], refs[-2:]
        at = 0
        for ref in left_refs:
            turned_ref[at : at + ref.shape[1]] = ref[...].T
            at += ref.shape[1]
        for n in range(count):
            start = pl.multiple_of(order_ref[n] * rows, rows)
            left_ref[n * rows : (n + 1) * rows] = turned_ref[pl.ds(start, rows)]
        at = 0
        for ref in right_refs:
            width = ref.shape[1]
            for begin in range(0, width, 512):
                end = min(begin + 512, width)
                cols = slice(at + begin, at + end)
                term = dot(left_ref[...], ref[:, begin:end], NN)
                if other is None:
                    out_refs[0][:, cols] = term.astype(BF)
                else:
                    other_ref = refs[len(flat) - 1]
                    near = term[:added] + other_ref[:, cols].astype(F32)
                    out_refs[0][:, cols] = near[:rows].astype(BF)
                    out_refs[1][: added - rows, cols] = near[rows:].astype(BF)
                    out_refs[1][added - rows :, cols] = term[added:].astype(BF)
            at += width

    shapes = [shaped((count * rows, columns))]
    if other is not None:
        shapes = [shaped((rows, columns)), shaped(((count - 1) * rows, columns))]
    size = 2 * (count * rows * columns + sum(v.size for v in flat))
    return call(
        kernel,
        "weight_rows",
        limit=max(8, 4 + int(1.25 * size) // (1024 * 1024)),
        flops=2 * count * rows * tokens * columns,
        moved=size,
        in_specs=[SMEM_SPEC] + [pl.BlockSpec(memory_space=pltpu.VMEM)] * len(flat),
        out_specs=[pl.BlockSpec(memory_space=pltpu.VMEM)] * outs,
        out_shape=shapes,
        scratch_shapes=[
            pltpu.VMEM((D, tokens), BF),
            pltpu.VMEM((count * rows, tokens), BF),
        ],
    )(order, *flat)


def ring_add(core, own, moving, first):
    rows = moving.shape[0] if first == 0 else moving.shape[0] // 2
    columns = own.shape[1]
    single = first == 0

    def kernel(core_ref, own_ref, moving_ref, out_ref):
        moved = moving_ref[...].astype(F32)
        if single:
            moved = jnp.where(core_ref[0] == pl.program_id(0), moved, 0.0)
        out_ref[...] = (own_ref[...].astype(F32) + moved).astype(BF)

    return call(
        kernel,
        "ring_add",
        limit=8,
        flops=4 * rows * columns,
        moved=12 * rows * columns,
        grid=(2,),
        in_specs=[
            SMEM_SPEC,
            pl.BlockSpec((rows, columns), lambda j: (first + j, 0)),
            pl.BlockSpec((rows, columns), (lambda j: (0, 0)) if single else (lambda j: (j, 0))),
        ],
        out_specs=pl.BlockSpec((rows, columns), lambda j: (j, 0)),
        out_shape=shaped((2 * rows, columns)),
    )(core, own, moving)


def blank(shape):
    def kernel(out_ref):
        pass

    return call(
        kernel,
        "blank",
        limit=1,
        out_specs=pl.BlockSpec(memory_space=pl.ANY),
        out_shape=shaped(shape),
    )()


class Plan:
    def __init__(self, boundary):
        self.micro = boundary.shape[1]
        self.tok_rows = boundary.shape[3]
        self.n_ctx = lax.axis_size("ctx")
        self.nw = lax.axis_size("wshard")
        self.g = self.n_ctx // (self.micro * self.nw)
        self.r = self.tok_rows // (self.g * self.nw)
        self.i = lax.axis_index("ctx")
        self.w = lax.axis_index("wshard")
        self.rows = self.n_ctx * self.r
        self.members = self.g * self.nw
        count = self.n_ctx
        chips = [2 * p if p < count // 2 else 2 * (count - 1 - p) + 1 for p in range(count)]
        self.half = count // 2
        self.way = 1 - 2 * self.w
        self.ring_pairs = []
        for p in range(count):
            self.ring_pairs.append((chips[p] * 2, chips[(p + 1) % count] * 2))
            self.ring_pairs.append((chips[p] * 2 + 1, chips[(p - 1) % count] * 2 + 1))
        place = jnp.where(self.i % 2 == 0, self.i // 2, count - 1 - self.i // 2)

        def chip(at):
            at = at % count
            return jnp.where(at < count // 2, 2 * at, 2 * (count - 1 - at) + 1)

        self.behind = [chip(place - self.way * k) for k in range(self.half + 1)]
        self.ahead = [chip(place + self.way * k) for k in range(self.half + 1)]
        self.wrows = D // (self.n_ctx * self.nw)
        near = range(self.half - 1, 0, -1)
        theirs = [2 * self.ahead[self.half] + 1 - self.w]
        mine = [2 * self.ahead[self.half] + self.w]
        for k in near:
            theirs += [2 * self.behind[k], 2 * self.behind[k] + 1]
            mine += [2 * self.ahead[k], 2 * self.ahead[k] + 1]
        mine += [2 * self.i, 2 * self.i + 1]
        self.theirs = jnp.stack(theirs).astype(jnp.int32)
        self.mine = jnp.stack(mine).astype(jnp.int32)
        self.core = self.w[None].astype(jnp.int32)

    def swap(self, array):
        return lax.ppermute(array, "wshard", [(0, 1), (1, 0)])

    def step(self, array):
        return lax.ppermute(array, BOTH, self.ring_pairs)

    def in_order(self, own, other):
        first = self.w == 0
        return jnp.concatenate(
            [jnp.where(first, own, other), jnp.where(first, other, own)], axis=0
        )

    def across(self, local):
        parts = local.reshape(self.micro, self.g, self.nw, self.r, D)
        parts = lax.all_to_all(parts.transpose(2, 0, 1, 3, 4), "wshard", 0, 0, tiled=True)
        return parts.transpose(1, 0, 2, 3, 4).reshape(self.n_ctx, self.r, D)

    def along(self, parts):
        return lax.all_to_all(parts, "ctx", 0, 0, tiled=True).reshape(self.rows, D)

    def from_sequences(self, rows):
        parts = lax.all_to_all(rows.reshape(self.n_ctx, self.r, D), "ctx", 0, 0, tiled=True)
        parts = parts.reshape(self.micro, self.nw, self.g, self.r, D).transpose(1, 0, 2, 3, 4)
        parts = lax.all_to_all(parts, "wshard", 0, 0, tiled=True)
        return parts.transpose(1, 2, 0, 3, 4).reshape(self.micro, self.tok_rows, D)

    def total(self, value):
        by = 1
        while by < self.n_ctx * self.nw:
            pairs = [(n, n ^ by) for n in range(self.n_ctx * self.nw)]
            value = value + lax.ppermute(value, BOTH, pairs)
            by *= 2
        return value

    def rotation(self, by):
        pairs = []
        for flat in range(self.n_ctx * self.nw):
            group, place = divmod(flat, self.members)
            pairs.append((flat, group * self.members + (place + by) % self.members))
        return pairs

    def gather_rows(self, rows):
        return [rows] + [
            lax.ppermute(rows, BOTH, self.rotation(by)) for by in range(1, self.members)
        ]

    def scatter_rows(self, terms):
        return [terms[0]] + [
            lax.ppermute(terms[by], BOTH, self.rotation(-by)) for by in range(1, self.members)
        ]


class Gather:
    def __init__(self, plan, shard, *deps):
        self.plan = plan
        self.rows = shard.shape[0]
        self.whole = blank((plan.n_ctx, plan.nw * self.rows, shard.shape[1]))
        self.current = plan.in_order(shard, plan.swap(shard))
        self.start = self.current
        self.put(self.current, plan.i)
        self.k = 0

    def put(self, block, chip):
        self.whole = lax.dynamic_update_index_in_dim(self.whole, block, chip, 0)

    def advance(self, *deps, late=()):
        plan = self.plan
        self.k += 1
        current = after(self.current, *deps) if deps else self.current
        if self.k < plan.half:
            current = plan.step(current)
            if late:
                current = after(current, *late)
            self.put(current, plan.behind[self.k])
            self.put(plan.swap(current), plan.ahead[self.k])
        else:
            part = lax.dynamic_slice_in_dim(current, plan.w * self.rows, self.rows, 0)
            current = plan.step(part)
            if late:
                current = after(current, *late)
            self.put(plan.in_order(current, plan.swap(current)), plan.behind[plan.half])
        self.current = current
        return current

    def result(self):
        return self.whole.reshape(D, self.whole.shape[2])


class Reduce:
    def __init__(self, plan, clock, lefts, rights):
        self.plan, self.clock = plan, clock
        self.lefts, self.rights = list(lefts), list(rights)
        self.k = plan.half

    def theirs(self):
        plan = self.plan
        lefts = [self.clock.tie(self.lefts[0])] + self.lefts[1:]
        (term,) = weight_rows(plan.theirs, plan.wrows, lefts, self.rights)
        self.other = plan.swap(self.clock.mark(term))

    def mine(self):
        plan = self.plan
        lefts = [self.clock.tie(self.lefts[0])] + self.lefts[1:]
        term, self.own = weight_rows(plan.mine, plan.wrows, lefts, self.rights, self.other)
        self.moving = plan.step(self.clock.mark(term))
        self.k -= 1

    def advance(self):
        plan = self.plan
        moving = self.clock.tie(self.moving)
        term = ring_add(plan.core, self.own, moving, 2 * (plan.half - 1 - self.k))
        self.moving = plan.step(self.clock.mark(term))
        self.k -= 1

    def result(self):
        plan = self.plan
        rows = plan.wrows
        final = self.moving.astype(F32) + self.own[-2 * rows :].astype(F32)
        keep = lax.dynamic_slice_in_dim(final, plan.w * rows, rows, 0)
        give = lax.dynamic_slice_in_dim(final, (1 - plan.w) * rows, rows, 0)
        return keep + plan.swap(give.astype(BF)).astype(F32)


class Clock:
    def __init__(self):
        self.last = None

    def tie(self, value):
        return value if self.last is None else after(value, self.last)

    def mark(self, value):
        self.last = value
        return value


def interleave(keys, values):
    lead = keys.shape[0]
    both = jnp.stack([keys.reshape(lead, PAIRS, LANES), values.reshape(lead, PAIRS, LANES)], axis=2)
    return both.reshape(lead, 2 * D)


def apart(both):
    lead = both.shape[0]
    both = both.reshape(lead, PAIRS, 2, LANES)
    return both[:, :, 0].reshape(lead, D), both[:, :, 1].reshape(lead, D)


def body(
    boundary, segment_ids, qkv_weight, attn_out_weight, ffn_in_weight, ffn_out_weight, norm_gains
):
    section = lax.axis_index("section")
    sections = lax.axis_size("section")
    plan = Plan(boundary)
    rows = plan.rows

    pad = FFP - FF
    wide_shard = jnp.concatenate(
        [
            interleave(qkv_weight[0][:, D : 2 * D], qkv_weight[0][:, 2 * D :]),
            qkv_weight[0][:, :D],
            attn_out_weight[0],
            jnp.pad(norm_gains[0].T, ((0, 0), (0, LANES - 2))),
        ],
        axis=1,
    )
    in_shard = jnp.pad(ffn_in_weight[0][:, :FF], ((0, 0), (0, pad)))
    gate_shard = jnp.pad(ffn_in_weight[0][:, FF:], ((0, 0), (0, pad)))
    back_shard = jnp.pad(ffn_out_weight[0].T, ((0, 0), (0, pad)))
    get_wide = Gather(plan, wide_shard)
    get_in = Gather(plan, in_shard)
    parts = plan.across(after(boundary[0, :, 0], get_wide.start, get_in.start))
    got = [get.advance() for get in (get_wide, get_in)]
    get_gate = Gather(plan, after(gate_shard, *got))
    get_back = Gather(plan, after(back_shard, *got))
    own = plan.along(after(parts, *got))
    got = [get.advance() for get in (get_wide, get_in)]
    ids = after(segment_ids[:, 0], *got)
    for _ in range(plan.half - 2):
        got = [get.advance() for get in (get_wide, get_in)]

    ids = plan.in_order(ids[None], plan.swap(ids[None])).transpose(1, 0, 2)
    ids = jnp.repeat(ids.reshape(plan.micro * plan.nw, plan.tok_rows), plan.g, axis=0)
    line = lax.all_to_all(ids, "ctx", 0, 0, tiled=True).reshape(-1)
    grid = line.reshape(plan.n_ctx, plan.members, plan.r)
    place = (plan.i % plan.g) * plan.nw + plan.w
    seg_pieces = [
        lax.dynamic_index_in_dim(grid, (place - by) % plan.members, 1, keepdims=False).reshape(rows)
        for by in range(plan.members)
    ]
    segq = seg_pieces[0]
    segk = jnp.concatenate(seg_pieces)
    token = (
        lax.broadcasted_iota(jnp.int32, (plan.n_ctx, plan.r), 0) * plan.tok_rows
        + place * plan.r
        + lax.broadcasted_iota(jnp.int32, (plan.n_ctx, plan.r), 1)
    ).reshape(rows)
    first = jnp.sum((line[None, :] < segq[:, None]).astype(jnp.int32), axis=1)
    position = (token - first).astype(F32)
    exponent = jnp.arange(HEAD_DIM // 2, dtype=F32) * (-2.0 / HEAD_DIM)
    angles = position[:, None] * (ROPE_BASE**exponent)[None, :]
    cosine, sine = jnp.cos(angles), jnp.sin(angles)
    cos_rows = jnp.concatenate([cosine] * 4, axis=1)
    sin_rows = jnp.concatenate([-sine, sine] * 2, axis=1)
    qmarks, kmarks = query_marks(segq), key_marks(segk)

    w_kv = w_mix = get_wide.result()
    w_in = get_in.result()
    gains = gains_of(w_mix)

    def first_half(x):
        a, kv = keys_values(x, gains, w_kv, cos_rows, sin_rows)
        kv_list = plan.gather_rows(kv)
        return a, kv_list, queries_of(a, w_mix, cos_rows, sin_rows)

    got = get_gate.advance(*got), get_back.advance(*got)
    _, kv_list, q = first_half(own)
    half = PAIRS // 2
    o_first, _ = attend(after(q, *got), kv_list, qmarks, kmarks, 0, half)
    got = get_gate.advance(late=(o_first,)), get_back.advance(late=(o_first,))
    o_last, _ = attend(after(q, *got), kv_list, qmarks, kmarks, half, half)
    while get_gate.k < plan.half:
        got = get_gate.advance(late=(o_last,)), get_back.advance(late=(o_last,))
    h, b = project(own, [o_first, o_last], gains, w_mix)
    w_gate, w_back = get_gate.result(), get_back.result()
    (z,) = ffn_in(b, w_in, w_gate, False)
    first_out = ffn_out(h, z, w_back)

    def forward(x):
        a, kv_list, q = first_half(x)
        o, lse = attend(q, kv_list, qmarks, kmarks, 0, PAIRS)
        h, b = project(x, [o], gains, w_mix)
        z, act, slope = ffn_in(b, w_in, w_gate, True)
        return ffn_out(h, z, w_back), (x, a, q, kv_list, o, lse, h, b, z, act, slope)

    def backward(stash, grad):
        x, a, q, kv_list, o, lse, h, b, z, act, slope = stash
        da, dg = ffn_back(grad, act, slope, w_back)
        dh, dh_low, _ = hidden_back(grad, da, dg, h, gains, w_in, w_gate)
        dq, terms = attend_back(
            q, kv_list, dh_low, o, lse, qmarks, kmarks, w_mix, cos_rows, sin_rows, 0
        )
        dkv = keys_back(plan.scatter_rows(terms), cos_rows, sin_rows)
        return input_back(x, dh, [dq], [dkv], gains, w_kv, w_mix)[0]

    def last_backward(stash, grad):
        x, a, q, kv_list, o, lse, h, b, z, act, slope = stash
        clock = Clock()
        back = Reduce(plan, clock, [grad], [z])
        da, dg = ffn_back(clock.tie(grad), act, slope, w_back)
        clock.mark(da)
        grow = Reduce(plan, clock, [b], [da, dg])
        grow.theirs()
        back.theirs()
        grow.mine()
        back.mine()
        dh, dh_low, gain_second = hidden_back(clock.tie(grad), da, dg, h, gains, w_in, w_gate)
        clock.mark(dh)
        grow.advance()
        back.advance()
        out = Reduce(plan, clock, [o], [dh_low])
        out.theirs()
        parts = []
        count = PAIRS // 4
        for n in range(4):
            cut = slice(n * count * LANES, (n + 1) * count * LANES)
            dq, terms = attend_back(
                clock.tie(q),
                kv_list,
                dh_low,
                o[:, cut],
                lse[n * count : (n + 1) * count],
                qmarks,
                kmarks,
                w_mix,
                cos_rows,
                sin_rows,
                n * count,
            )
            clock.mark(dq)
            parts.append((dq, plan.scatter_rows(terms)))
            if n == 0:
                out.mine()
            elif n == 1:
                for one in (grow, back, out):
                    one.advance()
        dkv_list = [keys_back(terms, cos_rows, sin_rows) for _, terms in parts]
        dq_list = [dq for dq, _ in parts]
        mixed = Reduce(plan, clock, [a], dkv_list + dq_list)
        mixed.theirs()
        for one in (grow, back, out):
            one.advance()
        dx, gain_first = input_back(clock.tie(x), dh, dq_list, dkv_list, gains, w_kv, w_mix)
        clock.mark(dx)
        mixed.mine()
        while mixed.k:
            for one in (grow, back, out, mixed):
                if one.k:
                    one.advance()
        gain = plan.total(jnp.concatenate([gain_first, gain_second], axis=0))
        start = (plan.i * plan.nw + plan.w) * plan.wrows
        gain = lax.dynamic_slice_in_dim(gain, start, plan.wrows, 1)
        return dx, [back.result(), grow.result(), out.result(), mixed.result(), gain]

    def handed(array, by):
        pairs = [(s, s + by) for s in range(sections) if 0 <= s + by < sections]
        return lax.ppermute(array, "section", pairs)

    x_in = jnp.where(section == 0, own, handed(first_out, 1))
    out, stash = forward(x_in)
    first_dx = backward(stash, own)
    grad_in = jnp.where(section == sections - 1, own, after(handed(first_dx, -1), out))
    dx, (g_back, g_in, g_attn, g_mix, g_gain) = last_backward(stash, grad_in)
    boundary_local = plan.from_sequences(jnp.where(section == 0, dx, out))
    g_key, g_value = apart(g_mix[:, : 2 * D])
    return (
        boundary_local[None, :, None],
        jnp.concatenate([g_mix[:, 2 * D :], g_key, g_value], axis=1)[None],
        g_attn[None],
        jnp.concatenate([g_in[:, :FF], g_in[:, FFP : FFP + FF]], axis=1)[None],
        g_back[:, :FF].T[None],
        g_gain[None],
    )


def solution(mesh):
    placed = (
        P("section", None, "wshard", "ctx", None),
        P(None, "wshard", "ctx"),
        P("section", ("ctx", "wshard"), None),
        P("section", ("ctx", "wshard"), None),
        P("section", ("ctx", "wshard"), None),
        P("section", None, ("ctx", "wshard")),
        P("section", None, ("ctx", "wshard")),
    )
    return jax.shard_map(
        body,
        mesh=mesh,
        in_specs=placed,
        out_specs=(placed[0],) + placed[2:],
        check_vma=False,
    )
```

time: 715 us -> 604 us (0.84)
  Pallas kernels: 334 us -> 251 us
  waiting for transfers between devices: 196 us -> 149 us
  starting transfers between devices: 72.5 us -> 96.5 us
  local copies, waits for them, and re-layouts: 67.5 us -> 55.8 us
    ppermute x24 -> x32, waiting for transfers between devices: 142 us -> 93.2 us  [step(): return lax.ppermute(array, BOTH, self.ring_pairs)]
    pallas_call x22 -> x37, Pallas kernels: 182 us -> 140 us  [the longest x5 60.8 us: attend_back(): call(kernel, 'attend_back', flops=20 * rows * keys * count * LANES, moved...]
    broadcast_in_dim x5 -> x0, local copies, waits for them, and re-layouts: 15 us -> none  [the longest x3 12.2 us: travel(): whole_of[name] = jnp.zeros((self.n_ctx, self.nw * rows, shard.shape[1]), BF)]
    pallas_call x2, Pallas kernels: 28.5 us -> 15.4 us  [input_back(): call(kernel, 'input_back', flops=6 * rows * D * D, moved=2 * (3 * D * D +...]
    ppermute x24 -> x32, starting transfers between devices: 19.2 us -> 31.2 us  [step(): return lax.ppermute(array, BOTH, self.ring_pairs)]
    ppermute x2, waiting for transfers between devices: 47.3 us -> 37.3 us  [handed(): return lax.ppermute(array, 'section', pairs)]
    ppermute x0 -> x4, starting transfers between devices: none -> 9.11 us  [total(): value = value + lax.ppermute(value, BOTH, pairs)]
    pallas_call x2, Pallas kernels: 28.6 us -> 19.7 us  [hidden_back(): call(kernel, 'hidden_back', flops=4 * rows * D * FFP, moved=2 * (2 * D *...]
  transfers between devices with their start and end apart: 56 -> 77, of which waited for: 19 -> 25; matrix products, arithmetic and copies ran while one was open for 11% -> 10% of each run, Pallas kernels for 25% -> 23%
where the time goes in v3:
time: 604 us; the launch traced here: 594 us
  Pallas kernels  251 us (42%)
  waiting for transfers between devices  149 us (25%)
  starting transfers between devices  96.5 us (16%)
  local copies, waits for them, and re-layouts  55.8 us (9%)
  other arithmetic  29.7 us (5%)
  blocking collectives  8.42 us (1%)
    ppermute x32, waiting for transfers between devices, step(): return lax.ppermute(array, BOTH, self.ring_pairs)  93.2 us
    pallas_call x5, Pallas kernels, attend_back(): call(kernel, 'attend_back', flops=20 * rows * keys * count * LANES, moved...  60.8 us
    ppermute x2, waiting for transfers between devices, handed(): return lax.ppermute(array, 'section', pairs)  37.3 us
    pallas_call x3, Pallas kernels, attend(): call(kernel, 'attend', flops=8 * rows * keys * count * LANES, moved=2 * (...  35.6 us
    pallas_call x8, Pallas kernels, weight_rows(): call(kernel, 'weight_rows', limit=max(8, 4 + int(1.25 * size) // (1024 *...  32.7 us
    ppermute x32, starting transfers between devices, step(): return lax.ppermute(array, BOTH, self.ring_pairs)  31.2 us
    ppermute x29, starting transfers between devices, swap(): return lax.ppermute(array, 'wshard', [(0, 1), (1, 0)])  30 us
    dynamic_update_slice x24, local copies, waits for them, and re-layouts, put(): self.whole = lax.dynamic_update_index_in_dim(self.whole, block, chip, 0)  24.7 us
  transfers between devices with their start and end apart: 77, of which 25 were waited for; matrix products, arithmetic and copies ran while one was open for 10% of the time, Pallas kernels for 23%

profile of v3, /device:TPU:13, one launch (start us, length us, event | category | flops | bytes accessed | tf_op | source)
XLA Modules:
  0.0 593.6 jit_solution(2817823540514214716)
XLA Ops:
  22.6 8.9 %collective-permute-done.2 = bf16[128,4224]{1,0:T(8,128)(2,1)S(1)} collective-permute-done((bf16[128,4224]{1,0:T(8,128)(2,1)S(1)}, bf16[128,4224]{1,0:T(8,128)(2,1)S(1)}, u32[]{:S(2)}, u32[]{:S(2)}) %collective-permute-start.2) | collective-permute-done | bytes 1081376 | tf_op jit(solution)/shard_map/ppermute | solution.py:666
  47.0 13.6 %collective-permute-done.14 = bf16[128,2688]{1,0:T(8,128)(2,1)} collective-permute-done((bf16[128,2688]{1,0:T(8,128)(2,1)S(1)}, bf16[128,2688]{1,0:T(8,128)(2,1)}, u32[]{:S(2)}, u32[]{:S(2)}) %collective-permute-start.14) | collective-permute-done | bytes 688160 | tf_op jit(solution)/shard_map/ppermute | solution.py:666
  102.5 15.2 %collective-permute-done.9 = bf16[64,4224]{1,0:T(8,128)(2,1)S(1)} collective-permute-done((bf16[64,4224]{1,0:T(8,128)(2,1)S(1)}, bf16[64,4224]{1,0:T(8,128)(2,1)S(1)}, u32[]{:S(2)}, u32[]{:S(2)}) %collective-permute-start.9) | collective-permute-done | bytes 540704 | tf_op jit(solution)/shard_map/ppermute | solution.py:666
  124.9 6.2 %keys_values.2 = (bf16[512,1024]{1,0:T(8,128)(2,1)S(1)}, bf16[512,2048]{1,0:T(8,128)(2,1)S(1)}) custom-call(bf16[512,1024]{1,0:T(8,128)(2,1)S(1)} %bitcast.160, f32[8,1024]{1,0:T(8,128)S(1)} %gains.1.gain_ref, bf16[1024,4224]{1,0:T(8,128)(2,1)} %bitcast.19.w_ref.wkv_ref.wq_ref, f32[512,128]{1,0:T(8,128)S(1)} %get-tuple-element.250.cos_ref, ...), custom_call_target="tpu_custom_call" | custom-call | flops 2147483648 | bytes 8388608 | tf_op jit(solution)/shard_map/keys_values/pallas_call | solution.py:129
  144.6 9.2 %attend.3 = (bf16[512,512]{1,0:T(8,128)(2,1)S(1)}, f32[4,2,512]{2,1,0:T(2,128)}) custom-call(bf16[512,1024]{1,0:T(8,128)(2,1)S(1)} %queries.2.q_ref, bf16[512,128]{1,0:T(8,128)(2,1)S(1)} %select_convert_fusion.1.qm_ref, bf16[1024,128]{1,0:T(8,128)(2,1)S(1)} %select_convert_fusion.km_ref, bf16[512,2048]{1,0:T(8,128)(2,1)S(1)} %get-tuple-element.107.refs_0_, ...), custom_call_target="tpu_custom_call" | custom-call | flops 2147483648 | bytes 3145728 | tf_op jit(solution)/shard_map/attend/pallas_call | solution.py:212
  159.4 9.2 %attend.4 = (bf16[512,512]{1,0:T(8,128)(2,1)S(1)}, f32[4,2,512]{2,1,0:T(2,128)}) custom-call(bf16[512,1024]{1,0:T(8,128)(2,1)S(1)} %queries.2.q_ref, bf16[512,128]{1,0:T(8,128)(2,1)S(1)} %select_convert_fusion.1.qm_ref, bf16[1024,128]{1,0:T(8,128)(2,1)S(1)} %select_convert_fusion.km_ref, bf16[512,2048]{1,0:T(8,128)(2,1)S(1)} %get-tuple-element.107.refs_0_, ...), custom_call_target="tpu_custom_call" | custom-call | flops 2147483648 | bytes 3145728 | tf_op jit(solution)/shard_map/attend/pallas_call | solution.py:212
  183.7 10.3 %ffn_in.2.z_ref = bf16[512,2688]{1,0:T(8,128)(2,1)S(1)} custom-call(bf16[512,1024]{1,0:T(8,128)(2,1)S(1)} %get-tuple-element.114.b_ref, bf16[1024,2688]{1,0:T(8,128)(2,1)} %bitcast.36.wa_ref, bf16[1024,2688]{1,0:T(8,128)(2,1)S(1)} %bitcast.166), custom_call_target="tpu_custom_call" | custom-call | flops 5637144576 | bytes 14811136 | tf_op jit(solution)/shard_map/ffn_in/pallas_call | solution.py:288
  196.0 5.8 ffn_out.2
  206.0 21.4 %collective-permute-done.38 = bf16[512,1024]{1,0:T(8,128)(2,1)} collective-permute-done((bf16[512,1024]{1,0:T(8,128)(2,1)S(1)}, bf16[512,1024]{1,0:T(8,128)(2,1)}, u32[]{:S(2)}, u32[]{:S(2)}) %collective-permute-start.38) | collective-permute-done | bytes 1048608 | tf_op jit(solution)/shard_map/ppermute | solution.py:967
  227.7 6.4 %keys_values.3 = (bf16[512,1024]{1,0:T(8,128)(2,1)S(1)}, bf16[512,2048]{1,0:T(8,128)(2,1)S(1)}) custom-call(bf16[512,1024]{1,0:T(8,128)(2,1)S(1)} %broadcast_select_fusion.2.x_ref, f32[8,1024]{1,0:T(8,128)S(1)} %gains.1.gain_ref, bf16[1024,4224]{1,0:T(8,128)(2,1)} %bitcast.19.w_ref.wkv_ref.wq_ref, f32[512,128]{1,0:T(8,128)S(1)} %get-tuple-element.250.cos_ref, ...), custom_call_target="tpu_custom_call" | custom-call | flops 2147483648 | bytes 8388608 | tf_op jit(solution)/shard_map/keys_values/pallas_call | solution.py:129
  239.0 17.2 %attend.5 = (bf16[512,1024]{1,0:T(8,128)(2,1)S(1)}, f32[8,2,512]{2,1,0:T(2,128)S(1)}) custom-call(bf16[512,1024]{1,0:T(8,128)(2,1)S(1)} %queries.3.q_ref, bf16[512,128]{1,0:T(8,128)(2,1)S(1)} %select_convert_fusion.1.qm_ref, bf16[1024,128]{1,0:T(8,128)(2,1)S(1)} %select_convert_fusion.km_ref, bf16[512,2048]{1,0:T(8,128)(2,1)S(1)} %get-tuple-element.120.refs_0_, ...), custom_call_target="tpu_custom_call" | custom-call | flops 4294967296 | bytes 6291456 | tf_op jit(solution)/shard_map/attend/pallas_call | solution.py:212
  259.9 10.5 %ffn_in.3 = (bf16[512,2688]{1,0:T(8,128)(2,1)S(1)}, bf16[512,2688]{1,0:T(8,128)(2,1)S(1)}, bf16[512,2688]{1,0:T(8,128)(2,1)S(1)}) custom-call(bf16[512,1024]{1,0:T(8,128)(2,1)S(1)} %get-tuple-element.141.b_ref.refs_0_, bf16[1024,2688]{1,0:T(8,128)(2,1)} %bitcast.36.wa_ref, bf16[1024,2688]{1,0:T(8,128)(2,1)S(1)} %bitcast.169), custom_call_target="tpu_custom_call" | custom-call | flops 5637144576 | bytes 20316160 | tf_op jit(solution)/shard_map/ffn_in/pallas_call | solution.py:288
  272.0 7.6 %ffn_back.2 = (bf16[512,2688]{1,0:T(8,128)(2,1)S(1)}, bf16[512,2688]{1,0:T(8,128)(2,1)S(1)}) custom-call(bf16[512,1024]{1,0:T(8,128)(2,1)S(1)} %bitcast.162, bf16[512,2688]{1,0:T(8,128)(2,1)S(1)} %get-tuple-element.123.act_ref, bf16[512,2688]{1,0:T(8,128)(2,1)S(1)} %get-tuple-element.124.slope_ref, bf16[1024,2688]{1,0:T(8,128)(2,1)} %bitcast.54.w_ref), custom_call_target="tpu_custom_call" | custom-call | flops 2818572288 | bytes 17563648 | tf_op jit(solution)/shard_map/ffn_back/pallas_call | solution.py:332
  279.7 10.1 %hidden_back.2 = (f32[512,1024]{1,0:T(8,128)S(1)}, bf16[512,1024]{1,0:T(8,128)(2,1)S(1)}, f32[1,1024]{1,0:T(1,128)}) custom-call(bf16[512,1024]{1,0:T(8,128)(2,1)S(1)} %bitcast.163, bf16[512,2688]{1,0:T(8,128)(2,1)S(1)} %get-tuple-element.125.da_ref, bf16[512,2688]{1,0:T(8,128)(2,1)S(1)} %get-tuple-element.126.dg_ref, ...), custom_call_target="tpu_custom_call" | custom-call | flops 5637144576 | bytes 22806528 | tf_op jit(solution)/shard_map/hidden_back/pallas_call | solution.py:362
  289.8 29.6 %attend_back.5 = (bf16[512,1024]{1,0:T(8,128)(2,1)S(1)}, bf16[512,2048]{1,0:T(8,128)(2,1)S(1)}, bf16[512,2048]{1,0:T(8,128)(2,1)S(1)}) custom-call(bf16[512,1024]{1,0:T(8,128)(2,1)S(1)} %queries.3.q_ref, bf16[512,1024]{1,0:T(8,128)(2,1)S(1)} %get-tuple-element.129.dh_ref, bf16[1024,4224]{1,0:T(8,128)(2,1)} %bitcast.19.w_ref.wkv_ref.wq_ref, ...), custom_call_target="tpu_custom_call" | custom-call | flops 10737418240 | bytes 14680064 | tf_op jit(solution)/shard_map/attend_back/pallas_call | solution.py:430
  326.1 8.0 %input_back.2 = (bf16[512,1024]{1,0:T(8,128)(2,1)S(1)}, f32[1,1024]{1,0:T(1,128)}) custom-call(bf16[512,1024]{1,0:T(8,128)(2,1)S(1)} %broadcast_select_fusion.2.x_ref, f32[512,1024]{1,0:T(8,128)S(1)} %get-tuple-element.128.dh_ref, f32[8,1024]{1,0:T(8,128)S(1)} %gains.1.gain_ref, bf16[1024,4224]{1,0:T(8,128)(2,1)} %bitcast.19.w_ref.wkv_ref.wq_ref, ...), custom_call_target="tpu_custom_call" | custom-call | flops 3221225472 | bytes 16777216 | tf_op jit(solution)/shard_map/input_back/pallas_call | solution.py:506
  338.9 6.4 %ffn_out.3 = bf16[512,1024]{1,0:T(8,128)(2,1)S(1)} custom-call(f32[512,1024]{1,0:T(8,128)S(1)} %copy-done.54, bf16[512,2688]{1,0:T(8,128)(2,1)S(1)} %copy-done.10, bf16[1024,2688]{1,0:T(8,128)(2,1)} %bitcast.54.w_ref), custom_call_target="tpu_custom_call" | custom-call | flops 2818572288 | bytes 11403264 | tf_op jit(solution)/shard_map/ffn_out/pallas_call | solution.py:307
  346.3 15.9 %collective-permute-done.41 = bf16[512,1024]{1,0:T(8,128)(2,1)} collective-permute-done((bf16[512,1024]{1,0:T(8,128)(2,1)S(1)}, bf16[512,1024]{1,0:T(8,128)(2,1)}, u32[]{:S(2)}, u32[]{:S(2)}) %collective-permute-start.41) | collective-permute-done | bytes 1048608 | tf_op jit(solution)/shard_map/ppermute | solution.py:967
  363.5 6.7 %ffn_back.3 = (bf16[512,2688]{1,0:T(8,128)(2,1)S(1)}, bf16[512,2688]{1,0:T(8,128)(2,1)S(1)}) custom-call(bf16[512,1024]{1,0:T(8,128)(2,1)S(1)} %broadcast_select_fusion.g_ref.refs_0_, bf16[512,2688]{1,0:T(8,128)(2,1)S(1)} %copy-done.20, bf16[512,2688]{1,0:T(8,128)(2,1)S(1)} %copy-done.22, bf16[1024,2688]{1,0:T(8,128)(2,1)} %bitcast.54.w_ref), custom_call_target="tpu_custom_call" | custom-call | flops 2818572288 | bytes 17563648 | tf_op jit(solution)/shard_map/ffn_back/pallas_call | solution.py:332
  370.3 5.8 weight_rows.8
  388.0 6.3 %weight_rows.10 = (bf16[64,5376]{1,0:T(8,128)(2,1)S(1)}, bf16[512,5376]{1,0:T(8,128)(2,1)S(1)}) custom-call(s32[9]{0:T(128)S(1)} %stack.67.order_ref, bf16[512,1024]{1,0:T(8,128)(2,1)S(1)} %copy-done.60, bf16[512,2688]{1,0:T(8,128)(2,1)S(1)} %get-tuple-element.137.refs_1_.da_ref, bf16[512,2688]{1,0:T(8,128)(2,1)S(1)} %copy-done.43, ...), custom_call_target="tpu_custom_call" | custom-call | flops 3170893824 | bytes 17563648 | tf_op jit(solution)/shard_map/weight_rows/pallas_call | solution.py:565
  404.3 9.6 %hidden_back.3 = (f32[512,1024]{1,0:T(8,128)S(1)}, bf16[512,1024]{1,0:T(8,128)(2,1)S(1)}, f32[1,1024]{1,0:T(1,128)S(1)}) custom-call(bf16[512,1024]{1,0:T(8,128)(2,1)S(1)} %copy-done.14, bf16[512,2688]{1,0:T(8,128)(2,1)S(1)} %copy-done.41, bf16[512,2688]{1,0:T(8,128)(2,1)S(1)} %copy-done.44, f32[512,1024]{1,0:T(8,128)S(1)} %copy-done.55, ...), custom_call_target="tpu_custom_call" | custom-call | flops 5637144576 | bytes 22806528 | tf_op jit(solution)/shard_map/hidden_back/pallas_call | solution.py:362
  419.5 7.8 %attend_back.6 = (bf16[512,256]{1,0:T(8,128)(2,1)S(1)}, bf16[512,512]{1,0:T(8,128)(2,1)S(1)}, bf16[512,512]{1,0:T(8,128)(2,1)S(1)}) custom-call(bf16[512,1024]{1,0:T(8,128)(2,1)S(1)} %copy-done.8, bf16[512,1024]{1,0:T(8,128)(2,1)S(1)} %get-tuple-element.152.refs_1_.dh_ref, bf16[1024,4224]{1,0:T(8,128)(2,1)} %bitcast.19.w_ref.wkv_ref.wq_ref, ...), custom_call_target="tpu_custom_call" | custom-call | flops 2684354560 | bytes 3670016 | tf_op jit(solution)/shard_map/attend_back/pallas_call | solution.py:430
  430.0 7.8 %attend_back.7 = (bf16[512,256]{1,0:T(8,128)(2,1)S(1)}, bf16[512,512]{1,0:T(8,128)(2,1)S(1)}, bf16[512,512]{1,0:T(8,128)(2,1)S(1)}) custom-call(bf16[512,1024]{1,0:T(8,128)(2,1)S(1)} %copy-done.8, bf16[512,1024]{1,0:T(8,128)(2,1)S(1)} %get-tuple-element.152.refs_1_.dh_ref, bf16[1024,4224]{1,0:T(8,128)(2,1)} %bitcast.19.w_ref.wkv_ref.wq_ref, ...), custom_call_target="tpu_custom_call" | custom-call | flops 2684354560 | bytes 3670016 | tf_op jit(solution)/shard_map/attend_back/pallas_call | solution.py:430
  440.8 7.8 %attend_back.8 = (bf16[512,256]{1,0:T(8,128)(2,1)S(1)}, bf16[512,512]{1,0:T(8,128)(2,1)S(1)}, bf16[512,512]{1,0:T(8,128)(2,1)S(1)}) custom-call(bf16[512,1024]{1,0:T(8,128)(2,1)S(1)} %copy-done.8, bf16[512,1024]{1,0:T(8,128)(2,1)S(1)} %get-tuple-element.152.refs_1_.dh_ref, bf16[1024,4224]{1,0:T(8,128)(2,1)} %bitcast.19.w_ref.wkv_ref.wq_ref, ...), custom_call_target="tpu_custom_call" | custom-call | flops 2684354560 | bytes 3670016 | tf_op jit(solution)/shard_map/attend_back/pallas_call | solution.py:430
  450.9 7.8 %attend_back.9 = (bf16[512,256]{1,0:T(8,128)(2,1)S(1)}, bf16[512,512]{1,0:T(8,128)(2,1)S(1)}, bf16[512,512]{1,0:T(8,128)(2,1)S(1)}) custom-call(bf16[512,1024]{1,0:T(8,128)(2,1)S(1)} %copy-done.8, bf16[512,1024]{1,0:T(8,128)(2,1)S(1)} %get-tuple-element.152.refs_1_.dh_ref, bf16[1024,4224]{1,0:T(8,128)(2,1)} %bitcast.19.w_ref.wkv_ref.wq_ref, ...), custom_call_target="tpu_custom_call" | custom-call | flops 2684354560 | bytes 3670016 | tf_op jit(solution)/shard_map/attend_back/pallas_call | solution.py:430
  472.5 7.4 %input_back.3 = (bf16[512,1024]{1,0:T(8,128)(2,1)S(1)}, f32[1,1024]{1,0:T(1,128)S(1)}) custom-call(bf16[512,1024]{1,0:T(8,128)(2,1)S(1)} %copy-done.6, f32[512,1024]{1,0:T(8,128)S(1)} %get-tuple-element.148.dh_ref, f32[8,1024]{1,0:T(8,128)S(1)} %copy-done.57, bf16[1024,4224]{1,0:T(8,128)(2,1)} %bitcast.19.w_ref.wkv_ref.wq_ref, ...), custom_call_target="tpu_custom_call" | custom-call | flops 3221225472 | bytes 16777216 | tf_op jit(solution)/shard_map/input_back/pallas_call | solution.py:506
  486.1 6.9 %collective-permute-start.72 = (f32[2,1024]{1,0:T(2,128)S(1)}, f32[2,1024]{1,0:T(2,128)S(1)}, u32[]{:S(2)}, u32[]{:S(2)}) collective-permute-start(f32[2,1024]{1,0:T(2,128)S(1)} %fusion.16), channel_id=1, source_target_pairs={{0,4},{1,5},{2,6},{3,7},{4,0},{5,1},{6,2},{7,3},{8,12},{9,13},{10,... | collective-permute-start | bytes 24584 | tf_op jit(solution)/shard_map/ppermute | solution.py:692
  518.7 15.6 %collective-permute-done.66 = bf16[128,5376]{1,0:T(8,128)(2,1)} collective-permute-done((bf16[128,5376]{1,0:T(8,128)(2,1)}, bf16[128,5376]{1,0:T(8,128)(2,1)}, u32[]{:S(2)}, u32[]{:S(2)}) %collective-permute-start.66) | collective-permute-done | bytes 1376288 | tf_op jit(solution)/shard_map/ppermute | solution.py:666
  537.7 6.4 %collective-permute-done.58.moving_ref = bf16[64,3072]{1,0:T(8,128)(2,1)S(1)} collective-permute-done((bf16[64,3072]{1,0:T(8,128)(2,1)S(1)}, bf16[64,3072]{1,0:T(8,128)(2,1)S(1)}, u32[]{:S(2)}, u32[]{:S(2)}) %collective-permute-start.58) | collective-permute-done | bytes 393248 | tf_op jit(solution)/shard_map/ppermute | solution.py:666
  563.0 9.7 %collective-permute-done.61.moving_ref = bf16[128,3072]{1,0:T(8,128)(2,1)S(1)} collective-permute-done((bf16[128,3072]{1,0:T(8,128)(2,1)S(1)}, bf16[128,3072]{1,0:T(8,128)(2,1)S(1)}, u32[]{:S(2)}, u32[]{:S(2)}) %collective-permute-start.61) | collective-permute-done | bytes 786464 | tf_op jit(solution)/shard_map/ppermute | solution.py:666
  577.1 7.0 %collective-permute-done.62 = bf16[128,3072]{1,0:T(8,128)(2,1)S(1)} collective-permute-done((bf16[128,3072]{1,0:T(8,128)(2,1)S(1)}, bf16[128,3072]{1,0:T(8,128)(2,1)S(1)}, u32[]{:S(2)}, u32[]{:S(2)}) %collective-permute-start.62) | collective-permute-done | bytes 786464 | tf_op jit(solution)/shard_map/ppermute | solution.py:666
  (450 shorter events, 266.3 us)
Async XLA Ops:
  12.3 19.2 %collective-permute-start.2 = (bf16[128,4224]{1,0:T(8,128)(2,1)S(1)}, bf16[128,4224]{1,0:T(8,128)(2,1)S(1)}, u32[]{:S(2)}, u32[]{:S(2)}) collective-permute-start(bf16[128,4224]{1,0:T(8,128)(2,1)S(1)} %pad_maximum_fusion), channel_id=1, source_target_pairs={{0,4},{1,3},{4,8},{5,1},{8,12},{9,5},{12,14},{13,9},{14,10},{15,13... | collective-permute-start | bytes 3244040 | tf_op jit(solution)/shard_map/ppermute | solution.py:666
  20.1 18.8 %collective-permute-start.11 = (bf16[128,2688]{1,0:T(8,128)(2,1)S(1)}, bf16[128,2688]{1,0:T(8,128)(2,1)S(1)}, u32[]{:S(2)}, u32[]{:S(2)}) collective-permute-start(bf16[128,2688]{1,0:T(8,128)(2,1)S(1)} %collective-permute-done.3), channel_id=1, source_target_pairs={{0,4},{1,3},{4,8},{5,1},{8,12},{9,5},{12,14},{13,9},{14,10},{15,13... | collective-permute-start | bytes 2064392 | tf_op jit(solution)/shard_map/ppermute | solution.py:666
  21.2 19.0 %collective-permute-start.22 = (bf16[128,2688]{1,0:T(8,128)(2,1)S(1)}, bf16[128,2688]{1,0:T(8,128)(2,1)S(1)}, u32[]{:S(2)}, u32[]{:S(2)}) collective-permute-start(bf16[128,2688]{1,0:T(8,128)(2,1)S(1)} %collective-permute-done.3), channel_id=1, source_target_pairs={{0,1},{1,0},{2,3},{3,2},{4,5},{5,4},{6,7},{7,6},{8,9},{9,8},{10,11... | collective-permute-start | bytes 2064392 | tf_op jit(solution)/shard_map/ppermute | solution.py:663
  32.8 34.9 %collective-permute-start.4 = (bf16[128,4224]{1,0:T(8,128)(2,1)S(1)}, bf16[128,4224]{1,0:T(8,128)(2,1)S(1)}, u32[]{:S(2)}, u32[]{:S(2)}) collective-permute-start(bf16[128,4224]{1,0:T(8,128)(2,1)S(1)} %collective-permute-done.2), channel_id=1, source_target_pairs={{0,1},{1,0},{2,3},{3,2},{4,5},{5,4},{6,7},{7,6},{8,9},{9,8},{10,11... | collective-permute-start | bytes 3244040 | tf_op jit(solution)/shard_map/ppermute | solution.py:663
  38.8 28.4 %collective-permute-start.5 = (bf16[128,4224]{1,0:T(8,128)(2,1)S(1)}, bf16[128,4224]{1,0:T(8,128)(2,1)}, u32[]{:S(2)}, u32[]{:S(2)}) collective-permute-start(bf16[128,4224]{1,0:T(8,128)(2,1)S(1)} %collective-permute-done.2), channel_id=1, source_target_pairs={{0,4},{1,3},{4,8},{5,1},{8,12},{9,5},{12,14},{13,9},{14,10},{15,13... | collective-permute-start | bytes 3244040 | tf_op jit(solution)/shard_map/ppermute | solution.py:666
  40.1 20.5 %collective-permute-start.14 = (bf16[128,2688]{1,0:T(8,128)(2,1)S(1)}, bf16[128,2688]{1,0:T(8,128)(2,1)}, u32[]{:S(2)}, u32[]{:S(2)}) collective-permute-start(bf16[128,2688]{1,0:T(8,128)(2,1)S(1)} %collective-permute-done.11), channel_id=1, source_target_pairs={{0,4},{1,3},{4,8},{5,1},{8,12},{9,5},{12,14},{13,9},{14,10},{15,13... | collective-permute-start | bytes 2064392 | tf_op jit(solution)/shard_map/ppermute | solution.py:666
  43.2 21.1 %collective-permute-start.23 = (bf16[128,2688]{1,0:T(8,128)(2,1)S(1)}, bf16[128,2688]{1,0:T(8,128)(2,1)S(1)}, u32[]{:S(2)}, u32[]{:S(2)}) collective-permute-start(bf16[128,2688]{1,0:T(8,128)(2,1)S(1)} %collective-permute-done.11), channel_id=1, source_target_pairs={{0,1},{1,0},{2,3},{3,2},{4,5},{5,4},{6,7},{7,6},{8,9},{9,8},{10,11... | collective-permute-start | bytes 2064392 | tf_op jit(solution)/shard_map/ppermute | solution.py:663
  61.6 30.0 %collective-permute-start.15 = (bf16[64,2688]{1,0:T(8,128)(2,1)S(1)}, bf16[64,2688]{1,0:T(8,128)(2,1)S(1)}, u32[]{:S(2)}, u32[]{:S(2)}) collective-permute-start(bf16[64,2688]{1,0:T(8,128)(2,1)S(1)} %constant_dynamic-slice_fusion.5), channel_id=1, source_target_pairs={{0,4},{1,3},{4,8},{5,1},{8,12},{9,5},{12,14},{13,9},{14,10},{15,13... | collective-permute-start | bytes 1032200 | tf_op jit(solution)/shard_map/ppermute | solution.py:666
  63.0 32.9 %collective-permute-start.24 = (bf16[128,2688]{1,0:T(8,128)(2,1)}, bf16[128,2688]{1,0:T(8,128)(2,1)}, u32[]{:S(2)}, u32[]{:S(2)}) collective-permute-start(bf16[128,2688]{1,0:T(8,128)(2,1)} %collective-permute-done.14), channel_id=1, source_target_pairs={{0,1},{1,0},{2,3},{3,2},{4,5},{5,4},{6,7},{7,6},{8,9},{9,8},{10,11... | collective-permute-start | bytes 2064392 | tf_op jit(solution)/shard_map/ppermute | solution.py:663
  67.2 32.9 %collective-permute-start.6 = (bf16[128,4224]{1,0:T(8,128)(2,1)}, bf16[128,4224]{1,0:T(8,128)(2,1)}, u32[]{:S(2)}, u32[]{:S(2)}) collective-permute-start(bf16[128,4224]{1,0:T(8,128)(2,1)} %collective-permute-done.5), channel_id=1, source_target_pairs={{0,1},{1,0},{2,3},{3,2},{4,5},{5,4},{6,7},{7,6},{8,9},{9,8},{10,11... | collective-permute-start | bytes 3244040 | tf_op jit(solution)/shard_map/ppermute | solution.py:663
  67.7 31.2 %collective-permute-start.7 = (bf16[128,4224]{1,0:T(8,128)(2,1)}, bf16[128,4224]{1,0:T(8,128)(2,1)S(1)}, u32[]{:S(2)}, u32[]{:S(2)}) collective-permute-start(bf16[128,4224]{1,0:T(8,128)(2,1)} %collective-permute-done.5), channel_id=1, source_target_pairs={{0,4},{1,3},{4,8},{5,1},{8,12},{9,5},{12,14},{13,9},{14,10},{15,13... | collective-permute-start | bytes 3244040 | tf_op jit(solution)/shard_map/ppermute | solution.py:666
  84.1 40.8 %all-to-all-start.1 = ((bf16[8,64,1024]{2,1,0:T(8,128)(2,1)}), bf16[8,64,1024]{2,1,0:T(8,128)(2,1)S(1)}, u32[]{:S(2)}, u32[]{:S(2)}) async-start(bf16[8,64,1024]{2,1,0:T(8,128)(2,1)} %bitcast.9), calls=%async_computation.1 | async-start | bytes 2097152 | tf_op jit(solution)/shard_map/all_to_all | solution.py:680
  98.9 18.8 %collective-permute-start.9 = (bf16[64,4224]{1,0:T(8,128)(2,1)S(1)}, bf16[64,4224]{1,0:T(8,128)(2,1)S(1)}, u32[]{:S(2)}, u32[]{:S(2)}) collective-permute-start(bf16[64,4224]{1,0:T(8,128)(2,1)S(1)} %constant_dynamic-slice_fusion.7), channel_id=1, source_target_pairs={{0,4},{1,3},{4,8},{5,1},{8,12},{9,5},{12,14},{13,9},{14,10},{15,13... | collective-permute-start | bytes 1622024 | tf_op jit(solution)/shard_map/ppermute | solution.py:666
  100.2 21.5 %collective-permute-start.8 = (bf16[128,4224]{1,0:T(8,128)(2,1)S(1)}, bf16[128,4224]{1,0:T(8,128)(2,1)S(1)}, u32[]{:S(2)}, u32[]{:S(2)}) collective-permute-start(bf16[128,4224]{1,0:T(8,128)(2,1)S(1)} %collective-permute-done.7), channel_id=1, source_target_pairs={{0,1},{1,0},{2,3},{3,2},{4,5},{5,4},{6,7},{7,6},{8,9},{9,8},{10,11... | collective-permute-start | bytes 3244040 | tf_op jit(solution)/shard_map/ppermute | solution.py:663
  153.8 20.3 %collective-permute-start.27 = (bf16[128,2688]{1,0:T(8,128)(2,1)S(1)}, bf16[128,2688]{1,0:T(8,128)(2,1)S(1)}, u32[]{:S(2)}, u32[]{:S(2)}) collective-permute-start(bf16[128,2688]{1,0:T(8,128)(2,1)S(1)} %collective-permute-done.20), channel_id=1, source_target_pairs={{0,1},{1,0},{2,3},{3,2},{4,5},{5,4},{6,7},{7,6},{8,9},{9,8},{10,11... | collective-permute-start | bytes 2064392 | tf_op jit(solution)/shard_map/ppermute | solution.py:663
  156.6 18.0 %collective-permute-start.33 = (bf16[128,2688]{1,0:T(8,128)(2,1)S(1)}, bf16[128,2688]{1,0:T(8,128)(2,1)S(1)}, u32[]{:S(2)}, u32[]{:S(2)}) collective-permute-start(bf16[128,2688]{1,0:T(8,128)(2,1)S(1)} %collective-permute-done.21), channel_id=1, source_target_pairs={{0,1},{1,0},{2,3},{3,2},{4,5},{5,4},{6,7},{7,6},{8,9},{9,8},{10,11... | collective-permute-start | bytes 2064392 | tf_op jit(solution)/shard_map/ppermute | solution.py:663
  173.6 20.6 %collective-permute-start.35 = (bf16[128,2688]{1,0:T(8,128)(2,1)S(1)}, bf16[128,2688]{1,0:T(8,128)(2,1)S(1)}, u32[]{:S(2)}, u32[]{:S(2)}) collective-permute-start(bf16[128,2688]{1,0:T(8,128)(2,1)S(1)} %collective-permute-done.34), channel_id=1, source_target_pairs={{0,1},{1,0},{2,3},{3,2},{4,5},{5,4},{6,7},{7,6},{8,9},{9,8},{10,11... | collective-permute-start | bytes 2064392 | tf_op jit(solution)/shard_map/ppermute | solution.py:663
  201.8 25.7 %collective-permute-start.38 = (bf16[512,1024]{1,0:T(8,128)(2,1)S(1)}, bf16[512,1024]{1,0:T(8,128)(2,1)}, u32[]{:S(2)}, u32[]{:S(2)}) collective-permute-start(bf16[512,1024]{1,0:T(8,128)(2,1)S(1)} %ffn_out.2), channel_id=1, source_target_pairs={{0,16},{1,17},{2,18},{3,19},{4,20},{5,21},{6,22},{7,23},{8,24},{9,... | collective-permute-start | bytes 3145736 | tf_op jit(solution)/shard_map/ppermute | solution.py:967
  334.1 28.1 %collective-permute-start.41 = (bf16[512,1024]{1,0:T(8,128)(2,1)S(1)}, bf16[512,1024]{1,0:T(8,128)(2,1)}, u32[]{:S(2)}, u32[]{:S(2)}) collective-permute-start(bf16[512,1024]{1,0:T(8,128)(2,1)S(1)} %get-tuple-element.134), channel_id=1, source_target_pairs={{16,0},{17,1},{18,2},{19,3},{20,4},{21,5},{22,6},{23,7},{24,8},{25... | collective-permute-start | bytes 3145736 | tf_op jit(solution)/shard_map/ppermute | solution.py:967
  394.4 19.6 %collective-permute-start.45 = (bf16[64,5376]{1,0:T(8,128)(2,1)S(1)}, bf16[64,5376]{1,0:T(8,128)(2,1)S(1)}, u32[]{:S(2)}, u32[]{:S(2)}) collective-permute-start(bf16[64,5376]{1,0:T(8,128)(2,1)S(1)} %get-tuple-element.142), channel_id=1, source_target_pairs={{0,4},{1,3},{4,8},{5,1},{8,12},{9,5},{12,14},{13,9},{14,10},{15,13... | collective-permute-start | bytes 2064392 | tf_op jit(solution)/shard_map/ppermute | solution.py:666
  414.4 23.9 %collective-permute-start.49 = (bf16[128,5376]{1,0:T(8,128)(2,1)S(1)}, bf16[128,5376]{1,0:T(8,128)(2,1)S(1)}, u32[]{:S(2)}, u32[]{:S(2)}) collective-permute-start(bf16[128,5376]{1,0:T(8,128)(2,1)S(1)} %ring_add.12), channel_id=1, source_target_pairs={{0,4},{1,3},{4,8},{5,1},{8,12},{9,5},{12,14},{13,9},{14,10},{15,13... | collective-permute-start | bytes 4128776 | tf_op jit(solution)/shard_map/ppermute | solution.py:666
  418.5 21.3 %collective-permute-start.48 = (bf16[128,2688]{1,0:T(8,128)(2,1)S(1)}, bf16[128,2688]{1,0:T(8,128)(2,1)S(1)}, u32[]{:S(2)}, u32[]{:S(2)}) collective-permute-start(bf16[128,2688]{1,0:T(8,128)(2,1)S(1)} %ring_add.13), channel_id=1, source_target_pairs={{0,4},{1,3},{4,8},{5,1},{8,12},{9,5},{12,14},{13,9},{14,10},{15,13... | collective-permute-start | bytes 2064392 | tf_op jit(solution)/shard_map/ppermute | solution.py:666
  427.3 31.4 %collective-permute-start.53 = (bf16[512,512]{1,0:T(8,128)(2,1)S(1)}, bf16[512,512]{1,0:T(8,128)(2,1)S(1)}, u32[]{:S(2)}, u32[]{:S(2)}) collective-permute-start(bf16[512,512]{1,0:T(8,128)(2,1)S(1)} %get-tuple-element.169), channel_id=1, source_target_pairs={{0,1},{1,0},{2,3},{3,2},{4,5},{5,4},{6,7},{7,6},{8,9},{9,8},{10,11... | collective-permute-start | bytes 1572872 | tf_op jit(solution)/shard_map/ppermute | solution.py:710
  437.8 22.2 %collective-permute-start.54 = (bf16[512,512]{1,0:T(8,128)(2,1)S(1)}, bf16[512,512]{1,0:T(8,128)(2,1)S(1)}, u32[]{:S(2)}, u32[]{:S(2)}) collective-permute-start(bf16[512,512]{1,0:T(8,128)(2,1)S(1)} %get-tuple-element.171), channel_id=1, source_target_pairs={{0,1},{1,0},{2,3},{3,2},{4,5},{5,4},{6,7},{7,6},{8,9},{9,8},{10,11... | collective-permute-start | bytes 1572872 | tf_op jit(solution)/shard_map/ppermute | solution.py:710
  438.7 28.5 %collective-permute-start.52 = (bf16[128,5376]{1,0:T(8,128)(2,1)S(1)}, bf16[128,5376]{1,0:T(8,128)(2,1)S(1)}, u32[]{:S(2)}, u32[]{:S(2)}) collective-permute-start(bf16[128,5376]{1,0:T(8,128)(2,1)S(1)} %ring_add.14), channel_id=1, source_target_pairs={{0,4},{1,3},{4,8},{5,1},{8,12},{9,5},{12,14},{13,9},{14,10},{15,13... | collective-permute-start | bytes 4128776 | tf_op jit(solution)/shard_map/ppermute | solution.py:666
  465.4 45.1 %collective-permute-start.57 = (bf16[448,3072]{1,0:T(8,128)(2,1)}, bf16[448,3072]{1,0:T(8,128)(2,1)}, u32[]{:S(2)}, u32[]{:S(2)}) collective-permute-start(bf16[448,3072]{1,0:T(8,128)(2,1)} %weight_rows.14), channel_id=1, source_target_pairs={{0,1},{1,0},{2,3},{3,2},{4,5},{5,4},{6,7},{7,6},{8,9},{9,8},{10,11... | collective-permute-start | bytes 8257544 | tf_op jit(solution)/shard_map/ppermute | solution.py:663
  482.2 22.9 %collective-permute-start.68 = (bf16[128,2688]{1,0:T(8,128)(2,1)S(1)}, bf16[128,2688]{1,0:T(8,128)(2,1)}, u32[]{:S(2)}, u32[]{:S(2)}) collective-permute-start(bf16[128,2688]{1,0:T(8,128)(2,1)S(1)} %ring_add.18), channel_id=1, source_target_pairs={{0,4},{1,3},{4,8},{5,1},{8,12},{9,5},{12,14},{13,9},{14,10},{15,13... | collective-permute-start | bytes 2064392 | tf_op jit(solution)/shard_map/ppermute | solution.py:666
  497.0 39.4 %collective-permute-start.59 = (bf16[128,1024]{1,0:T(8,128)(2,1)}, bf16[128,1024]{1,0:T(8,128)(2,1)}, u32[]{:S(2)}, u32[]{:S(2)}) collective-permute-start(bf16[128,1024]{1,0:T(8,128)(2,1)} %ring_add.19), channel_id=1, source_target_pairs={{0,4},{1,3},{4,8},{5,1},{8,12},{9,5},{12,14},{13,9},{14,10},{15,13... | collective-permute-start | bytes 786440 | tf_op jit(solution)/shard_map/ppermute | solution.py:666
  499.0 35.3 %collective-permute-start.66 = (bf16[128,5376]{1,0:T(8,128)(2,1)}, bf16[128,5376]{1,0:T(8,128)(2,1)}, u32[]{:S(2)}, u32[]{:S(2)}) collective-permute-start(bf16[128,5376]{1,0:T(8,128)(2,1)} %ring_add.17), channel_id=1, source_target_pairs={{0,4},{1,3},{4,8},{5,1},{8,12},{9,5},{12,14},{13,9},{14,10},{15,13... | collective-permute-start | bytes 4128776 | tf_op jit(solution)/shard_map/ppermute | solution.py:666
  499.1 52.8 %all-to-all-start.3 = ((bf16[8,64,1024]{2,1,0:T(8,128)(2,1)}), bf16[8,64,1024]{2,1,0:T(8,128)(2,1)}, u32[]{:S(2)}, u32[]{:S(2)}) async-start(bf16[8,64,1024]{2,1,0:T(8,128)(2,1)} %bitcast.172), calls=%async_computation.3 | async-start | bytes 2097152 | tf_op jit(solution)/shard_map/all_to_all | solution.py:683
  506.8 44.2 %collective-permute-start.69 = (bf16[64,2688]{1,0:T(8,128)(2,1)S(1)}, bf16[64,2688]{1,0:T(8,128)(2,1)S(1)}, u32[]{:S(2)}, u32[]{:S(2)}) collective-permute-start(bf16[64,2688]{1,0:T(8,128)(2,1)S(1)} %dynamic-slice_convert_fusion.2), channel_id=1, source_target_pairs={{0,1},{1,0},{2,3},{3,2},{4,5},{5,4},{6,7},{7,6},{8,9},{9,8},{10,11... | collective-permute-start | bytes 1032200 | tf_op jit(solution)/shard_map/ppermute | solution.py:663
  517.5 26.6 %collective-permute-start.58 = (bf16[64,3072]{1,0:T(8,128)(2,1)S(1)}, bf16[64,3072]{1,0:T(8,128)(2,1)S(1)}, u32[]{:S(2)}, u32[]{:S(2)}) collective-permute-start(bf16[64,3072]{1,0:T(8,128)(2,1)S(1)} %get-tuple-element.183), channel_id=1, source_target_pairs={{0,4},{1,3},{4,8},{5,1},{8,12},{9,5},{12,14},{13,9},{14,10},{15,13... | collective-permute-start | bytes 1179656 | tf_op jit(solution)/shard_map/ppermute | solution.py:666
  (121 other events, 1877.9 us)

commit v4 on v3

--- a/solution.py
+++ b/solution.py
@@ -523,43 +523,55 @@
     )(x, dh, gains, w_kv, w_mix, *grads)
 
 
-def weight_rows(order, rows, lefts, rights, other=None):
+def weight_rows(order, rows, pairs, others=None):
     count = order.shape[0]
-    tokens = lefts[0].shape[0]
-    columns = sum(r.shape[1] for r in rights)
-    flat = list(lefts) + list(rights) + ([] if other is None else [other])
-    added = 0 if other is None else other.shape[0]
-    outs = 1 if other is None else 2
+    tokens = pairs[0][0][0].shape[0]
+    widths = [sum(r.shape[1] for r in rights) for _, rights in pairs]
+    columns = sum(widths)
+    flat = [v for lefts, rights in pairs for v in list(lefts) + list(rights)]
+    flat += [] if others is None else list(others)
+    added = 0 if others is None else others[0].shape[0]
+    outs = 1 if others is None else 2
 
     def kernel(order_ref, *refs):
-        left_refs, right_refs = refs[: len(lefts)], refs[len(lefts) : len(lefts) + len(rights)]
         out_refs, (turned_ref, left_ref) = refs[len(flat) : len(flat) + outs], refs[-2:]
-        at = 0
-        for ref in left_refs:
-            turned_ref[at : at + ref.shape[1]] = ref[...].T
+        other_refs = [] if others is None else refs[len(flat) - len(others) : len(flat)]
+        spans, at = [], 0
+        for ref in other_refs:
+            spans.append((at, at + ref.shape[1], ref))
             at += ref.shape[1]
-        for n in range(count):
-            start = pl.multiple_of(order_ref[n] * rows, rows)
-            left_ref[n * rows : (n + 1) * rows] = turned_ref[pl.ds(start, rows)]
-        at = 0
-        for ref in right_refs:
-            width = ref.shape[1]
-            for begin in range(0, width, 512):
-                end = min(begin + 512, width)
-                cols = slice(at + begin, at + end)
-                term = dot(left_ref[...], ref[:, begin:end], NN)
-                if other is None:
-                    out_refs[0][:, cols] = term.astype(BF)
-                else:
-                    other_ref = refs[len(flat) - 1]
-                    near = term[:added] + other_ref[:, cols].astype(F32)
+        at = where = 0
+        for lefts, rights in pairs:
+            row = 0
+            for _ in lefts:
+                ref = refs[where]
+                turned_ref[row : row + ref.shape[1]] = ref[...].T
+                row += ref.shape[1]
+                where += 1
+            for n in range(count):
+                start = pl.multiple_of(order_ref[n] * rows, rows)
+                left_ref[n * rows : (n + 1) * rows] = turned_ref[pl.ds(start, rows)]
+            for _ in rights:
+                ref = refs[where]
+                width = ref.shape[1]
+                for begin in range(0, width, 512):
+                    end = min(begin + 512, width)
+                    cols = slice(at + begin, at + end)
+                    term = dot(left_ref[...], ref[:, begin:end], NN)
+                    if others is None:
+                        out_refs[0][:, cols] = term.astype(BF)
+                        continue
+                    low, other_ref = next((a, r) for a, b, r in spans if a <= cols.start < b)
+                    there = slice(cols.start - low, cols.stop - low)
+                    near = term[:added] + other_ref[:, there].astype(F32)
                     out_refs[0][:, cols] = near[:rows].astype(BF)
                     out_refs[1][: added - rows, cols] = near[rows:].astype(BF)
                     out_refs[1][added - rows :, cols] = term[added:].astype(BF)
-            at += width
+                at += width
+                where += 1
 
     shapes = [shaped((count * rows, columns))]
-    if other is not None:
+    if others is not None:
         shapes = [shaped((rows, columns)), shaped(((count - 1) * rows, columns))]
     size = 2 * (count * rows * columns + sum(v.size for v in flat))
     return call(
@@ -679,8 +691,10 @@
     def along(self, parts):
         return lax.all_to_all(parts, "ctx", 0, 0, tiled=True).reshape(self.rows, D)
 
-    def from_sequences(self, rows):
-        parts = lax.all_to_all(rows.reshape(self.n_ctx, self.r, D), "ctx", 0, 0, tiled=True)
+    def back_along(self, rows):
+        return lax.all_to_all(rows.reshape(self.n_ctx, self.r, D), "ctx", 0, 0, tiled=True)
+
+    def back_across(self, parts):
         parts = parts.reshape(self.micro, self.nw, self.g, self.r, D).transpose(1, 0, 2, 3, 4)
         parts = lax.all_to_all(parts, "wshard", 0, 0, tiled=True)
         return parts.transpose(1, 2, 0, 3, 4).reshape(self.micro, self.tok_rows, D)
@@ -748,21 +762,24 @@
 
 
 class Reduce:
-    def __init__(self, plan, clock, lefts, rights):
+    def __init__(self, plan, clock):
         self.plan, self.clock = plan, clock
-        self.lefts, self.rights = list(lefts), list(rights)
+        self.pairs, self.others = [], []
         self.k = plan.half
 
-    def theirs(self):
+    def theirs(self, *pairs):
         plan = self.plan
-        lefts = [self.clock.tie(self.lefts[0])] + self.lefts[1:]
-        (term,) = weight_rows(plan.theirs, plan.wrows, lefts, self.rights)
-        self.other = plan.swap(self.clock.mark(term))
+        lefts, rights = pairs[0]
+        tied = [([self.clock.tie(lefts[0])] + list(lefts[1:]), rights)] + list(pairs[1:])
+        (term,) = weight_rows(plan.theirs, plan.wrows, tied)
+        self.others.append(plan.swap(self.clock.mark(term)))
+        self.pairs += list(pairs)
 
     def mine(self):
         plan = self.plan
-        lefts = [self.clock.tie(self.lefts[0])] + self.lefts[1:]
-        term, self.own = weight_rows(plan.mine, plan.wrows, lefts, self.rights, self.other)
+        lefts, rights = self.pairs[0]
+        tied = [([self.clock.tie(lefts[0])] + list(lefts[1:]), rights)] + self.pairs[1:]
+        term, self.own = weight_rows(plan.mine, plan.wrows, tied, self.others)
         self.moving = plan.step(self.clock.mark(term))
         self.k -= 1
 
@@ -836,12 +853,15 @@
     own = plan.along(after(parts, *got))
     got = [get.advance() for get in (get_wide, get_in)]
     ids = after(segment_ids[:, 0], *got)
-    for _ in range(plan.half - 2):
-        got = [get.advance() for get in (get_wide, get_in)]
+    for n in range(plan.half - 2):
+        got = get_wide.advance(), get_in.advance(*([own] if n == plan.half - 3 else []))
+        if n == 0:
+            got_first = got
+    got_gate, got_back = get_gate.advance(got[1]), get_back.advance(got[0])
 
     ids = plan.in_order(ids[None], plan.swap(ids[None])).transpose(1, 0, 2)
     ids = jnp.repeat(ids.reshape(plan.micro * plan.nw, plan.tok_rows), plan.g, axis=0)
-    line = lax.all_to_all(ids, "ctx", 0, 0, tiled=True).reshape(-1)
+    line = after(lax.all_to_all(ids, "ctx", 0, 0, tiled=True).reshape(-1), *got_first)
     grid = line.reshape(plan.n_ctx, plan.members, plan.r)
     place = (plan.i % plan.g) * plan.nw + plan.w
     seg_pieces = [
@@ -873,15 +893,14 @@
         kv_list = plan.gather_rows(kv)
         return a, kv_list, queries_of(a, w_mix, cos_rows, sin_rows)
 
-    got = get_gate.advance(*got), get_back.advance(*got)
-    _, kv_list, q = first_half(own)
-    half = PAIRS // 2
-    o_first, _ = attend(after(q, *got), kv_list, qmarks, kmarks, 0, half)
-    got = get_gate.advance(late=(o_first,)), get_back.advance(late=(o_first,))
-    o_last, _ = attend(after(q, *got), kv_list, qmarks, kmarks, half, half)
-    while get_gate.k < plan.half:
-        got = get_gate.advance(late=(o_last,)), get_back.advance(late=(o_last,))
-    h, b = project(own, [o_first, o_last], gains, w_mix)
+    _, kv_list, q = first_half(after(own, got_gate))
+    got_gate = get_gate.advance()
+    o, _ = attend(after(q, got_back, got_gate), kv_list, qmarks, kmarks, 0, PAIRS)
+    got = get_back.advance(late=(o,)), get_gate.advance(late=(o,))
+    h, b = project(own, [after(o, *got)], gains, w_mix)
+    for one in (get_gate, get_back):
+        while one.k < plan.half:
+            one.advance()
     w_gate, w_back = get_gate.result(), get_back.result()
     (z,) = ffn_in(b, w_in, w_gate, False)
     first_out = ffn_out(h, z, w_back)
@@ -903,23 +922,21 @@
         dkv = keys_back(plan.scatter_rows(terms), cos_rows, sin_rows)
         return input_back(x, dh, [dq], [dkv], gains, w_kv, w_mix)[0]
 
-    def last_backward(stash, grad):
+    def last_backward(stash, grad, choose):
         x, a, q, kv_list, o, lse, h, b, z, act, slope = stash
         clock = Clock()
-        back = Reduce(plan, clock, [grad], [z])
+        back, grow, out, mixed = (Reduce(plan, clock) for _ in range(4))
         da, dg = ffn_back(clock.tie(grad), act, slope, w_back)
         clock.mark(da)
-        grow = Reduce(plan, clock, [b], [da, dg])
-        grow.theirs()
-        back.theirs()
+        grow.theirs(([b], [da, dg]))
+        back.theirs(([grad], [z]))
         grow.mine()
         back.mine()
         dh, dh_low, gain_second = hidden_back(clock.tie(grad), da, dg, h, gains, w_in, w_gate)
         clock.mark(dh)
         grow.advance()
         back.advance()
-        out = Reduce(plan, clock, [o], [dh_low])
-        out.theirs()
+        out.theirs(([o], [dh_low]))
         parts = []
         count = PAIRS // 4
         for n in range(4):
@@ -946,21 +963,27 @@
                     one.advance()
         dkv_list = [keys_back(terms, cos_rows, sin_rows) for _, terms in parts]
         dq_list = [dq for dq, _ in parts]
-        mixed = Reduce(plan, clock, [a], dkv_list + dq_list)
-        mixed.theirs()
+        mixed.theirs(([a], dkv_list + dq_list))
         for one in (grow, back, out):
             one.advance()
         dx, gain_first = input_back(clock.tie(x), dh, dq_list, dkv_list, gains, w_kv, w_mix)
         clock.mark(dx)
         mixed.mine()
+        mixed.moving = after(mixed.moving, grow.moving, back.moving)
+        mixed.advance()
+        sent = plan.back_along(after(choose(dx), clock.last))
+        gain = jnp.concatenate([gain_first, gain_second], axis=0)
+        gain = plan.total(after(gain, clock.last))
+        for one in (grow, back, out):
+            while one.k:
+                one.advance()
         while mixed.k:
-            for one in (grow, back, out, mixed):
-                if one.k:
-                    one.advance()
-        gain = plan.total(jnp.concatenate([gain_first, gain_second], axis=0))
+            if mixed.k == 1:
+                mixed.moving = after(mixed.moving, sent)
+            mixed.advance()
         start = (plan.i * plan.nw + plan.w) * plan.wrows
         gain = lax.dynamic_slice_in_dim(gain, start, plan.wrows, 1)
-        return dx, [back.result(), grow.result(), out.result(), mixed.result(), gain]
+        return sent, [back.result(), grow.result(), out.result(), mixed.result(), gain]
 
     def handed(array, by):
         pairs = [(s, s + by) for s in range(sections) if 0 <= s + by < sections]
@@ -970,14 +993,16 @@
     out, stash = forward(x_in)
     first_dx = backward(stash, own)
     grad_in = jnp.where(section == sections - 1, own, after(handed(first_dx, -1), out))
-    dx, (g_back, g_in, g_attn, g_mix, g_gain) = last_backward(stash, grad_in)
-    boundary_local = plan.from_sequences(jnp.where(section == 0, dx, out))
+    sent, (g_back, g_grow, g_attn, g_mix, g_gain) = last_backward(
+        stash, grad_in, lambda dx: jnp.where(section == 0, dx, out)
+    )
+    boundary_local = plan.back_across(sent)
     g_key, g_value = apart(g_mix[:, : 2 * D])
     return (
         boundary_local[None, :, None],
         jnp.concatenate([g_mix[:, 2 * D :], g_key, g_value], axis=1)[None],
         g_attn[None],
-        jnp.concatenate([g_in[:, :FF], g_in[:, FFP : FFP + FF]], axis=1)[None],
+        jnp.concatenate([g_grow[:, :FF], g_grow[:, FFP : FFP + FF]], axis=1)[None],
         g_back[:, :FF].T[None],
         g_gain[None],
     )

time: 604 us -> 597 us (0.988)
  starting transfers between devices: 96.5 us -> 85.5 us
    ppermute x32, waiting for transfers between devices: 93.2 us -> 108 us  [step(): return lax.ppermute(array, BOTH, self.ring_pairs)]
    ppermute x4, starting transfers between devices: 9.11 us -> 2.19 us  [total(): value = value + lax.ppermute(value, BOTH, pairs)]
    unnamed x157 -> x189, local copies, waits for them, and re-layouts: 20.2 us -> 27 us
    pallas_call x3 -> x2, Pallas kernels: 35.6 us -> 35 us  [attend(): call(kernel, 'attend', flops=8 * rows * keys * count * LANES, moved=2 * (...]
  transfers between devices with their start and end apart: 77 -> 77, of which waited for: 25 -> 20; matrix products, arithmetic and copies ran while one was open for 10% -> 10% of each run, Pallas kernels for 23% -> 23%
where the time goes in v4:
time: 597 us; the launch traced here: 587 us
  Pallas kernels  246 us (41%)
  waiting for transfers between devices  155 us (26%)
  starting transfers between devices  85.5 us (14%)
  local copies, waits for them, and re-layouts  59.3 us (10%)
  other arithmetic  30.5 us (5%)
  blocking collectives  8.43 us (1%)
    ppermute x32, waiting for transfers between devices, step(): return lax.ppermute(array, BOTH, self.ring_pairs)  108 us
    pallas_call x5, Pallas kernels, attend_back(): call(kernel, 'attend_back', flops=20 * rows * keys * count * LANES, moved...  60.8 us
    ppermute x2, waiting for transfers between devices, handed(): return lax.ppermute(array, 'section', pairs)  36.6 us
    pallas_call x2, Pallas kernels, attend(): call(kernel, 'attend', flops=8 * rows * keys * count * LANES, moved=2 * (...  35 us
    pallas_call x8, Pallas kernels, weight_rows(): call(kernel, 'weight_rows', limit=max(8, 4 + int(1.25 * size) // (1024 *...  32.9 us
    ppermute x32, starting transfers between devices, step(): return lax.ppermute(array, BOTH, self.ring_pairs)  32.6 us
    unnamed x189, local copies, waits for them, and re-layouts  27 us
    ppermute x29, starting transfers between devices, swap(): return lax.ppermute(array, 'wshard', [(0, 1), (1, 0)])  24.5 us
  transfers between devices with their start and end apart: 77, of which 20 were waited for; matrix products, arithmetic and copies ran while one was open for 10% of the time, Pallas kernels for 23%

profile of v4, /device:TPU:13, one launch (start us, length us, event | category | flops | bytes accessed | tf_op | source)
XLA Modules:
  0.0 587.4 jit_solution(15608161790011923049)
XLA Ops:
  24.5 7.6 %collective-permute-done.2 = bf16[128,4224]{1,0:T(8,128)(2,1)} collective-permute-done((bf16[128,4224]{1,0:T(8,128)(2,1)S(1)}, bf16[128,4224]{1,0:T(8,128)(2,1)}, u32[]{:S(2)}, u32[]{:S(2)}) %collective-permute-start.2) | collective-permute-done | bytes 1081376 | tf_op jit(solution)/shard_map/ppermute | solution.py:678
  32.0 5.7 all-to-all-start.1
  51.5 28.4 %collective-permute-done.13 = bf16[128,2688]{1,0:T(8,128)(2,1)S(1)} collective-permute-done((bf16[128,2688]{1,0:T(8,128)(2,1)S(1)}, bf16[128,2688]{1,0:T(8,128)(2,1)S(1)}, u32[]{:S(2)}, u32[]{:S(2)}) %collective-permute-start.13) | collective-permute-done | bytes 688160 | tf_op jit(solution)/shard_map/ppermute | solution.py:678
  111.9 5.3 collective-permute-done.15
  124.9 6.3 %keys_values.2 = (bf16[512,1024]{1,0:T(8,128)(2,1)S(1)}, bf16[512,2048]{1,0:T(8,128)(2,1)S(1)}) custom-call(bf16[512,1024]{1,0:T(8,128)(2,1)S(1)} %bitcast.168, f32[8,1024]{1,0:T(8,128)S(1)} %gains.1.gain_ref, bf16[1024,4224]{1,0:T(8,128)(2,1)} %bitcast.19.w_ref.wkv_ref.wq_ref, f32[512,128]{1,0:T(8,128)S(1)} %get-tuple-element.254.cos_ref, ...), custom_call_target="tpu_custom_call" | custom-call | flops 2147483648 | bytes 8388608 | tf_op jit(solution)/shard_map/keys_values/pallas_call | solution.py:129
  140.9 17.8 %attend.2 = (bf16[512,1024]{1,0:T(8,128)(2,1)S(1)}, f32[8,2,512]{2,1,0:T(2,128)}) custom-call(bf16[512,1024]{1,0:T(8,128)(2,1)S(1)} %queries.2.q_ref, bf16[512,128]{1,0:T(8,128)(2,1)S(1)} %select_convert_fusion.1.qm_ref, bf16[1024,128]{1,0:T(8,128)(2,1)S(1)} %select_convert_fusion.km_ref, bf16[512,2048]{1,0:T(8,128)(2,1)S(1)} %get-tuple-element.112.refs_0_, ...), custom_call_target="tpu_custom_call" | custom-call | flops 4294967296 | bytes 6291456 | tf_op jit(solution)/shard_map/attend/pallas_call | solution.py:212
  164.5 8.7 %collective-permute-done.30 = bf16[64,2688]{1,0:T(8,128)(2,1)S(1)} collective-permute-done((bf16[64,2688]{1,0:T(8,128)(2,1)S(1)}, bf16[64,2688]{1,0:T(8,128)(2,1)S(1)}, u32[]{:S(2)}, u32[]{:S(2)}) %collective-permute-start.30) | collective-permute-done | bytes 344096 | tf_op jit(solution)/shard_map/ppermute | solution.py:678
  181.7 8.9 %ffn_in.2.z_ref = bf16[512,2688]{1,0:T(8,128)(2,1)S(1)} custom-call(bf16[512,1024]{1,0:T(8,128)(2,1)S(1)} %get-tuple-element.118.b_ref, bf16[1024,2688]{1,0:T(8,128)(2,1)} %bitcast.36.wa_ref, bf16[1024,2688]{1,0:T(8,128)(2,1)S(1)} %bitcast.174), custom_call_target="tpu_custom_call" | custom-call | flops 5637144576 | bytes 14811136 | tf_op jit(solution)/shard_map/ffn_in/pallas_call | solution.py:288
  199.5 21.2 %collective-permute-done.38 = bf16[512,1024]{1,0:T(8,128)(2,1)} collective-permute-done((bf16[512,1024]{1,0:T(8,128)(2,1)S(1)}, bf16[512,1024]{1,0:T(8,128)(2,1)}, u32[]{:S(2)}, u32[]{:S(2)}) %collective-permute-start.38) | collective-permute-done | bytes 1048608 | tf_op jit(solution)/shard_map/ppermute | solution.py:990
  220.9 6.4 %keys_values.3 = (bf16[512,1024]{1,0:T(8,128)(2,1)S(1)}, bf16[512,2048]{1,0:T(8,128)(2,1)S(1)}) custom-call(bf16[512,1024]{1,0:T(8,128)(2,1)S(1)} %broadcast_select_fusion.2.x_ref, f32[8,1024]{1,0:T(8,128)S(1)} %gains.1.gain_ref, bf16[1024,4224]{1,0:T(8,128)(2,1)} %bitcast.19.w_ref.wkv_ref.wq_ref, f32[512,128]{1,0:T(8,128)S(1)} %get-tuple-element.254.cos_ref, ...), custom_call_target="tpu_custom_call" | custom-call | flops 2147483648 | bytes 8388608 | tf_op jit(solution)/shard_map/keys_values/pallas_call | solution.py:129
  232.3 17.2 %attend.3 = (bf16[512,1024]{1,0:T(8,128)(2,1)S(1)}, f32[8,2,512]{2,1,0:T(2,128)S(1)}) custom-call(bf16[512,1024]{1,0:T(8,128)(2,1)S(1)} %queries.3.q_ref, bf16[512,128]{1,0:T(8,128)(2,1)S(1)} %select_convert_fusion.1.qm_ref, bf16[1024,128]{1,0:T(8,128)(2,1)S(1)} %select_convert_fusion.km_ref, bf16[512,2048]{1,0:T(8,128)(2,1)S(1)} %get-tuple-element.120.refs_0_, ...), custom_call_target="tpu_custom_call" | custom-call | flops 4294967296 | bytes 6291456 | tf_op jit(solution)/shard_map/attend/pallas_call | solution.py:212
  253.2 10.5 %ffn_in.3 = (bf16[512,2688]{1,0:T(8,128)(2,1)S(1)}, bf16[512,2688]{1,0:T(8,128)(2,1)S(1)}, bf16[512,2688]{1,0:T(8,128)(2,1)S(1)}) custom-call(bf16[512,1024]{1,0:T(8,128)(2,1)S(1)} %get-tuple-element.141.b_ref.refs_0_, bf16[1024,2688]{1,0:T(8,128)(2,1)} %bitcast.36.wa_ref, bf16[1024,2688]{1,0:T(8,128)(2,1)S(1)} %bitcast.177), custom_call_target="tpu_custom_call" | custom-call | flops 5637144576 | bytes 20316160 | tf_op jit(solution)/shard_map/ffn_in/pallas_call | solution.py:288
  265.3 5.3 ffn_back.2
  270.7 10.1 %hidden_back.2 = (f32[512,1024]{1,0:T(8,128)S(1)}, bf16[512,1024]{1,0:T(8,128)(2,1)S(1)}, f32[1,1024]{1,0:T(1,128)}) custom-call(bf16[512,1024]{1,0:T(8,128)(2,1)S(1)} %bitcast.171, bf16[512,2688]{1,0:T(8,128)(2,1)S(1)} %get-tuple-element.125.da_ref, bf16[512,2688]{1,0:T(8,128)(2,1)S(1)} %get-tuple-element.126.dg_ref, ...), custom_call_target="tpu_custom_call" | custom-call | flops 5637144576 | bytes 22806528 | tf_op jit(solution)/shard_map/hidden_back/pallas_call | solution.py:362
  280.8 29.5 %attend_back.5 = (bf16[512,1024]{1,0:T(8,128)(2,1)S(1)}, bf16[512,2048]{1,0:T(8,128)(2,1)S(1)}, bf16[512,2048]{1,0:T(8,128)(2,1)S(1)}) custom-call(bf16[512,1024]{1,0:T(8,128)(2,1)S(1)} %queries.3.q_ref, bf16[512,1024]{1,0:T(8,128)(2,1)S(1)} %get-tuple-element.129.dh_ref, bf16[1024,4224]{1,0:T(8,128)(2,1)} %bitcast.19.w_ref.wkv_ref.wq_ref, ...), custom_call_target="tpu_custom_call" | custom-call | flops 10737418240 | bytes 14680064 | tf_op jit(solution)/shard_map/attend_back/pallas_call | solution.py:430
  317.0 8.0 %input_back.2 = (bf16[512,1024]{1,0:T(8,128)(2,1)S(1)}, f32[1,1024]{1,0:T(1,128)}) custom-call(bf16[512,1024]{1,0:T(8,128)(2,1)S(1)} %broadcast_select_fusion.2.x_ref, f32[512,1024]{1,0:T(8,128)S(1)} %get-tuple-element.128.dh_ref, f32[8,1024]{1,0:T(8,128)S(1)} %gains.1.gain_ref, bf16[1024,4224]{1,0:T(8,128)(2,1)} %bitcast.19.w_ref.wkv_ref.wq_ref, ...), custom_call_target="tpu_custom_call" | custom-call | flops 3221225472 | bytes 16777216 | tf_op jit(solution)/shard_map/input_back/pallas_call | solution.py:506
  337.6 15.4 %collective-permute-done.41 = bf16[512,1024]{1,0:T(8,128)(2,1)} collective-permute-done((bf16[512,1024]{1,0:T(8,128)(2,1)S(1)}, bf16[512,1024]{1,0:T(8,128)(2,1)}, u32[]{:S(2)}, u32[]{:S(2)}) %collective-permute-start.41) | collective-permute-done | bytes 1048608 | tf_op jit(solution)/shard_map/ppermute | solution.py:990
  354.4 5.3 ffn_back.3
  359.8 5.8 weight_rows.8
  377.5 6.4 %weight_rows.10 = (bf16[64,5376]{1,0:T(8,128)(2,1)S(1)}, bf16[512,5376]{1,0:T(8,128)(2,1)S(1)}) custom-call(s32[9]{0:T(128)S(1)} %stack.67.order_ref, bf16[512,1024]{1,0:T(8,128)(2,1)S(1)} %copy-done.69, bf16[512,2688]{1,0:T(8,128)(2,1)S(1)} %get-tuple-element.137.refs_1_.da_ref, bf16[512,2688]{1,0:T(8,128)(2,1)S(1)} %copy-done.49, ...), custom_call_target="tpu_custom_call" | custom-call | flops 3170893824 | bytes 17563648 | tf_op jit(solution)/shard_map/weight_rows/pallas_call | solution.py:577
  384.1 5.9 %weight_rows.11 = (bf16[64,2688]{1,0:T(8,128)(2,1)S(1)}, bf16[512,2688]{1,0:T(8,128)(2,1)S(1)}) custom-call(s32[9]{0:T(128)S(1)} %stack.67.order_ref, bf16[512,1024]{1,0:T(8,128)(2,1)S(1)} %copy-done.18, bf16[512,2688]{1,0:T(8,128)(2,1)S(1)} %copy-done.16, bf16[448,2688]{1,0:T(8,128)(2,1)} %collective-permute-done.43.refs_2_), custom_call_target="tpu_custom_call" | custom-call | flops 1585446912 | bytes 9306112 | tf_op jit(solution)/shard_map/weight_rows/pallas_call | solution.py:577
  393.6 9.9 %hidden_back.3 = (f32[512,1024]{1,0:T(8,128)S(1)}, bf16[512,1024]{1,0:T(8,128)(2,1)S(1)}, f32[1,1024]{1,0:T(1,128)S(1)}) custom-call(bf16[512,1024]{1,0:T(8,128)(2,1)S(1)} %copy-done.18, bf16[512,2688]{1,0:T(8,128)(2,1)S(1)} %copy-done.47, bf16[512,2688]{1,0:T(8,128)(2,1)S(1)} %copy-done.50, f32[512,1024]{1,0:T(8,128)S(1)} %copy-done.63, ...), custom_call_target="tpu_custom_call" | custom-call | flops 5637144576 | bytes 22806528 | tf_op jit(solution)/shard_map/hidden_back/pallas_call | solution.py:362
  409.6 7.8 %attend_back.6 = (bf16[512,256]{1,0:T(8,128)(2,1)S(1)}, bf16[512,512]{1,0:T(8,128)(2,1)S(1)}, bf16[512,512]{1,0:T(8,128)(2,1)S(1)}) custom-call(bf16[512,1024]{1,0:T(8,128)(2,1)S(1)} %copy-done.12, bf16[512,1024]{1,0:T(8,128)(2,1)S(1)} %get-tuple-element.152.refs_1_.dh_ref, bf16[1024,4224]{1,0:T(8,128)(2,1)} %bitcast.19.w_ref.wkv_ref.wq_ref, ...), custom_call_target="tpu_custom_call" | custom-call | flops 2684354560 | bytes 3670016 | tf_op jit(solution)/shard_map/attend_back/pallas_call | solution.py:430
  420.1 8.0 %attend_back.7 = (bf16[512,256]{1,0:T(8,128)(2,1)S(1)}, bf16[512,512]{1,0:T(8,128)(2,1)S(1)}, bf16[512,512]{1,0:T(8,128)(2,1)S(1)}) custom-call(bf16[512,1024]{1,0:T(8,128)(2,1)S(1)} %copy-done.12, bf16[512,1024]{1,0:T(8,128)(2,1)S(1)} %get-tuple-element.152.refs_1_.dh_ref, bf16[1024,4224]{1,0:T(8,128)(2,1)} %bitcast.19.w_ref.wkv_ref.wq_ref, ...), custom_call_target="tpu_custom_call" | custom-call | flops 2684354560 | bytes 3670016 | tf_op jit(solution)/shard_map/attend_back/pallas_call | solution.py:430
  431.9 7.8 %attend_back.8 = (bf16[512,256]{1,0:T(8,128)(2,1)S(1)}, bf16[512,512]{1,0:T(8,128)(2,1)S(1)}, bf16[512,512]{1,0:T(8,128)(2,1)S(1)}) custom-call(bf16[512,1024]{1,0:T(8,128)(2,1)S(1)} %copy-done.12, bf16[512,1024]{1,0:T(8,128)(2,1)S(1)} %get-tuple-element.152.refs_1_.dh_ref, bf16[1024,4224]{1,0:T(8,128)(2,1)} %bitcast.19.w_ref.wkv_ref.wq_ref, ...), custom_call_target="tpu_custom_call" | custom-call | flops 2684354560 | bytes 3670016 | tf_op jit(solution)/shard_map/attend_back/pallas_call | solution.py:430
  441.4 7.8 %attend_back.9 = (bf16[512,256]{1,0:T(8,128)(2,1)S(1)}, bf16[512,512]{1,0:T(8,128)(2,1)S(1)}, bf16[512,512]{1,0:T(8,128)(2,1)S(1)}) custom-call(bf16[512,1024]{1,0:T(8,128)(2,1)S(1)} %copy-done.12, bf16[512,1024]{1,0:T(8,128)(2,1)S(1)} %get-tuple-element.152.refs_1_.dh_ref, bf16[1024,4224]{1,0:T(8,128)(2,1)} %bitcast.19.w_ref.wkv_ref.wq_ref, ...), custom_call_target="tpu_custom_call" | custom-call | flops 2684354560 | bytes 3670016 | tf_op jit(solution)/shard_map/attend_back/pallas_call | solution.py:430
  458.7 8.6 %collective-permute-done.52.moving_ref = bf16[128,5376]{1,0:T(8,128)(2,1)} collective-permute-done((bf16[128,5376]{1,0:T(8,128)(2,1)}, bf16[128,5376]{1,0:T(8,128)(2,1)}, u32[]{:S(2)}, u32[]{:S(2)}) %collective-permute-start.52) | collective-permute-done | bytes 1376288 | tf_op jit(solution)/shard_map/ppermute | solution.py:678
  480.2 7.4 %input_back.3 = (bf16[512,1024]{1,0:T(8,128)(2,1)S(1)}, f32[1,1024]{1,0:T(1,128)S(1)}) custom-call(bf16[512,1024]{1,0:T(8,128)(2,1)S(1)} %copy-done.10, f32[512,1024]{1,0:T(8,128)S(1)} %copy-done.60, f32[8,1024]{1,0:T(8,128)S(1)} %copy-done.66, bf16[1024,4224]{1,0:T(8,128)(2,1)} %bitcast.19.w_ref.wkv_ref.wq_ref, ...), custom_call_target="tpu_custom_call" | custom-call | flops 3221225472 | bytes 16777216 | tf_op jit(solution)/shard_map/input_back/pallas_call | solution.py:506
  489.4 10.2 %collective-permute-done.60 = bf16[128,2688]{1,0:T(8,128)(2,1)S(1)} collective-permute-done((bf16[128,2688]{1,0:T(8,128)(2,1)S(1)}, bf16[128,2688]{1,0:T(8,128)(2,1)S(1)}, u32[]{:S(2)}, u32[]{:S(2)}) %collective-permute-start.60) | collective-permute-done | bytes 688160 | tf_op jit(solution)/shard_map/ppermute | solution.py:678
  518.9 5.6 all-to-all-start.3
  539.2 17.9 %collective-permute-done.63.moving_ref = bf16[128,3072]{1,0:T(8,128)(2,1)S(1)} collective-permute-done((bf16[128,3072]{1,0:T(8,128)(2,1)S(1)}, bf16[128,3072]{1,0:T(8,128)(2,1)S(1)}, u32[]{:S(2)}, u32[]{:S(2)}) %collective-permute-start.63) | collective-permute-done | bytes 786464 | tf_op jit(solution)/shard_map/ppermute | solution.py:678
  564.8 5.8 collective-permute-done.64
  (481 shorter events, 252.1 us)
Async XLA Ops:
  13.9 18.2 %collective-permute-start.2 = (bf16[128,4224]{1,0:T(8,128)(2,1)S(1)}, bf16[128,4224]{1,0:T(8,128)(2,1)}, u32[]{:S(2)}, u32[]{:S(2)}) collective-permute-start(bf16[128,4224]{1,0:T(8,128)(2,1)S(1)} %pad_maximum_fusion), channel_id=1, source_target_pairs={{0,4},{1,3},{4,8},{5,1},{8,12},{9,5},{12,14},{13,9},{14,10},{15,13... | collective-permute-start | bytes 3244040 | tf_op jit(solution)/shard_map/ppermute | solution.py:678
  21.6 20.9 %collective-permute-start.12 = (bf16[128,2688]{1,0:T(8,128)(2,1)}, bf16[128,2688]{1,0:T(8,128)(2,1)S(1)}, u32[]{:S(2)}, u32[]{:S(2)}) collective-permute-start(bf16[128,2688]{1,0:T(8,128)(2,1)} %collective-permute-done.3), channel_id=1, source_target_pairs={{0,4},{1,3},{4,8},{5,1},{8,12},{9,5},{12,14},{13,9},{14,10},{15,13... | collective-permute-start | bytes 2064392 | tf_op jit(solution)/shard_map/ppermute | solution.py:678
  21.9 21.7 %collective-permute-start.23 = (bf16[128,2688]{1,0:T(8,128)(2,1)}, bf16[128,2688]{1,0:T(8,128)(2,1)}, u32[]{:S(2)}, u32[]{:S(2)}) collective-permute-start(bf16[128,2688]{1,0:T(8,128)(2,1)} %collective-permute-done.3), channel_id=1, source_target_pairs={{0,1},{1,0},{2,3},{3,2},{4,5},{5,4},{6,7},{7,6},{8,9},{9,8},{10,11... | collective-permute-start | bytes 2064392 | tf_op jit(solution)/shard_map/ppermute | solution.py:675
  32.0 57.5 %all-to-all-start.1 = ((bf16[8,64,1024]{2,1,0:T(8,128)(2,1)}), bf16[8,64,1024]{2,1,0:T(8,128)(2,1)S(1)}, u32[]{:S(2)}, u32[]{:S(2)}) async-start(bf16[8,64,1024]{2,1,0:T(8,128)(2,1)} %bitcast.9), calls=%async_computation.1 | async-start | bytes 2097152 | tf_op jit(solution)/shard_map/all_to_all | solution.py:692
  39.6 45.0 %collective-permute-start.4 = (bf16[128,4224]{1,0:T(8,128)(2,1)}, bf16[128,4224]{1,0:T(8,128)(2,1)S(1)}, u32[]{:S(2)}, u32[]{:S(2)}) collective-permute-start(bf16[128,4224]{1,0:T(8,128)(2,1)} %collective-permute-done.2), channel_id=1, source_target_pairs={{0,1},{1,0},{2,3},{3,2},{4,5},{5,4},{6,7},{7,6},{8,9},{9,8},{10,11... | collective-permute-start | bytes 3244040 | tf_op jit(solution)/shard_map/ppermute | solution.py:675
  42.4 41.6 %collective-permute-start.5 = (bf16[128,4224]{1,0:T(8,128)(2,1)}, bf16[128,4224]{1,0:T(8,128)(2,1)}, u32[]{:S(2)}, u32[]{:S(2)}) collective-permute-start(bf16[128,4224]{1,0:T(8,128)(2,1)} %collective-permute-done.2), channel_id=1, source_target_pairs={{0,4},{1,3},{4,8},{5,1},{8,12},{9,5},{12,14},{13,9},{14,10},{15,13... | collective-permute-start | bytes 3244040 | tf_op jit(solution)/shard_map/ppermute | solution.py:678
  43.6 36.3 %collective-permute-start.13 = (bf16[128,2688]{1,0:T(8,128)(2,1)S(1)}, bf16[128,2688]{1,0:T(8,128)(2,1)S(1)}, u32[]{:S(2)}, u32[]{:S(2)}) collective-permute-start(bf16[128,2688]{1,0:T(8,128)(2,1)S(1)} %collective-permute-done.12), channel_id=1, source_target_pairs={{0,4},{1,3},{4,8},{5,1},{8,12},{9,5},{12,14},{13,9},{14,10},{15,13... | collective-permute-start | bytes 2064392 | tf_op jit(solution)/shard_map/ppermute | solution.py:678
  47.8 34.4 %collective-permute-start.24 = (bf16[128,2688]{1,0:T(8,128)(2,1)S(1)}, bf16[128,2688]{1,0:T(8,128)(2,1)S(1)}, u32[]{:S(2)}, u32[]{:S(2)}) collective-permute-start(bf16[128,2688]{1,0:T(8,128)(2,1)S(1)} %collective-permute-done.12), channel_id=1, source_target_pairs={{0,1},{1,0},{2,3},{3,2},{4,5},{5,4},{6,7},{7,6},{8,9},{9,8},{10,11... | collective-permute-start | bytes 2064392 | tf_op jit(solution)/shard_map/ppermute | solution.py:675
  110.8 24.3 %collective-permute-start.18 = (bf16[128,2688]{1,0:T(8,128)(2,1)}, bf16[128,2688]{1,0:T(8,128)(2,1)S(1)}, u32[]{:S(2)}, u32[]{:S(2)}) collective-permute-start(bf16[128,2688]{1,0:T(8,128)(2,1)} %pad_maximum_fusion.3), channel_id=1, source_target_pairs={{0,4},{1,3},{4,8},{5,1},{8,12},{9,5},{12,14},{13,9},{14,10},{15,13... | collective-permute-start | bytes 2064392 | tf_op jit(solution)/shard_map/ppermute | solution.py:678
  117.3 19.9 %collective-permute-start.19 = (bf16[128,2688]{1,0:T(8,128)(2,1)S(1)}, bf16[128,2688]{1,0:T(8,128)(2,1)S(1)}, u32[]{:S(2)}, u32[]{:S(2)}) collective-permute-start(bf16[128,2688]{1,0:T(8,128)(2,1)S(1)} %collective-permute-done.15), channel_id=1, source_target_pairs={{0,4},{1,3},{4,8},{5,1},{8,12},{9,5},{12,14},{13,9},{14,10},{15,13... | collective-permute-start | bytes 2064392 | tf_op jit(solution)/shard_map/ppermute | solution.py:678
  119.1 19.1 %collective-permute-start.27 = (bf16[128,2688]{1,0:T(8,128)(2,1)S(1)}, bf16[128,2688]{1,0:T(8,128)(2,1)S(1)}, u32[]{:S(2)}, u32[]{:S(2)}) collective-permute-start(bf16[128,2688]{1,0:T(8,128)(2,1)S(1)} %collective-permute-done.15), channel_id=1, source_target_pairs={{0,1},{1,0},{2,3},{3,2},{4,5},{5,4},{6,7},{7,6},{8,9},{9,8},{10,11... | collective-permute-start | bytes 2064392 | tf_op jit(solution)/shard_map/ppermute | solution.py:675
  135.1 24.0 %collective-permute-start.21 = (bf16[128,2688]{1,0:T(8,128)(2,1)S(1)}, bf16[128,2688]{1,0:T(8,128)(2,1)S(1)}, u32[]{:S(2)}, u32[]{:S(2)}) collective-permute-start(bf16[128,2688]{1,0:T(8,128)(2,1)S(1)} %collective-permute-done.18), channel_id=1, source_target_pairs={{0,4},{1,3},{4,8},{5,1},{8,12},{9,5},{12,14},{13,9},{14,10},{15,13... | collective-permute-start | bytes 2064392 | tf_op jit(solution)/shard_map/ppermute | solution.py:678
  137.2 21.5 %collective-permute-start.22 = (bf16[128,2688]{1,0:T(8,128)(2,1)S(1)}, bf16[128,2688]{1,0:T(8,128)(2,1)S(1)}, u32[]{:S(2)}, u32[]{:S(2)}) collective-permute-start(bf16[128,2688]{1,0:T(8,128)(2,1)S(1)} %collective-permute-done.19), channel_id=1, source_target_pairs={{0,4},{1,3},{4,8},{5,1},{8,12},{9,5},{12,14},{13,9},{14,10},{15,13... | collective-permute-start | bytes 2064392 | tf_op jit(solution)/shard_map/ppermute | solution.py:678
  195.0 25.7 %collective-permute-start.38 = (bf16[512,1024]{1,0:T(8,128)(2,1)S(1)}, bf16[512,1024]{1,0:T(8,128)(2,1)}, u32[]{:S(2)}, u32[]{:S(2)}) collective-permute-start(bf16[512,1024]{1,0:T(8,128)(2,1)S(1)} %ffn_out.2), channel_id=1, source_target_pairs={{0,16},{1,17},{2,18},{3,19},{4,20},{5,21},{6,22},{7,23},{8,24},{9,... | collective-permute-start | bytes 3145736 | tf_op jit(solution)/shard_map/ppermute | solution.py:990
  325.0 28.1 %collective-permute-start.41 = (bf16[512,1024]{1,0:T(8,128)(2,1)S(1)}, bf16[512,1024]{1,0:T(8,128)(2,1)}, u32[]{:S(2)}, u32[]{:S(2)}) collective-permute-start(bf16[512,1024]{1,0:T(8,128)(2,1)S(1)} %get-tuple-element.134), channel_id=1, source_target_pairs={{16,0},{17,1},{18,2},{19,3},{20,4},{21,5},{22,6},{23,7},{24,8},{25... | collective-permute-start | bytes 3145736 | tf_op jit(solution)/shard_map/ppermute | solution.py:990
  383.9 19.7 %collective-permute-start.45 = (bf16[64,5376]{1,0:T(8,128)(2,1)S(1)}, bf16[64,5376]{1,0:T(8,128)(2,1)S(1)}, u32[]{:S(2)}, u32[]{:S(2)}) collective-permute-start(bf16[64,5376]{1,0:T(8,128)(2,1)S(1)} %get-tuple-element.142), channel_id=1, source_target_pairs={{0,4},{1,3},{4,8},{5,1},{8,12},{9,5},{12,14},{13,9},{14,10},{15,13... | collective-permute-start | bytes 2064392 | tf_op jit(solution)/shard_map/ppermute | solution.py:678
  404.9 23.8 %collective-permute-start.49 = (bf16[128,5376]{1,0:T(8,128)(2,1)S(1)}, bf16[128,5376]{1,0:T(8,128)(2,1)S(1)}, u32[]{:S(2)}, u32[]{:S(2)}) collective-permute-start(bf16[128,5376]{1,0:T(8,128)(2,1)S(1)} %ring_add.12), channel_id=1, source_target_pairs={{0,4},{1,3},{4,8},{5,1},{8,12},{9,5},{12,14},{13,9},{14,10},{15,13... | collective-permute-start | bytes 4128776 | tf_op jit(solution)/shard_map/ppermute | solution.py:678
  408.6 21.4 %collective-permute-start.48 = (bf16[128,2688]{1,0:T(8,128)(2,1)S(1)}, bf16[128,2688]{1,0:T(8,128)(2,1)S(1)}, u32[]{:S(2)}, u32[]{:S(2)}) collective-permute-start(bf16[128,2688]{1,0:T(8,128)(2,1)S(1)} %ring_add.13), channel_id=1, source_target_pairs={{0,4},{1,3},{4,8},{5,1},{8,12},{9,5},{12,14},{13,9},{14,10},{15,13... | collective-permute-start | bytes 2064392 | tf_op jit(solution)/shard_map/ppermute | solution.py:678
  417.4 33.1 %collective-permute-start.53 = (bf16[512,512]{1,0:T(8,128)(2,1)S(1)}, bf16[512,512]{1,0:T(8,128)(2,1)S(1)}, u32[]{:S(2)}, u32[]{:S(2)}) collective-permute-start(bf16[512,512]{1,0:T(8,128)(2,1)S(1)} %get-tuple-element.169), channel_id=1, source_target_pairs={{0,1},{1,0},{2,3},{3,2},{4,5},{5,4},{6,7},{7,6},{8,9},{9,8},{10,11... | collective-permute-start | bytes 1572872 | tf_op jit(solution)/shard_map/ppermute | solution.py:724
  428.1 23.0 %collective-permute-start.54 = (bf16[512,512]{1,0:T(8,128)(2,1)S(1)}, bf16[512,512]{1,0:T(8,128)(2,1)S(1)}, u32[]{:S(2)}, u32[]{:S(2)}) collective-permute-start(bf16[512,512]{1,0:T(8,128)(2,1)S(1)} %get-tuple-element.171), channel_id=1, source_target_pairs={{0,1},{1,0},{2,3},{3,2},{4,5},{5,4},{6,7},{7,6},{8,9},{9,8},{10,11... | collective-permute-start | bytes 1572872 | tf_op jit(solution)/shard_map/ppermute | solution.py:724
  449.3 18.0 %collective-permute-start.52 = (bf16[128,5376]{1,0:T(8,128)(2,1)}, bf16[128,5376]{1,0:T(8,128)(2,1)}, u32[]{:S(2)}, u32[]{:S(2)}) collective-permute-start(bf16[128,5376]{1,0:T(8,128)(2,1)} %ring_add.14), channel_id=1, source_target_pairs={{0,4},{1,3},{4,8},{5,1},{8,12},{9,5},{12,14},{13,9},{14,10},{15,13... | collective-permute-start | bytes 4128776 | tf_op jit(solution)/shard_map/ppermute | solution.py:678
  456.5 47.5 %collective-permute-start.57 = (bf16[448,3072]{1,0:T(8,128)(2,1)}, bf16[448,3072]{1,0:T(8,128)(2,1)}, u32[]{:S(2)}, u32[]{:S(2)}) collective-permute-start(bf16[448,3072]{1,0:T(8,128)(2,1)} %weight_rows.14), channel_id=1, source_target_pairs={{0,1},{1,0},{2,3},{3,2},{4,5},{5,4},{6,7},{7,6},{8,9},{9,8},{10,11... | collective-permute-start | bytes 8257544 | tf_op jit(solution)/shard_map/ppermute | solution.py:675
  457.1 17.5 %collective-permute-start.51 = (bf16[128,2688]{1,0:T(8,128)(2,1)}, bf16[128,2688]{1,0:T(8,128)(2,1)S(1)}, u32[]{:S(2)}, u32[]{:S(2)}) collective-permute-start(bf16[128,2688]{1,0:T(8,128)(2,1)} %ring_add.15), channel_id=1, source_target_pairs={{0,4},{1,3},{4,8},{5,1},{8,12},{9,5},{12,14},{13,9},{14,10},{15,13... | collective-permute-start | bytes 2064392 | tf_op jit(solution)/shard_map/ppermute | solution.py:678
  457.8 19.7 %collective-permute-start.50 = (bf16[128,1024]{1,0:T(8,128)(2,1)}, bf16[128,1024]{1,0:T(8,128)(2,1)}, u32[]{:S(2)}, u32[]{:S(2)}) collective-permute-start(bf16[128,1024]{1,0:T(8,128)(2,1)} %ring_add.16), channel_id=1, source_target_pairs={{0,4},{1,3},{4,8},{5,1},{8,12},{9,5},{12,14},{13,9},{14,10},{15,13... | collective-permute-start | bytes 786440 | tf_op jit(solution)/shard_map/ppermute | solution.py:678
  471.7 37.4 %collective-permute-start.59 = (bf16[128,5376]{1,0:T(8,128)(2,1)S(1)}, bf16[128,5376]{1,0:T(8,128)(2,1)S(1)}, u32[]{:S(2)}, u32[]{:S(2)}) collective-permute-start(bf16[128,5376]{1,0:T(8,128)(2,1)S(1)} %ring_add.17), channel_id=1, source_target_pairs={{0,4},{1,3},{4,8},{5,1},{8,12},{9,5},{12,14},{13,9},{14,10},{15,13... | collective-permute-start | bytes 4128776 | tf_op jit(solution)/shard_map/ppermute | solution.py:678
  474.8 24.7 %collective-permute-start.60 = (bf16[128,2688]{1,0:T(8,128)(2,1)S(1)}, bf16[128,2688]{1,0:T(8,128)(2,1)S(1)}, u32[]{:S(2)}, u32[]{:S(2)}) collective-permute-start(bf16[128,2688]{1,0:T(8,128)(2,1)S(1)} %ring_add.18), channel_id=1, source_target_pairs={{0,4},{1,3},{4,8},{5,1},{8,12},{9,5},{12,14},{13,9},{14,10},{15,13... | collective-permute-start | bytes 2064392 | tf_op jit(solution)/shard_map/ppermute | solution.py:678
  479.2 47.7 %collective-permute-start.62 = (bf16[128,1024]{1,0:T(8,128)(2,1)}, bf16[128,1024]{1,0:T(8,128)(2,1)}, u32[]{:S(2)}, u32[]{:S(2)}) collective-permute-start(bf16[128,1024]{1,0:T(8,128)(2,1)} %ring_add.19), channel_id=1, source_target_pairs={{0,4},{1,3},{4,8},{5,1},{8,12},{9,5},{12,14},{13,9},{14,10},{15,13... | collective-permute-start | bytes 786440 | tf_op jit(solution)/shard_map/ppermute | solution.py:678
  502.7 22.1 %collective-permute-start.69 = (bf16[64,2688]{1,0:T(8,128)(2,1)}, bf16[64,2688]{1,0:T(8,128)(2,1)}, u32[]{:S(2)}, u32[]{:S(2)}) collective-permute-start(bf16[64,2688]{1,0:T(8,128)(2,1)} %dynamic-slice_convert_fusion.2), channel_id=1, source_target_pairs={{0,1},{1,0},{2,3},{3,2},{4,5},{5,4},{6,7},{7,6},{8,9},{9,8},{10,11... | collective-permute-start | bytes 1032200 | tf_op jit(solution)/shard_map/ppermute | solution.py:675
  518.9 39.1 %all-to-all-start.3 = ((bf16[8,64,1024]{2,1,0:T(8,128)(2,1)}), bf16[8,64,1024]{2,1,0:T(8,128)(2,1)}, u32[]{:S(2)}, u32[]{:S(2)}) async-start(bf16[8,64,1024]{2,1,0:T(8,128)(2,1)} %bitcast.180), calls=%async_computation.3 | async-start | bytes 2097152 | tf_op jit(solution)/shard_map/all_to_all | solution.py:695
  530.9 26.2 %collective-permute-start.63 = (bf16[128,3072]{1,0:T(8,128)(2,1)S(1)}, bf16[128,3072]{1,0:T(8,128)(2,1)S(1)}, u32[]{:S(2)}, u32[]{:S(2)}) collective-permute-start(bf16[128,3072]{1,0:T(8,128)(2,1)S(1)} %ring_add.22), channel_id=1, source_target_pairs={{0,4},{1,3},{4,8},{5,1},{8,12},{9,5},{12,14},{13,9},{14,10},{15,13... | collective-permute-start | bytes 2359304 | tf_op jit(solution)/shard_map/ppermute | solution.py:678
  537.7 23.8 %collective-permute-start.66 = (bf16[128,1024]{1,0:T(8,128)(2,1)S(1)}, bf16[128,1024]{1,0:T(8,128)(2,1)}, u32[]{:S(2)}, u32[]{:S(2)}) collective-permute-start(bf16[128,1024]{1,0:T(8,128)(2,1)S(1)} %ring_add.21), channel_id=1, source_target_pairs={{0,4},{1,3},{4,8},{5,1},{8,12},{9,5},{12,14},{13,9},{14,10},{15,13... | collective-permute-start | bytes 786440 | tf_op jit(solution)/shard_map/ppermute | solution.py:678
  537.7 23.7 %collective-permute-start.72 = (f32[2,1024]{1,0:T(2,128)S(1)}, f32[2,1024]{1,0:T(2,128)S(1)}, u32[]{:S(2)}, u32[]{:S(2)}) collective-permute-start(f32[2,1024]{1,0:T(2,128)S(1)} %add.327), channel_id=1, source_target_pairs={{0,4},{1,5},{2,6},{3,7},{4,0},{5,1},{6,2},{7,3},{8,12},{9,13},{10,... | collective-permute-start | bytes 24584 | tf_op jit(solution)/shard_map/ppermute | solution.py:706
  (137 other events, 1858.0 us)

commit v5 on v4

--- a/solution.py
+++ b/solution.py
@@ -184,50 +184,65 @@
     return a, b, v - a - b
 
 
-def attend(q, kv_list, qmarks, kmarks, begin, count):
+def attend(q, kv_list, qmarks, kmarks, begin, count, wide=2, ahead=2):
     rows = q.shape[0]
     members = len(kv_list)
     keys = members * rows
 
     def kernel(q_ref, qm_ref, km_ref, *refs):
         kv_refs, (o_ref, lse_ref) = refs[:members], refs[members:]
-        k = jnp.concatenate([r[:, :LANES] for r in kv_refs], axis=0)
-        v = jnp.concatenate([r[:, LANES:] for r in kv_refs], axis=0)
-        q = q_ref[...] * jnp.asarray(HEAD_DIM**-0.5, BF)
+        heads = []
+        for w in range(wide):
+            k = jnp.concatenate([r[:, 2 * w * LANES : (2 * w + 1) * LANES] for r in kv_refs], axis=0)
+            v = jnp.concatenate([r[:, (2 * w + 1) * LANES : (2 * w + 2) * LANES] for r in kv_refs], axis=0)
+            q = q_ref[:, w * LANES : (w + 1) * LANES] * jnp.asarray(HEAD_DIM**-0.5, BF)
+            for head in range(2):
+                heads.append((w, head, q, k, v))
+
+        def score(n):
+            w, head, q, k, v = heads[n]
+            mine, theirs = head_mask(q.shape, head), head_mask(k.shape, head)
+            return dot(jnp.where(theirs, k, km_ref[...]), jnp.where(mine, q, qm_ref[...]), NT)
+
+        waiting = [score(n) for n in range(ahead)]
         parts, stats = [], []
-        for head in range(2):
-            mine = head_mask((rows, LANES), head)
-            theirs = head_mask((keys, LANES), head)
-            s = dot(jnp.where(theirs, k, km_ref[...]), jnp.where(mine, q, qm_ref[...]), NT)
+        for n, (w, head, q, k, v) in enumerate(heads):
+            if n + ahead < len(heads):
+                waiting.append(score(n + ahead))
+            s = waiting[n]
             top = jnp.max(s, axis=0, keepdims=True)
             e = jnp.exp(s - top).astype(BF)
-            u = dot(pick(theirs, v, 1.0), e, TN)
+            u = dot(pick(head_mask(v.shape, head), v, 1.0), e, TN)
             low, high = u[:HEAD_DIM], u[HEAD_DIM:]
             value, total = (high, low) if head else (low, high)
             parts.append(value / total)
             stats.append(top + jnp.log(total[:1]))
-        o_ref[...] = jnp.concatenate(parts, axis=0).T.astype(BF)
-        lse_ref[0] = jnp.concatenate(stats, axis=0)
-
+        for w in range(wide):
+            o_ref[:, w * LANES : (w + 1) * LANES] = jnp.concatenate(parts[2 * w : 2 * w + 2], axis=0).T.astype(BF)
+            lse_ref[w] = jnp.concatenate(stats[2 * w : 2 * w + 2], axis=0)
+
+    first = begin // wide
     return call(
         kernel,
         "attend",
+        limit=28,
         flops=8 * rows * keys * count * LANES,
         moved=2 * (2 * rows + 2 * keys) * count * LANES,
         exps=rows * keys * count * 2,
-        grid=(count,),
+        grid=(count // wide,),
         in_specs=[
-            pl.BlockSpec((rows, LANES), lambda p: (0, begin + p)),
+            pl.BlockSpec((rows, wide * LANES), lambda p: (0, first + p)),
             whole((rows, LANES)),
             whole((keys, LANES)),
         ]
-        + [pl.BlockSpec((rows, 2 * LANES), lambda p: (0, begin + p))] * members,
+        + [pl.BlockSpec((rows, 2 * wide * LANES), lambda p: (0, first + p))] * members,
         out_specs=[
-            pl.BlockSpec((rows, LANES), lambda p: (0, p)),
-            pl.BlockSpec((1, 2, rows), lambda p: (p, 0, 0)),
+            pl.BlockSpec((rows, wide * LANES), lambda p: (0, p)),
+            pl.BlockSpec((wide, 2, rows), lambda p: (p, 0, 0)),
         ],
         out_shape=[shaped((rows, count * LANES)), shaped((count, 2, rows), F32)],
     )(q, qmarks, kmarks, *kv_list)
+
 
 def project(x, o_list, gains, w_mix):
     rows = x.shape[0]

time: 597 us -> 588 us (0.985)
  Pallas kernels: 246 us -> 236 us
    pallas_call x2, Pallas kernels: 35 us -> 25.3 us  [attend(): call(kernel, 'attend', limit=28, flops=8 * rows * keys * count * LANES, m...]
  transfers between devices with their start and end apart: 77 -> 77, of which waited for: 20 -> 19; matrix products, arithmetic and copies ran while one was open for 10% -> 10% of each run, Pallas kernels for 23% -> 23%
where the time goes in v5:
time: 588 us; the launch traced here: 578 us
  Pallas kernels  236 us (40%)
  waiting for transfers between devices  159 us (27%)
  starting transfers between devices  82.1 us (14%)
  local copies, waits for them, and re-layouts  59.6 us (10%)
  other arithmetic  30.5 us (5%)
  blocking collectives  8.43 us (1%)
    ppermute x32, waiting for transfers between devices, step(): return lax.ppermute(array, BOTH, self.ring_pairs)  112 us
    pallas_call x5, Pallas kernels, attend_back(): call(kernel, 'attend_back', flops=20 * rows * keys * count * LANES, moved...  60.7 us
    ppermute x2, waiting for transfers between devices, handed(): return lax.ppermute(array, 'section', pairs)  36.6 us
    pallas_call x8, Pallas kernels, weight_rows(): call(kernel, 'weight_rows', limit=max(8, 4 + int(1.25 * size) // (1024 *...  33.1 us
    ppermute x32, starting transfers between devices, step(): return lax.ppermute(array, BOTH, self.ring_pairs)  28.7 us
    unnamed x189, local copies, waits for them, and re-layouts  27.3 us
    ppermute x29, starting transfers between devices, swap(): return lax.ppermute(array, 'wshard', [(0, 1), (1, 0)])  25.7 us
    pallas_call x2, Pallas kernels, attend(): call(kernel, 'attend', limit=28, flops=8 * rows * keys * count * LANES, m...  25.3 us
  transfers between devices with their start and end apart: 77, of which 19 were waited for; matrix products, arithmetic and copies ran while one was open for 10% of the time, Pallas kernels for 23%

profile of v5, /device:TPU:13, one launch (start us, length us, event | category | flops | bytes accessed | tf_op | source)
XLA Modules:
  0.0 578.3 jit_solution(1212622549501939127)
XLA Ops:
  24.5 7.6 %collective-permute-done.2 = bf16[128,4224]{1,0:T(8,128)(2,1)} collective-permute-done((bf16[128,4224]{1,0:T(8,128)(2,1)S(1)}, bf16[128,4224]{1,0:T(8,128)(2,1)}, u32[]{:S(2)}, u32[]{:S(2)}) %collective-permute-start.2) | collective-permute-done | bytes 1081376 | tf_op jit(solution)/shard_map/ppermute | solution.py:693
  32.0 5.7 all-to-all-start.1
  51.5 28.4 %collective-permute-done.13 = bf16[128,2688]{1,0:T(8,128)(2,1)S(1)} collective-permute-done((bf16[128,2688]{1,0:T(8,128)(2,1)S(1)}, bf16[128,2688]{1,0:T(8,128)(2,1)S(1)}, u32[]{:S(2)}, u32[]{:S(2)}) %collective-permute-start.13) | collective-permute-done | bytes 688160 | tf_op jit(solution)/shard_map/ppermute | solution.py:693
  111.9 5.3 collective-permute-done.15
  124.9 6.3 %keys_values.2 = (bf16[512,1024]{1,0:T(8,128)(2,1)S(1)}, bf16[512,2048]{1,0:T(8,128)(2,1)S(1)}) custom-call(bf16[512,1024]{1,0:T(8,128)(2,1)S(1)} %bitcast.168, f32[8,1024]{1,0:T(8,128)S(1)} %gains.1.gain_ref, bf16[1024,4224]{1,0:T(8,128)(2,1)} %bitcast.19.w_ref.wkv_ref.wq_ref, f32[512,128]{1,0:T(8,128)S(1)} %get-tuple-element.254.cos_ref, ...), custom_call_target="tpu_custom_call" | custom-call | flops 2147483648 | bytes 8388608 | tf_op jit(solution)/shard_map/keys_values/pallas_call | solution.py:129
  140.9 12.9 %attend.2 = (bf16[512,1024]{1,0:T(8,128)(2,1)S(1)}, f32[8,2,512]{2,1,0:T(2,128)}) custom-call(bf16[512,1024]{1,0:T(8,128)(2,1)S(1)} %queries.2.q_ref, bf16[512,128]{1,0:T(8,128)(2,1)S(1)} %select_convert_fusion.1.qm_ref, bf16[1024,128]{1,0:T(8,128)(2,1)S(1)} %select_convert_fusion.km_ref, bf16[512,2048]{1,0:T(8,128)(2,1)S(1)} %get-tuple-element.112.refs_0_, ...), custom_call_target="tpu_custom_call" | custom-call | flops 4294967296 | bytes 6291456 | tf_op jit(solution)/shard_map/attend/pallas_call | solution.py:225
  160.2 8.1 %collective-permute-done.30 = bf16[64,2688]{1,0:T(8,128)(2,1)S(1)} collective-permute-done((bf16[64,2688]{1,0:T(8,128)(2,1)S(1)}, bf16[64,2688]{1,0:T(8,128)(2,1)S(1)}, u32[]{:S(2)}, u32[]{:S(2)}) %collective-permute-start.30) | collective-permute-done | bytes 344096 | tf_op jit(solution)/shard_map/ppermute | solution.py:693
  176.8 8.9 %ffn_in.2.z_ref = bf16[512,2688]{1,0:T(8,128)(2,1)S(1)} custom-call(bf16[512,1024]{1,0:T(8,128)(2,1)S(1)} %get-tuple-element.118.b_ref, bf16[1024,2688]{1,0:T(8,128)(2,1)} %bitcast.36.wa_ref, bf16[1024,2688]{1,0:T(8,128)(2,1)S(1)} %bitcast.174), custom_call_target="tpu_custom_call" | custom-call | flops 5637144576 | bytes 14811136 | tf_op jit(solution)/shard_map/ffn_in/pallas_call | solution.py:303
  194.7 21.2 %collective-permute-done.38 = bf16[512,1024]{1,0:T(8,128)(2,1)} collective-permute-done((bf16[512,1024]{1,0:T(8,128)(2,1)S(1)}, bf16[512,1024]{1,0:T(8,128)(2,1)}, u32[]{:S(2)}, u32[]{:S(2)}) %collective-permute-start.38) | collective-permute-done | bytes 1048608 | tf_op jit(solution)/shard_map/ppermute | solution.py:1005
  216.0 6.4 %keys_values.3 = (bf16[512,1024]{1,0:T(8,128)(2,1)S(1)}, bf16[512,2048]{1,0:T(8,128)(2,1)S(1)}) custom-call(bf16[512,1024]{1,0:T(8,128)(2,1)S(1)} %broadcast_select_fusion.2.x_ref, f32[8,1024]{1,0:T(8,128)S(1)} %gains.1.gain_ref, bf16[1024,4224]{1,0:T(8,128)(2,1)} %bitcast.19.w_ref.wkv_ref.wq_ref, f32[512,128]{1,0:T(8,128)S(1)} %get-tuple-element.254.cos_ref, ...), custom_call_target="tpu_custom_call" | custom-call | flops 2147483648 | bytes 8388608 | tf_op jit(solution)/shard_map/keys_values/pallas_call | solution.py:129
  227.3 12.4 %attend.3 = (bf16[512,1024]{1,0:T(8,128)(2,1)S(1)}, f32[8,2,512]{2,1,0:T(2,128)S(1)}) custom-call(bf16[512,1024]{1,0:T(8,128)(2,1)S(1)} %queries.3.q_ref, bf16[512,128]{1,0:T(8,128)(2,1)S(1)} %select_convert_fusion.1.qm_ref, bf16[1024,128]{1,0:T(8,128)(2,1)S(1)} %select_convert_fusion.km_ref, bf16[512,2048]{1,0:T(8,128)(2,1)S(1)} %get-tuple-element.120.refs_0_, ...), custom_call_target="tpu_custom_call" | custom-call | flops 4294967296 | bytes 6291456 | tf_op jit(solution)/shard_map/attend/pallas_call | solution.py:225
  243.5 10.5 %ffn_in.3 = (bf16[512,2688]{1,0:T(8,128)(2,1)S(1)}, bf16[512,2688]{1,0:T(8,128)(2,1)S(1)}, bf16[512,2688]{1,0:T(8,128)(2,1)S(1)}) custom-call(bf16[512,1024]{1,0:T(8,128)(2,1)S(1)} %get-tuple-element.141.b_ref.refs_0_, bf16[1024,2688]{1,0:T(8,128)(2,1)} %bitcast.36.wa_ref, bf16[1024,2688]{1,0:T(8,128)(2,1)S(1)} %bitcast.177), custom_call_target="tpu_custom_call" | custom-call | flops 5637144576 | bytes 20316160 | tf_op jit(solution)/shard_map/ffn_in/pallas_call | solution.py:303
  255.6 5.3 ffn_back.2
  260.9 10.3 %hidden_back.2 = (f32[512,1024]{1,0:T(8,128)S(1)}, bf16[512,1024]{1,0:T(8,128)(2,1)S(1)}, f32[1,1024]{1,0:T(1,128)}) custom-call(bf16[512,1024]{1,0:T(8,128)(2,1)S(1)} %bitcast.171, bf16[512,2688]{1,0:T(8,128)(2,1)S(1)} %get-tuple-element.125.da_ref, bf16[512,2688]{1,0:T(8,128)(2,1)S(1)} %get-tuple-element.126.dg_ref, ...), custom_call_target="tpu_custom_call" | custom-call | flops 5637144576 | bytes 22806528 | tf_op jit(solution)/shard_map/hidden_back/pallas_call | solution.py:377
  271.2 29.3 %attend_back.5 = (bf16[512,1024]{1,0:T(8,128)(2,1)S(1)}, bf16[512,2048]{1,0:T(8,128)(2,1)S(1)}, bf16[512,2048]{1,0:T(8,128)(2,1)S(1)}) custom-call(bf16[512,1024]{1,0:T(8,128)(2,1)S(1)} %queries.3.q_ref, bf16[512,1024]{1,0:T(8,128)(2,1)S(1)} %get-tuple-element.129.dh_ref, bf16[1024,4224]{1,0:T(8,128)(2,1)} %bitcast.19.w_ref.wkv_ref.wq_ref, ...), custom_call_target="tpu_custom_call" | custom-call | flops 10737418240 | bytes 14680064 | tf_op jit(solution)/shard_map/attend_back/pallas_call | solution.py:445
  307.3 8.0 %input_back.2 = (bf16[512,1024]{1,0:T(8,128)(2,1)S(1)}, f32[1,1024]{1,0:T(1,128)}) custom-call(bf16[512,1024]{1,0:T(8,128)(2,1)S(1)} %broadcast_select_fusion.2.x_ref, f32[512,1024]{1,0:T(8,128)S(1)} %get-tuple-element.128.dh_ref, f32[8,1024]{1,0:T(8,128)S(1)} %gains.1.gain_ref, bf16[1024,4224]{1,0:T(8,128)(2,1)} %bitcast.19.w_ref.wkv_ref.wq_ref, ...), custom_call_target="tpu_custom_call" | custom-call | flops 3221225472 | bytes 16777216 | tf_op jit(solution)/shard_map/input_back/pallas_call | solution.py:521
  327.9 15.4 %collective-permute-done.41 = bf16[512,1024]{1,0:T(8,128)(2,1)} collective-permute-done((bf16[512,1024]{1,0:T(8,128)(2,1)S(1)}, bf16[512,1024]{1,0:T(8,128)(2,1)}, u32[]{:S(2)}, u32[]{:S(2)}) %collective-permute-start.41) | collective-permute-done | bytes 1048608 | tf_op jit(solution)/shard_map/ppermute | solution.py:1005
  344.7 5.3 ffn_back.3
  350.1 5.8 weight_rows.8
  367.7 6.4 %weight_rows.10 = (bf16[64,5376]{1,0:T(8,128)(2,1)S(1)}, bf16[512,5376]{1,0:T(8,128)(2,1)S(1)}) custom-call(s32[9]{0:T(128)S(1)} %stack.67.order_ref, bf16[512,1024]{1,0:T(8,128)(2,1)S(1)} %copy-done.69, bf16[512,2688]{1,0:T(8,128)(2,1)S(1)} %get-tuple-element.137.refs_1_.da_ref, bf16[512,2688]{1,0:T(8,128)(2,1)S(1)} %copy-done.49, ...), custom_call_target="tpu_custom_call" | custom-call | flops 3170893824 | bytes 17563648 | tf_op jit(solution)/shard_map/weight_rows/pallas_call | solution.py:592
  374.8 6.1 %weight_rows.11 = (bf16[64,2688]{1,0:T(8,128)(2,1)S(1)}, bf16[512,2688]{1,0:T(8,128)(2,1)S(1)}) custom-call(s32[9]{0:T(128)S(1)} %stack.67.order_ref, bf16[512,1024]{1,0:T(8,128)(2,1)S(1)} %copy-done.18, bf16[512,2688]{1,0:T(8,128)(2,1)S(1)} %copy-done.16, bf16[448,2688]{1,0:T(8,128)(2,1)} %collective-permute-done.43.refs_2_), custom_call_target="tpu_custom_call" | custom-call | flops 1585446912 | bytes 9306112 | tf_op jit(solution)/shard_map/weight_rows/pallas_call | solution.py:592
  384.4 9.9 %hidden_back.3 = (f32[512,1024]{1,0:T(8,128)S(1)}, bf16[512,1024]{1,0:T(8,128)(2,1)S(1)}, f32[1,1024]{1,0:T(1,128)S(1)}) custom-call(bf16[512,1024]{1,0:T(8,128)(2,1)S(1)} %copy-done.18, bf16[512,2688]{1,0:T(8,128)(2,1)S(1)} %copy-done.47, bf16[512,2688]{1,0:T(8,128)(2,1)S(1)} %copy-done.50, f32[512,1024]{1,0:T(8,128)S(1)} %copy-done.63, ...), custom_call_target="tpu_custom_call" | custom-call | flops 5637144576 | bytes 22806528 | tf_op jit(solution)/shard_map/hidden_back/pallas_call | solution.py:377
  400.4 7.8 %attend_back.6 = (bf16[512,256]{1,0:T(8,128)(2,1)S(1)}, bf16[512,512]{1,0:T(8,128)(2,1)S(1)}, bf16[512,512]{1,0:T(8,128)(2,1)S(1)}) custom-call(bf16[512,1024]{1,0:T(8,128)(2,1)S(1)} %copy-done.12, bf16[512,1024]{1,0:T(8,128)(2,1)S(1)} %get-tuple-element.152.refs_1_.dh_ref, bf16[1024,4224]{1,0:T(8,128)(2,1)} %bitcast.19.w_ref.wkv_ref.wq_ref, ...), custom_call_target="tpu_custom_call" | custom-call | flops 2684354560 | bytes 3670016 | tf_op jit(solution)/shard_map/attend_back/pallas_call | solution.py:445
  410.9 8.0 %attend_back.7 = (bf16[512,256]{1,0:T(8,128)(2,1)S(1)}, bf16[512,512]{1,0:T(8,128)(2,1)S(1)}, bf16[512,512]{1,0:T(8,128)(2,1)S(1)}) custom-call(bf16[512,1024]{1,0:T(8,128)(2,1)S(1)} %copy-done.12, bf16[512,1024]{1,0:T(8,128)(2,1)S(1)} %get-tuple-element.152.refs_1_.dh_ref, bf16[1024,4224]{1,0:T(8,128)(2,1)} %bitcast.19.w_ref.wkv_ref.wq_ref, ...), custom_call_target="tpu_custom_call" | custom-call | flops 2684354560 | bytes 3670016 | tf_op jit(solution)/shard_map/attend_back/pallas_call | solution.py:445
  422.7 7.8 %attend_back.8 = (bf16[512,256]{1,0:T(8,128)(2,1)S(1)}, bf16[512,512]{1,0:T(8,128)(2,1)S(1)}, bf16[512,512]{1,0:T(8,128)(2,1)S(1)}) custom-call(bf16[512,1024]{1,0:T(8,128)(2,1)S(1)} %copy-done.12, bf16[512,1024]{1,0:T(8,128)(2,1)S(1)} %get-tuple-element.152.refs_1_.dh_ref, bf16[1024,4224]{1,0:T(8,128)(2,1)} %bitcast.19.w_ref.wkv_ref.wq_ref, ...), custom_call_target="tpu_custom_call" | custom-call | flops 2684354560 | bytes 3670016 | tf_op jit(solution)/shard_map/attend_back/pallas_call | solution.py:445
  432.3 7.8 %attend_back.9 = (bf16[512,256]{1,0:T(8,128)(2,1)S(1)}, bf16[512,512]{1,0:T(8,128)(2,1)S(1)}, bf16[512,512]{1,0:T(8,128)(2,1)S(1)}) custom-call(bf16[512,1024]{1,0:T(8,128)(2,1)S(1)} %copy-done.12, bf16[512,1024]{1,0:T(8,128)(2,1)S(1)} %get-tuple-element.152.refs_1_.dh_ref, bf16[1024,4224]{1,0:T(8,128)(2,1)} %bitcast.19.w_ref.wkv_ref.wq_ref, ...), custom_call_target="tpu_custom_call" | custom-call | flops 2684354560 | bytes 3670016 | tf_op jit(solution)/shard_map/attend_back/pallas_call | solution.py:445
  449.2 9.1 %collective-permute-done.52.moving_ref = bf16[128,5376]{1,0:T(8,128)(2,1)} collective-permute-done((bf16[128,5376]{1,0:T(8,128)(2,1)}, bf16[128,5376]{1,0:T(8,128)(2,1)}, u32[]{:S(2)}, u32[]{:S(2)}) %collective-permute-start.52) | collective-permute-done | bytes 1376288 | tf_op jit(solution)/shard_map/ppermute | solution.py:693
  470.6 7.4 %input_back.3 = (bf16[512,1024]{1,0:T(8,128)(2,1)S(1)}, f32[1,1024]{1,0:T(1,128)S(1)}) custom-call(bf16[512,1024]{1,0:T(8,128)(2,1)S(1)} %copy-done.10, f32[512,1024]{1,0:T(8,128)S(1)} %copy-done.60, f32[8,1024]{1,0:T(8,128)S(1)} %copy-done.66, bf16[1024,4224]{1,0:T(8,128)(2,1)} %bitcast.19.w_ref.wkv_ref.wq_ref, ...), custom_call_target="tpu_custom_call" | custom-call | flops 3221225472 | bytes 16777216 | tf_op jit(solution)/shard_map/input_back/pallas_call | solution.py:521
  479.8 10.7 %collective-permute-done.60 = bf16[128,2688]{1,0:T(8,128)(2,1)S(1)} collective-permute-done((bf16[128,2688]{1,0:T(8,128)(2,1)S(1)}, bf16[128,2688]{1,0:T(8,128)(2,1)S(1)}, u32[]{:S(2)}, u32[]{:S(2)}) %collective-permute-start.60) | collective-permute-done | bytes 688160 | tf_op jit(solution)/shard_map/ppermute | solution.py:693
  509.3 5.6 all-to-all-start.3
  526.9 20.7 %collective-permute-done.63.moving_ref = bf16[128,3072]{1,0:T(8,128)(2,1)S(1)} collective-permute-done((bf16[128,3072]{1,0:T(8,128)(2,1)S(1)}, bf16[128,3072]{1,0:T(8,128)(2,1)S(1)}, u32[]{:S(2)}, u32[]{:S(2)}) %collective-permute-start.63) | collective-permute-done | bytes 786464 | tf_op jit(solution)/shard_map/ppermute | solution.py:693
  555.7 5.3 collective-permute-done.64
  (481 shorter events, 249.9 us)
Async XLA Ops:
  13.9 18.2 %collective-permute-start.2 = (bf16[128,4224]{1,0:T(8,128)(2,1)S(1)}, bf16[128,4224]{1,0:T(8,128)(2,1)}, u32[]{:S(2)}, u32[]{:S(2)}) collective-permute-start(bf16[128,4224]{1,0:T(8,128)(2,1)S(1)} %pad_maximum_fusion), channel_id=1, source_target_pairs={{0,4},{1,3},{4,8},{5,1},{8,12},{9,5},{12,14},{13,9},{14,10},{15,13... | collective-permute-start | bytes 3244040 | tf_op jit(solution)/shard_map/ppermute | solution.py:693
  21.6 20.9 %collective-permute-start.12 = (bf16[128,2688]{1,0:T(8,128)(2,1)}, bf16[128,2688]{1,0:T(8,128)(2,1)S(1)}, u32[]{:S(2)}, u32[]{:S(2)}) collective-permute-start(bf16[128,2688]{1,0:T(8,128)(2,1)} %collective-permute-done.3), channel_id=1, source_target_pairs={{0,4},{1,3},{4,8},{5,1},{8,12},{9,5},{12,14},{13,9},{14,10},{15,13... | collective-permute-start | bytes 2064392 | tf_op jit(solution)/shard_map/ppermute | solution.py:693
  21.9 21.7 %collective-permute-start.23 = (bf16[128,2688]{1,0:T(8,128)(2,1)}, bf16[128,2688]{1,0:T(8,128)(2,1)}, u32[]{:S(2)}, u32[]{:S(2)}) collective-permute-start(bf16[128,2688]{1,0:T(8,128)(2,1)} %collective-permute-done.3), channel_id=1, source_target_pairs={{0,1},{1,0},{2,3},{3,2},{4,5},{5,4},{6,7},{7,6},{8,9},{9,8},{10,11... | collective-permute-start | bytes 2064392 | tf_op jit(solution)/shard_map/ppermute | solution.py:690
  32.0 57.5 %all-to-all-start.1 = ((bf16[8,64,1024]{2,1,0:T(8,128)(2,1)}), bf16[8,64,1024]{2,1,0:T(8,128)(2,1)S(1)}, u32[]{:S(2)}, u32[]{:S(2)}) async-start(bf16[8,64,1024]{2,1,0:T(8,128)(2,1)} %bitcast.9), calls=%async_computation.1 | async-start | bytes 2097152 | tf_op jit(solution)/shard_map/all_to_all | solution.py:707
  39.6 45.0 %collective-permute-start.4 = (bf16[128,4224]{1,0:T(8,128)(2,1)}, bf16[128,4224]{1,0:T(8,128)(2,1)S(1)}, u32[]{:S(2)}, u32[]{:S(2)}) collective-permute-start(bf16[128,4224]{1,0:T(8,128)(2,1)} %collective-permute-done.2), channel_id=1, source_target_pairs={{0,1},{1,0},{2,3},{3,2},{4,5},{5,4},{6,7},{7,6},{8,9},{9,8},{10,11... | collective-permute-start | bytes 3244040 | tf_op jit(solution)/shard_map/ppermute | solution.py:690
  42.4 41.6 %collective-permute-start.5 = (bf16[128,4224]{1,0:T(8,128)(2,1)}, bf16[128,4224]{1,0:T(8,128)(2,1)}, u32[]{:S(2)}, u32[]{:S(2)}) collective-permute-start(bf16[128,4224]{1,0:T(8,128)(2,1)} %collective-permute-done.2), channel_id=1, source_target_pairs={{0,4},{1,3},{4,8},{5,1},{8,12},{9,5},{12,14},{13,9},{14,10},{15,13... | collective-permute-start | bytes 3244040 | tf_op jit(solution)/shard_map/ppermute | solution.py:693
  43.6 36.3 %collective-permute-start.13 = (bf16[128,2688]{1,0:T(8,128)(2,1)S(1)}, bf16[128,2688]{1,0:T(8,128)(2,1)S(1)}, u32[]{:S(2)}, u32[]{:S(2)}) collective-permute-start(bf16[128,2688]{1,0:T(8,128)(2,1)S(1)} %collective-permute-done.12), channel_id=1, source_target_pairs={{0,4},{1,3},{4,8},{5,1},{8,12},{9,5},{12,14},{13,9},{14,10},{15,13... | collective-permute-start | bytes 2064392 | tf_op jit(solution)/shard_map/ppermute | solution.py:693
  47.8 34.4 %collective-permute-start.24 = (bf16[128,2688]{1,0:T(8,128)(2,1)S(1)}, bf16[128,2688]{1,0:T(8,128)(2,1)S(1)}, u32[]{:S(2)}, u32[]{:S(2)}) collective-permute-start(bf16[128,2688]{1,0:T(8,128)(2,1)S(1)} %collective-permute-done.12), channel_id=1, source_target_pairs={{0,1},{1,0},{2,3},{3,2},{4,5},{5,4},{6,7},{7,6},{8,9},{9,8},{10,11... | collective-permute-start | bytes 2064392 | tf_op jit(solution)/shard_map/ppermute | solution.py:690
  110.8 24.3 %collective-permute-start.18 = (bf16[128,2688]{1,0:T(8,128)(2,1)}, bf16[128,2688]{1,0:T(8,128)(2,1)S(1)}, u32[]{:S(2)}, u32[]{:S(2)}) collective-permute-start(bf16[128,2688]{1,0:T(8,128)(2,1)} %pad_maximum_fusion.3), channel_id=1, source_target_pairs={{0,4},{1,3},{4,8},{5,1},{8,12},{9,5},{12,14},{13,9},{14,10},{15,13... | collective-permute-start | bytes 2064392 | tf_op jit(solution)/shard_map/ppermute | solution.py:693
  117.3 19.9 %collective-permute-start.19 = (bf16[128,2688]{1,0:T(8,128)(2,1)S(1)}, bf16[128,2688]{1,0:T(8,128)(2,1)S(1)}, u32[]{:S(2)}, u32[]{:S(2)}) collective-permute-start(bf16[128,2688]{1,0:T(8,128)(2,1)S(1)} %collective-permute-done.15), channel_id=1, source_target_pairs={{0,4},{1,3},{4,8},{5,1},{8,12},{9,5},{12,14},{13,9},{14,10},{15,13... | collective-permute-start | bytes 2064392 | tf_op jit(solution)/shard_map/ppermute | solution.py:693
  119.1 19.1 %collective-permute-start.27 = (bf16[128,2688]{1,0:T(8,128)(2,1)S(1)}, bf16[128,2688]{1,0:T(8,128)(2,1)S(1)}, u32[]{:S(2)}, u32[]{:S(2)}) collective-permute-start(bf16[128,2688]{1,0:T(8,128)(2,1)S(1)} %collective-permute-done.15), channel_id=1, source_target_pairs={{0,1},{1,0},{2,3},{3,2},{4,5},{5,4},{6,7},{7,6},{8,9},{9,8},{10,11... | collective-permute-start | bytes 2064392 | tf_op jit(solution)/shard_map/ppermute | solution.py:690
  135.1 19.2 %collective-permute-start.21 = (bf16[128,2688]{1,0:T(8,128)(2,1)S(1)}, bf16[128,2688]{1,0:T(8,128)(2,1)S(1)}, u32[]{:S(2)}, u32[]{:S(2)}) collective-permute-start(bf16[128,2688]{1,0:T(8,128)(2,1)S(1)} %collective-permute-done.18), channel_id=1, source_target_pairs={{0,4},{1,3},{4,8},{5,1},{8,12},{9,5},{12,14},{13,9},{14,10},{15,13... | collective-permute-start | bytes 2064392 | tf_op jit(solution)/shard_map/ppermute | solution.py:693
  153.9 17.2 %collective-permute-start.29 = (bf16[128,2688]{1,0:T(8,128)(2,1)S(1)}, bf16[128,2688]{1,0:T(8,128)(2,1)S(1)}, u32[]{:S(2)}, u32[]{:S(2)}) collective-permute-start(bf16[128,2688]{1,0:T(8,128)(2,1)S(1)} %collective-permute-done.22), channel_id=1, source_target_pairs={{0,1},{1,0},{2,3},{3,2},{4,5},{5,4},{6,7},{7,6},{8,9},{9,8},{10,11... | collective-permute-start | bytes 2064392 | tf_op jit(solution)/shard_map/ppermute | solution.py:690
  190.2 25.7 %collective-permute-start.38 = (bf16[512,1024]{1,0:T(8,128)(2,1)S(1)}, bf16[512,1024]{1,0:T(8,128)(2,1)}, u32[]{:S(2)}, u32[]{:S(2)}) collective-permute-start(bf16[512,1024]{1,0:T(8,128)(2,1)S(1)} %ffn_out.2), channel_id=1, source_target_pairs={{0,16},{1,17},{2,18},{3,19},{4,20},{5,21},{6,22},{7,23},{8,24},{9,... | collective-permute-start | bytes 3145736 | tf_op jit(solution)/shard_map/ppermute | solution.py:1005
  315.3 28.1 %collective-permute-start.41 = (bf16[512,1024]{1,0:T(8,128)(2,1)S(1)}, bf16[512,1024]{1,0:T(8,128)(2,1)}, u32[]{:S(2)}, u32[]{:S(2)}) collective-permute-start(bf16[512,1024]{1,0:T(8,128)(2,1)S(1)} %get-tuple-element.134), channel_id=1, source_target_pairs={{16,0},{17,1},{18,2},{19,3},{20,4},{21,5},{22,6},{23,7},{24,8},{25... | collective-permute-start | bytes 3145736 | tf_op jit(solution)/shard_map/ppermute | solution.py:1005
  374.1 20.2 %collective-permute-start.45 = (bf16[64,5376]{1,0:T(8,128)(2,1)S(1)}, bf16[64,5376]{1,0:T(8,128)(2,1)S(1)}, u32[]{:S(2)}, u32[]{:S(2)}) collective-permute-start(bf16[64,5376]{1,0:T(8,128)(2,1)S(1)} %get-tuple-element.142), channel_id=1, source_target_pairs={{0,4},{1,3},{4,8},{5,1},{8,12},{9,5},{12,14},{13,9},{14,10},{15,13... | collective-permute-start | bytes 2064392 | tf_op jit(solution)/shard_map/ppermute | solution.py:693
  395.7 23.7 %collective-permute-start.49 = (bf16[128,5376]{1,0:T(8,128)(2,1)S(1)}, bf16[128,5376]{1,0:T(8,128)(2,1)S(1)}, u32[]{:S(2)}, u32[]{:S(2)}) collective-permute-start(bf16[128,5376]{1,0:T(8,128)(2,1)S(1)} %ring_add.12), channel_id=1, source_target_pairs={{0,4},{1,3},{4,8},{5,1},{8,12},{9,5},{12,14},{13,9},{14,10},{15,13... | collective-permute-start | bytes 4128776 | tf_op jit(solution)/shard_map/ppermute | solution.py:693
  399.4 21.3 %collective-permute-start.48 = (bf16[128,2688]{1,0:T(8,128)(2,1)S(1)}, bf16[128,2688]{1,0:T(8,128)(2,1)S(1)}, u32[]{:S(2)}, u32[]{:S(2)}) collective-permute-start(bf16[128,2688]{1,0:T(8,128)(2,1)S(1)} %ring_add.13), channel_id=1, source_target_pairs={{0,4},{1,3},{4,8},{5,1},{8,12},{9,5},{12,14},{13,9},{14,10},{15,13... | collective-permute-start | bytes 2064392 | tf_op jit(solution)/shard_map/ppermute | solution.py:693
  408.2 32.8 %collective-permute-start.53 = (bf16[512,512]{1,0:T(8,128)(2,1)S(1)}, bf16[512,512]{1,0:T(8,128)(2,1)S(1)}, u32[]{:S(2)}, u32[]{:S(2)}) collective-permute-start(bf16[512,512]{1,0:T(8,128)(2,1)S(1)} %get-tuple-element.169), channel_id=1, source_target_pairs={{0,1},{1,0},{2,3},{3,2},{4,5},{5,4},{6,7},{7,6},{8,9},{9,8},{10,11... | collective-permute-start | bytes 1572872 | tf_op jit(solution)/shard_map/ppermute | solution.py:739
  418.9 22.6 %collective-permute-start.54 = (bf16[512,512]{1,0:T(8,128)(2,1)S(1)}, bf16[512,512]{1,0:T(8,128)(2,1)S(1)}, u32[]{:S(2)}, u32[]{:S(2)}) collective-permute-start(bf16[512,512]{1,0:T(8,128)(2,1)S(1)} %get-tuple-element.171), channel_id=1, source_target_pairs={{0,1},{1,0},{2,3},{3,2},{4,5},{5,4},{6,7},{7,6},{8,9},{9,8},{10,11... | collective-permute-start | bytes 1572872 | tf_op jit(solution)/shard_map/ppermute | solution.py:739
  440.2 18.0 %collective-permute-start.52 = (bf16[128,5376]{1,0:T(8,128)(2,1)}, bf16[128,5376]{1,0:T(8,128)(2,1)}, u32[]{:S(2)}, u32[]{:S(2)}) collective-permute-start(bf16[128,5376]{1,0:T(8,128)(2,1)} %ring_add.14), channel_id=1, source_target_pairs={{0,4},{1,3},{4,8},{5,1},{8,12},{9,5},{12,14},{13,9},{14,10},{15,13... | collective-permute-start | bytes 4128776 | tf_op jit(solution)/shard_map/ppermute | solution.py:693
  446.9 48.0 %collective-permute-start.57 = (bf16[448,3072]{1,0:T(8,128)(2,1)}, bf16[448,3072]{1,0:T(8,128)(2,1)}, u32[]{:S(2)}, u32[]{:S(2)}) collective-permute-start(bf16[448,3072]{1,0:T(8,128)(2,1)} %weight_rows.14), channel_id=1, source_target_pairs={{0,1},{1,0},{2,3},{3,2},{4,5},{5,4},{6,7},{7,6},{8,9},{9,8},{10,11... | collective-permute-start | bytes 8257544 | tf_op jit(solution)/shard_map/ppermute | solution.py:690
  447.4 18.1 %collective-permute-start.51 = (bf16[128,2688]{1,0:T(8,128)(2,1)}, bf16[128,2688]{1,0:T(8,128)(2,1)S(1)}, u32[]{:S(2)}, u32[]{:S(2)}) collective-permute-start(bf16[128,2688]{1,0:T(8,128)(2,1)} %ring_add.15), channel_id=1, source_target_pairs={{0,4},{1,3},{4,8},{5,1},{8,12},{9,5},{12,14},{13,9},{14,10},{15,13... | collective-permute-start | bytes 2064392 | tf_op jit(solution)/shard_map/ppermute | solution.py:693
  448.7 19.7 %collective-permute-start.50 = (bf16[128,1024]{1,0:T(8,128)(2,1)}, bf16[128,1024]{1,0:T(8,128)(2,1)}, u32[]{:S(2)}, u32[]{:S(2)}) collective-permute-start(bf16[128,1024]{1,0:T(8,128)(2,1)} %ring_add.16), channel_id=1, source_target_pairs={{0,4},{1,3},{4,8},{5,1},{8,12},{9,5},{12,14},{13,9},{14,10},{15,13... | collective-permute-start | bytes 786440 | tf_op jit(solution)/shard_map/ppermute | solution.py:693
  462.6 36.9 %collective-permute-start.59 = (bf16[128,5376]{1,0:T(8,128)(2,1)S(1)}, bf16[128,5376]{1,0:T(8,128)(2,1)S(1)}, u32[]{:S(2)}, u32[]{:S(2)}) collective-permute-start(bf16[128,5376]{1,0:T(8,128)(2,1)S(1)} %ring_add.17), channel_id=1, source_target_pairs={{0,4},{1,3},{4,8},{5,1},{8,12},{9,5},{12,14},{13,9},{14,10},{15,13... | collective-permute-start | bytes 4128776 | tf_op jit(solution)/shard_map/ppermute | solution.py:693
  465.7 24.7 %collective-permute-start.60 = (bf16[128,2688]{1,0:T(8,128)(2,1)S(1)}, bf16[128,2688]{1,0:T(8,128)(2,1)S(1)}, u32[]{:S(2)}, u32[]{:S(2)}) collective-permute-start(bf16[128,2688]{1,0:T(8,128)(2,1)S(1)} %ring_add.18), channel_id=1, source_target_pairs={{0,4},{1,3},{4,8},{5,1},{8,12},{9,5},{12,14},{13,9},{14,10},{15,13... | collective-permute-start | bytes 2064392 | tf_op jit(solution)/shard_map/ppermute | solution.py:693
  470.1 47.1 %collective-permute-start.62 = (bf16[128,1024]{1,0:T(8,128)(2,1)}, bf16[128,1024]{1,0:T(8,128)(2,1)}, u32[]{:S(2)}, u32[]{:S(2)}) collective-permute-start(bf16[128,1024]{1,0:T(8,128)(2,1)} %ring_add.19), channel_id=1, source_target_pairs={{0,4},{1,3},{4,8},{5,1},{8,12},{9,5},{12,14},{13,9},{14,10},{15,13... | collective-permute-start | bytes 786440 | tf_op jit(solution)/shard_map/ppermute | solution.py:693
  493.6 21.5 %collective-permute-start.69 = (bf16[64,2688]{1,0:T(8,128)(2,1)}, bf16[64,2688]{1,0:T(8,128)(2,1)}, u32[]{:S(2)}, u32[]{:S(2)}) collective-permute-start(bf16[64,2688]{1,0:T(8,128)(2,1)} %dynamic-slice_convert_fusion.2), channel_id=1, source_target_pairs={{0,1},{1,0},{2,3},{3,2},{4,5},{5,4},{6,7},{7,6},{8,9},{9,8},{10,11... | collective-permute-start | bytes 1032200 | tf_op jit(solution)/shard_map/ppermute | solution.py:690
  509.3 39.1 %all-to-all-start.3 = ((bf16[8,64,1024]{2,1,0:T(8,128)(2,1)}), bf16[8,64,1024]{2,1,0:T(8,128)(2,1)}, u32[]{:S(2)}, u32[]{:S(2)}) async-start(bf16[8,64,1024]{2,1,0:T(8,128)(2,1)} %bitcast.180), calls=%async_computation.3 | async-start | bytes 2097152 | tf_op jit(solution)/shard_map/all_to_all | solution.py:710
  521.3 26.2 %collective-permute-start.63 = (bf16[128,3072]{1,0:T(8,128)(2,1)S(1)}, bf16[128,3072]{1,0:T(8,128)(2,1)S(1)}, u32[]{:S(2)}, u32[]{:S(2)}) collective-permute-start(bf16[128,3072]{1,0:T(8,128)(2,1)S(1)} %ring_add.22), channel_id=1, source_target_pairs={{0,4},{1,3},{4,8},{5,1},{8,12},{9,5},{12,14},{13,9},{14,10},{15,13... | collective-permute-start | bytes 2359304 | tf_op jit(solution)/shard_map/ppermute | solution.py:693
  524.9 27.0 %collective-permute-start.66 = (bf16[128,1024]{1,0:T(8,128)(2,1)S(1)}, bf16[128,1024]{1,0:T(8,128)(2,1)}, u32[]{:S(2)}, u32[]{:S(2)}) collective-permute-start(bf16[128,1024]{1,0:T(8,128)(2,1)S(1)} %ring_add.21), channel_id=1, source_target_pairs={{0,4},{1,3},{4,8},{5,1},{8,12},{9,5},{12,14},{13,9},{14,10},{15,13... | collective-permute-start | bytes 786440 | tf_op jit(solution)/shard_map/ppermute | solution.py:693
  526.1 25.7 %collective-permute-start.72 = (f32[2,1024]{1,0:T(2,128)S(1)}, f32[2,1024]{1,0:T(2,128)S(1)}, u32[]{:S(2)}, u32[]{:S(2)}) collective-permute-start(f32[2,1024]{1,0:T(2,128)S(1)} %add.327), channel_id=1, source_target_pairs={{0,4},{1,5},{2,6},{3,7},{4,0},{5,1},{6,2},{7,3},{8,12},{9,13},{10,... | collective-permute-start | bytes 24584 | tf_op jit(solution)/shard_map/ppermute | solution.py:721
  (137 other events, 1798.3 us)

commit v6 on v5

--- a/solution.py
+++ b/solution.py
@@ -393,7 +393,7 @@
     )(grad, da, dg, h, gains, w_in, w_gate)
 
 
-def attend_back(q, kv_list, dh_low, o, lse, qmarks, kmarks, w_mix, cosine, sine, begin):
+def attend_back(q, kv_list, dh_low, o, lse, qmarks, kmarks, w_mix, cosine, sine, begin, wide=2, ahead=1):
     count = o.shape[1] // LANES
     rows = q.shape[0]
     members = len(kv_list)
@@ -401,66 +401,87 @@
 
     def kernel(q_ref, dh_ref, w_ref, o_ref, lse_ref, qm_ref, km_ref, cos_ref, sin_ref, *refs):
         kv_refs, (dq_ref, *dkv_refs) = refs[:members], refs[members:]
-        k = jnp.concatenate([r[:, :LANES] for r in kv_refs], axis=0)
-        v = jnp.concatenate([r[:, LANES:] for r in kv_refs], axis=0)
-        do = dot(dh_ref[...], w_ref[...], NT).astype(BF)
-        q = q_ref[...] * jnp.asarray(HEAD_DIM**-0.5, BF)
-        prod = do.astype(F32) * o_ref[...].astype(F32)
-        lse = lse_ref[0]
         row = lax.broadcasted_iota(jnp.int32, (LANES, rows), 0)
-        beside = jnp.zeros((LANES, rows), F32)
-        for head in range(2):
-            for n, part in enumerate(split3(-lse[head : head + 1])):
-                beside = jnp.where(row == IDS + n + (HEAD_DIM if head == 0 else 0), part, beside)
-        beside = beside.T.astype(BF) + qm_ref[...]
         lane = lax.broadcasted_iota(jnp.int32, (rows, LANES), 1)
+        first = head_mask((rows, LANES), 0)
+        do_wide = dot(dh_ref[...], w_ref[...], NT).astype(BF)
+        heads = []
+        for w in range(wide):
+            at = slice(w * LANES, (w + 1) * LANES)
+            k = jnp.concatenate([r[:, 2 * w * LANES : (2 * w + 1) * LANES] for r in kv_refs], axis=0)
+            v = jnp.concatenate([r[:, (2 * w + 1) * LANES : (2 * w + 2) * LANES] for r in kv_refs], axis=0)
+            do = do_wide[:, at]
+            q = q_ref[:, at] * jnp.asarray(HEAD_DIM**-0.5, BF)
+            prod = do.astype(F32) * o_ref[:, at].astype(F32)
+            beside = jnp.zeros((LANES, rows), F32)
+            for head in range(2):
+                for n, part in enumerate(split3(-lse_ref[w, head : head + 1])):
+                    beside = jnp.where(row == IDS + n + (HEAD_DIM if head == 0 else 0), part, beside)
+            beside = beside.T.astype(BF) + qm_ref[...]
+            for head in range(2):
+                mine = head_mask((rows, LANES), head)
+                theirs = head_mask((keys, LANES), head)
+                delta = jnp.sum(jnp.where(mine, prod, 0.0), axis=1, keepdims=True)
+                there = jnp.zeros((rows, LANES), F32)
+                for n, part in enumerate(split3(-delta)):
+                    there = jnp.where(lane == IDS + n + (HEAD_DIM if head == 0 else 0), part, there)
+                qh = jnp.where(mine, q, beside)
+                doh = jnp.where(mine, do, there.astype(BF))
+                kh = jnp.where(theirs, k, km_ref[...])
+                vh = jnp.where(theirs, v, km_ref[...])
+                heads.append((q, k, do, qh, doh, kh, vh))
+
+        def score(n):
+            q, k, do, qh, doh, kh, vh = heads[n]
+            return dot(kh, qh, NT), dot(vh, doh, NT)
+
         dks, dvs, dqs = [], [], []
-        for head in range(2):
-            mine = head_mask((rows, LANES), head)
-            theirs = head_mask((keys, LANES), head)
-            delta = jnp.sum(jnp.where(mine, prod, 0.0), axis=1, keepdims=True)
-            there = jnp.zeros((rows, LANES), F32)
-            for n, part in enumerate(split3(-delta)):
-                there = jnp.where(lane == IDS + n + (HEAD_DIM if head == 0 else 0), part, there)
-            qh = jnp.where(mine, q, beside)
-            doh = jnp.where(mine, do, there.astype(BF))
-            kh = jnp.where(theirs, k, km_ref[...])
-            vh = jnp.where(theirs, v, km_ref[...])
-            p = jnp.exp(dot(kh, qh, NT))
-            ds = (p * dot(vh, doh, NT)).astype(BF)
+        waiting = [score(n) for n in range(ahead)]
+        for n, (q, k, do, *_) in enumerate(heads):
+            if n + ahead < len(heads):
+                waiting.append(score(n + ahead))
+            s, dp = waiting[n]
+            p = jnp.exp(s)
+            ds = (p * dp).astype(BF)
             dvs.append(dot(p.astype(BF), do, NN))
             dks.append(dot(ds, q, NN))
             dqs.append(dot(ds, k, TN))
-        first = head_mask((rows, LANES), 0)
-        dq = jnp.where(first, dqs[0], dqs[1])
-        dq = rope_block(dq * HEAD_DIM**-0.5, cos_ref[...], -sin_ref[...])
-        dq_ref[...] = dq.astype(BF)
-        for m, out in enumerate(dkv_refs):
-            cut = slice(m * rows, (m + 1) * rows)
-            out[:, :LANES] = jnp.where(first, dks[0][cut], dks[1][cut]).astype(BF)
-            out[:, LANES:] = jnp.where(first, dvs[0][cut], dvs[1][cut]).astype(BF)
-
-    spec = pl.BlockSpec((rows, LANES), lambda p: (0, p))
-    kv_spec = pl.BlockSpec((rows, 2 * LANES), lambda p: (0, p))
+        for w in range(wide):
+            at = slice(w * LANES, (w + 1) * LANES)
+            a, b = 2 * w, 2 * w + 1
+            dq = jnp.where(first, dqs[a], dqs[b])
+            dq = rope_block(dq * HEAD_DIM**-0.5, cos_ref[...], -sin_ref[...])
+            dq_ref[:, at] = dq.astype(BF)
+            for m, out in enumerate(dkv_refs):
+                cut = slice(m * rows, (m + 1) * rows)
+                low = slice(2 * w * LANES, (2 * w + 1) * LANES)
+                high = slice((2 * w + 1) * LANES, (2 * w + 2) * LANES)
+                out[:, low] = jnp.where(first, dks[a][cut], dks[b][cut]).astype(BF)
+                out[:, high] = jnp.where(first, dvs[a][cut], dvs[b][cut]).astype(BF)
+
+    start = begin // wide
+    spec = pl.BlockSpec((rows, wide * LANES), lambda p: (0, p))
+    kv_spec = pl.BlockSpec((rows, 2 * wide * LANES), lambda p: (0, p))
     results = call(
         kernel,
         "attend_back",
+        limit=28,
         flops=20 * rows * keys * count * LANES,
         moved=2 * (6 * rows + 4 * keys) * count * LANES,
         exps=rows * keys * 2 * count,
-        grid=(count,),
+        grid=(count // wide,),
         in_specs=[
-            pl.BlockSpec((rows, LANES), lambda p: (0, begin + p)),
+            pl.BlockSpec((rows, wide * LANES), lambda p: (0, start + p)),
             whole((rows, D)),
-            pl.BlockSpec((LANES, D), lambda p: (begin + p, 3)),
+            pl.BlockSpec((wide * LANES, D), lambda p: (start + p, 3)),
             spec,
-            pl.BlockSpec((1, 2, rows), lambda p: (p, 0, 0)),
+            pl.BlockSpec((wide, 2, rows), lambda p: (p, 0, 0)),
             whole((rows, LANES)),
             whole((keys, LANES)),
             whole((rows, LANES)),
             whole((rows, LANES)),
         ]
-        + [pl.BlockSpec((rows, 2 * LANES), lambda p: (0, begin + p))] * members,
+        + [pl.BlockSpec((rows, 2 * wide * LANES), lambda p: (0, start + p))] * members,
         out_specs=[spec] + [kv_spec] * members,
         out_shape=[shaped((rows, count * LANES))] + [shaped((rows, 2 * count * LANES))] * members,
     )(q, dh_low, w_mix, o, lse, qmarks, kmarks, cosine, sine, *kv_list)

time: 588 us -> 586 us (level)
  no operation moved by 1% of the time
where the time goes in v6:
time: 586 us; the launch traced here: 576 us
  Pallas kernels  233 us (40%)
  waiting for transfers between devices  159 us (27%)
  starting transfers between devices  83.6 us (14%)
  local copies, waits for them, and re-layouts  59.3 us (10%)
  other arithmetic  30.5 us (5%)
  blocking collectives  8.43 us (1%)
    ppermute x32, waiting for transfers between devices, step(): return lax.ppermute(array, BOTH, self.ring_pairs)  112 us
    pallas_call x5, Pallas kernels, attend_back(): call(kernel, 'attend_back', limit=28, flops=20 * rows * keys * count * LA...  57.5 us
    ppermute x2, waiting for transfers between devices, handed(): return lax.ppermute(array, 'section', pairs)  36.7 us
    pallas_call x8, Pallas kernels, weight_rows(): call(kernel, 'weight_rows', limit=max(8, 4 + int(1.25 * size) // (1024 *...  32.9 us
    ppermute x32, starting transfers between devices, step(): return lax.ppermute(array, BOTH, self.ring_pairs)  29.6 us
    unnamed x189, local copies, waits for them, and re-layouts  27 us
    ppermute x29, starting transfers between devices, swap(): return lax.ppermute(array, 'wshard', [(0, 1), (1, 0)])  26.3 us
    pallas_call x2, Pallas kernels, attend(): call(kernel, 'attend', limit=28, flops=8 * rows * keys * count * LANES, m...  25.3 us
  transfers between devices with their start and end apart: 77, of which 19 were waited for; matrix products, arithmetic and copies ran while one was open for 10% of the time, Pallas kernels for 23%

profile of v6, /device:TPU:13, one launch (start us, length us, event | category | flops | bytes accessed | tf_op | source)
XLA Modules:
  0.0 576.3 jit_solution(16745741804777807264)
XLA Ops:
  24.5 7.6 %collective-permute-done.2 = bf16[128,4224]{1,0:T(8,128)(2,1)} collective-permute-done((bf16[128,4224]{1,0:T(8,128)(2,1)S(1)}, bf16[128,4224]{1,0:T(8,128)(2,1)}, u32[]{:S(2)}, u32[]{:S(2)}) %collective-permute-start.2) | collective-permute-done | bytes 1081376 | tf_op jit(solution)/shard_map/ppermute | solution.py:714
  32.0 5.7 all-to-all-start.1
  51.5 28.4 %collective-permute-done.13 = bf16[128,2688]{1,0:T(8,128)(2,1)S(1)} collective-permute-done((bf16[128,2688]{1,0:T(8,128)(2,1)S(1)}, bf16[128,2688]{1,0:T(8,128)(2,1)S(1)}, u32[]{:S(2)}, u32[]{:S(2)}) %collective-permute-start.13) | collective-permute-done | bytes 688160 | tf_op jit(solution)/shard_map/ppermute | solution.py:714
  111.9 5.3 collective-permute-done.15
  124.9 6.3 %keys_values.2 = (bf16[512,1024]{1,0:T(8,128)(2,1)S(1)}, bf16[512,2048]{1,0:T(8,128)(2,1)S(1)}) custom-call(bf16[512,1024]{1,0:T(8,128)(2,1)S(1)} %bitcast.168, f32[8,1024]{1,0:T(8,128)S(1)} %gains.1.gain_ref, bf16[1024,4224]{1,0:T(8,128)(2,1)} %bitcast.19.w_ref.wkv_ref.wq_ref, f32[512,128]{1,0:T(8,128)S(1)} %get-tuple-element.254.cos_ref, ...), custom_call_target="tpu_custom_call" | custom-call | flops 2147483648 | bytes 8388608 | tf_op jit(solution)/shard_map/keys_values/pallas_call | solution.py:129
  140.9 12.9 %attend.2 = (bf16[512,1024]{1,0:T(8,128)(2,1)S(1)}, f32[8,2,512]{2,1,0:T(2,128)}) custom-call(bf16[512,1024]{1,0:T(8,128)(2,1)S(1)} %queries.2.q_ref, bf16[512,128]{1,0:T(8,128)(2,1)S(1)} %select_convert_fusion.1.qm_ref, bf16[1024,128]{1,0:T(8,128)(2,1)S(1)} %select_convert_fusion.km_ref, bf16[512,2048]{1,0:T(8,128)(2,1)S(1)} %get-tuple-element.112.refs_0_, ...), custom_call_target="tpu_custom_call" | custom-call | flops 4294967296 | bytes 6291456 | tf_op jit(solution)/shard_map/attend/pallas_call | solution.py:225
  160.2 8.1 %collective-permute-done.30 = bf16[64,2688]{1,0:T(8,128)(2,1)S(1)} collective-permute-done((bf16[64,2688]{1,0:T(8,128)(2,1)S(1)}, bf16[64,2688]{1,0:T(8,128)(2,1)S(1)}, u32[]{:S(2)}, u32[]{:S(2)}) %collective-permute-start.30) | collective-permute-done | bytes 344096 | tf_op jit(solution)/shard_map/ppermute | solution.py:714
  176.8 8.9 %ffn_in.2.z_ref = bf16[512,2688]{1,0:T(8,128)(2,1)S(1)} custom-call(bf16[512,1024]{1,0:T(8,128)(2,1)S(1)} %get-tuple-element.118.b_ref, bf16[1024,2688]{1,0:T(8,128)(2,1)} %bitcast.36.wa_ref, bf16[1024,2688]{1,0:T(8,128)(2,1)S(1)} %bitcast.174), custom_call_target="tpu_custom_call" | custom-call | flops 5637144576 | bytes 14811136 | tf_op jit(solution)/shard_map/ffn_in/pallas_call | solution.py:303
  194.7 21.2 %collective-permute-done.38 = bf16[512,1024]{1,0:T(8,128)(2,1)} collective-permute-done((bf16[512,1024]{1,0:T(8,128)(2,1)S(1)}, bf16[512,1024]{1,0:T(8,128)(2,1)}, u32[]{:S(2)}, u32[]{:S(2)}) %collective-permute-start.38) | collective-permute-done | bytes 1048608 | tf_op jit(solution)/shard_map/ppermute | solution.py:1026
  216.0 6.4 %keys_values.3 = (bf16[512,1024]{1,0:T(8,128)(2,1)S(1)}, bf16[512,2048]{1,0:T(8,128)(2,1)S(1)}) custom-call(bf16[512,1024]{1,0:T(8,128)(2,1)S(1)} %broadcast_select_fusion.2.x_ref, f32[8,1024]{1,0:T(8,128)S(1)} %gains.1.gain_ref, bf16[1024,4224]{1,0:T(8,128)(2,1)} %bitcast.19.w_ref.wkv_ref.wq_ref, f32[512,128]{1,0:T(8,128)S(1)} %get-tuple-element.254.cos_ref, ...), custom_call_target="tpu_custom_call" | custom-call | flops 2147483648 | bytes 8388608 | tf_op jit(solution)/shard_map/keys_values/pallas_call | solution.py:129
  227.3 12.4 %attend.3 = (bf16[512,1024]{1,0:T(8,128)(2,1)S(1)}, f32[8,2,512]{2,1,0:T(2,128)S(1)}) custom-call(bf16[512,1024]{1,0:T(8,128)(2,1)S(1)} %queries.3.q_ref, bf16[512,128]{1,0:T(8,128)(2,1)S(1)} %select_convert_fusion.1.qm_ref, bf16[1024,128]{1,0:T(8,128)(2,1)S(1)} %select_convert_fusion.km_ref, bf16[512,2048]{1,0:T(8,128)(2,1)S(1)} %get-tuple-element.120.refs_0_, ...), custom_call_target="tpu_custom_call" | custom-call | flops 4294967296 | bytes 6291456 | tf_op jit(solution)/shard_map/attend/pallas_call | solution.py:225
  243.5 10.5 %ffn_in.3 = (bf16[512,2688]{1,0:T(8,128)(2,1)S(1)}, bf16[512,2688]{1,0:T(8,128)(2,1)S(1)}, bf16[512,2688]{1,0:T(8,128)(2,1)S(1)}) custom-call(bf16[512,1024]{1,0:T(8,128)(2,1)S(1)} %get-tuple-element.141.b_ref.refs_0_, bf16[1024,2688]{1,0:T(8,128)(2,1)} %bitcast.36.wa_ref, bf16[1024,2688]{1,0:T(8,128)(2,1)S(1)} %bitcast.177), custom_call_target="tpu_custom_call" | custom-call | flops 5637144576 | bytes 20316160 | tf_op jit(solution)/shard_map/ffn_in/pallas_call | solution.py:303
  255.6 5.3 ffn_back.2
  260.9 10.3 %hidden_back.2 = (f32[512,1024]{1,0:T(8,128)S(1)}, bf16[512,1024]{1,0:T(8,128)(2,1)S(1)}, f32[1,1024]{1,0:T(1,128)}) custom-call(bf16[512,1024]{1,0:T(8,128)(2,1)S(1)} %bitcast.171, bf16[512,2688]{1,0:T(8,128)(2,1)S(1)} %get-tuple-element.125.da_ref, bf16[512,2688]{1,0:T(8,128)(2,1)S(1)} %get-tuple-element.126.dg_ref, ...), custom_call_target="tpu_custom_call" | custom-call | flops 5637144576 | bytes 22806528 | tf_op jit(solution)/shard_map/hidden_back/pallas_call | solution.py:377
  271.2 27.4 %attend_back.5 = (bf16[512,1024]{1,0:T(8,128)(2,1)S(1)}, bf16[512,2048]{1,0:T(8,128)(2,1)S(1)}, bf16[512,2048]{1,0:T(8,128)(2,1)S(1)}) custom-call(bf16[512,1024]{1,0:T(8,128)(2,1)S(1)} %queries.3.q_ref, bf16[512,1024]{1,0:T(8,128)(2,1)S(1)} %get-tuple-element.129.dh_ref, bf16[1024,4224]{1,0:T(8,128)(2,1)} %bitcast.19.w_ref.wkv_ref.wq_ref, ...), custom_call_target="tpu_custom_call" | custom-call | flops 10737418240 | bytes 14680064 | tf_op jit(solution)/shard_map/attend_back/pallas_call | solution.py:465
  305.4 8.2 %input_back.2 = (bf16[512,1024]{1,0:T(8,128)(2,1)S(1)}, f32[1,1024]{1,0:T(1,128)}) custom-call(bf16[512,1024]{1,0:T(8,128)(2,1)S(1)} %broadcast_select_fusion.2.x_ref, f32[512,1024]{1,0:T(8,128)S(1)} %get-tuple-element.128.dh_ref, f32[8,1024]{1,0:T(8,128)S(1)} %gains.1.gain_ref, bf16[1024,4224]{1,0:T(8,128)(2,1)} %bitcast.19.w_ref.wkv_ref.wq_ref, ...), custom_call_target="tpu_custom_call" | custom-call | flops 3221225472 | bytes 16777216 | tf_op jit(solution)/shard_map/input_back/pallas_call | solution.py:542
  326.0 15.6 %collective-permute-done.41 = bf16[512,1024]{1,0:T(8,128)(2,1)} collective-permute-done((bf16[512,1024]{1,0:T(8,128)(2,1)S(1)}, bf16[512,1024]{1,0:T(8,128)(2,1)}, u32[]{:S(2)}, u32[]{:S(2)}) %collective-permute-start.41) | collective-permute-done | bytes 1048608 | tf_op jit(solution)/shard_map/ppermute | solution.py:1026
  343.0 5.3 ffn_back.3
  348.3 5.8 %weight_rows.8 = bf16[448,5376]{1,0:T(8,128)(2,1)} custom-call(s32[7]{0:T(128)S(1)} %stack.75.order_ref, bf16[512,1024]{1,0:T(8,128)(2,1)S(1)} %copy-done.68, bf16[512,2688]{1,0:T(8,128)(2,1)S(1)} %get-tuple-element.137.refs_1_.da_ref, bf16[512,2688]{1,0:T(8,128)(2,1)S(1)} %get-tuple-element.139.refs_2_.dg_ref), custom_call_target="tpu_custom_call" | custom-call | flops 2466250752 | bytes 11370496 | tf_op jit(solution)/shard_map/weight_rows/pallas_call | solution.py:613
  366.0 6.3 %weight_rows.10 = (bf16[64,5376]{1,0:T(8,128)(2,1)S(1)}, bf16[512,5376]{1,0:T(8,128)(2,1)S(1)}) custom-call(s32[9]{0:T(128)S(1)} %stack.67.order_ref, bf16[512,1024]{1,0:T(8,128)(2,1)S(1)} %copy-done.69, bf16[512,2688]{1,0:T(8,128)(2,1)S(1)} %get-tuple-element.137.refs_1_.da_ref, bf16[512,2688]{1,0:T(8,128)(2,1)S(1)} %copy-done.49, ...), custom_call_target="tpu_custom_call" | custom-call | flops 3170893824 | bytes 17563648 | tf_op jit(solution)/shard_map/weight_rows/pallas_call | solution.py:613
  373.3 6.0 %weight_rows.11 = (bf16[64,2688]{1,0:T(8,128)(2,1)S(1)}, bf16[512,2688]{1,0:T(8,128)(2,1)S(1)}) custom-call(s32[9]{0:T(128)S(1)} %stack.67.order_ref, bf16[512,1024]{1,0:T(8,128)(2,1)S(1)} %copy-done.18, bf16[512,2688]{1,0:T(8,128)(2,1)S(1)} %copy-done.16, bf16[448,2688]{1,0:T(8,128)(2,1)} %collective-permute-done.43.refs_2_), custom_call_target="tpu_custom_call" | custom-call | flops 1585446912 | bytes 9306112 | tf_op jit(solution)/shard_map/weight_rows/pallas_call | solution.py:613
  382.8 9.5 %hidden_back.3 = (f32[512,1024]{1,0:T(8,128)S(1)}, bf16[512,1024]{1,0:T(8,128)(2,1)S(1)}, f32[1,1024]{1,0:T(1,128)S(1)}) custom-call(bf16[512,1024]{1,0:T(8,128)(2,1)S(1)} %copy-done.18, bf16[512,2688]{1,0:T(8,128)(2,1)S(1)} %copy-done.47, bf16[512,2688]{1,0:T(8,128)(2,1)S(1)} %copy-done.50, f32[512,1024]{1,0:T(8,128)S(1)} %copy-done.63, ...), custom_call_target="tpu_custom_call" | custom-call | flops 5637144576 | bytes 22806528 | tf_op jit(solution)/shard_map/hidden_back/pallas_call | solution.py:377
  398.8 7.5 %attend_back.6 = (bf16[512,256]{1,0:T(8,128)(2,1)S(1)}, bf16[512,512]{1,0:T(8,128)(2,1)S(1)}, bf16[512,512]{1,0:T(8,128)(2,1)S(1)}) custom-call(bf16[512,1024]{1,0:T(8,128)(2,1)S(1)} %copy-done.12, bf16[512,1024]{1,0:T(8,128)(2,1)S(1)} %get-tuple-element.152.refs_1_.dh_ref, bf16[1024,4224]{1,0:T(8,128)(2,1)} %bitcast.19.w_ref.wkv_ref.wq_ref, ...), custom_call_target="tpu_custom_call" | custom-call | flops 2684354560 | bytes 3670016 | tf_op jit(solution)/shard_map/attend_back/pallas_call | solution.py:465
  409.1 7.5 %attend_back.7 = (bf16[512,256]{1,0:T(8,128)(2,1)S(1)}, bf16[512,512]{1,0:T(8,128)(2,1)S(1)}, bf16[512,512]{1,0:T(8,128)(2,1)S(1)}) custom-call(bf16[512,1024]{1,0:T(8,128)(2,1)S(1)} %copy-done.12, bf16[512,1024]{1,0:T(8,128)(2,1)S(1)} %get-tuple-element.152.refs_1_.dh_ref, bf16[1024,4224]{1,0:T(8,128)(2,1)} %bitcast.19.w_ref.wkv_ref.wq_ref, ...), custom_call_target="tpu_custom_call" | custom-call | flops 2684354560 | bytes 3670016 | tf_op jit(solution)/shard_map/attend_back/pallas_call | solution.py:465
  420.8 7.5 %attend_back.8 = (bf16[512,256]{1,0:T(8,128)(2,1)S(1)}, bf16[512,512]{1,0:T(8,128)(2,1)S(1)}, bf16[512,512]{1,0:T(8,128)(2,1)S(1)}) custom-call(bf16[512,1024]{1,0:T(8,128)(2,1)S(1)} %copy-done.12, bf16[512,1024]{1,0:T(8,128)(2,1)S(1)} %get-tuple-element.152.refs_1_.dh_ref, bf16[1024,4224]{1,0:T(8,128)(2,1)} %bitcast.19.w_ref.wkv_ref.wq_ref, ...), custom_call_target="tpu_custom_call" | custom-call | flops 2684354560 | bytes 3670016 | tf_op jit(solution)/shard_map/attend_back/pallas_call | solution.py:465
  430.2 7.7 %attend_back.9 = (bf16[512,256]{1,0:T(8,128)(2,1)S(1)}, bf16[512,512]{1,0:T(8,128)(2,1)S(1)}, bf16[512,512]{1,0:T(8,128)(2,1)S(1)}) custom-call(bf16[512,1024]{1,0:T(8,128)(2,1)S(1)} %copy-done.12, bf16[512,1024]{1,0:T(8,128)(2,1)S(1)} %get-tuple-element.152.refs_1_.dh_ref, bf16[1024,4224]{1,0:T(8,128)(2,1)} %bitcast.19.w_ref.wkv_ref.wq_ref, ...), custom_call_target="tpu_custom_call" | custom-call | flops 2684354560 | bytes 3670016 | tf_op jit(solution)/shard_map/attend_back/pallas_call | solution.py:465
  446.7 9.1 %collective-permute-done.52.moving_ref = bf16[128,5376]{1,0:T(8,128)(2,1)} collective-permute-done((bf16[128,5376]{1,0:T(8,128)(2,1)}, bf16[128,5376]{1,0:T(8,128)(2,1)}, u32[]{:S(2)}, u32[]{:S(2)}) %collective-permute-start.52) | collective-permute-done | bytes 1376288 | tf_op jit(solution)/shard_map/ppermute | solution.py:714
  468.2 7.4 %input_back.3 = (bf16[512,1024]{1,0:T(8,128)(2,1)S(1)}, f32[1,1024]{1,0:T(1,128)S(1)}) custom-call(bf16[512,1024]{1,0:T(8,128)(2,1)S(1)} %copy-done.10, f32[512,1024]{1,0:T(8,128)S(1)} %copy-done.60, f32[8,1024]{1,0:T(8,128)S(1)} %copy-done.66, bf16[1024,4224]{1,0:T(8,128)(2,1)} %bitcast.19.w_ref.wkv_ref.wq_ref, ...), custom_call_target="tpu_custom_call" | custom-call | flops 3221225472 | bytes 16777216 | tf_op jit(solution)/shard_map/input_back/pallas_call | solution.py:542
  477.3 10.7 %collective-permute-done.60 = bf16[128,2688]{1,0:T(8,128)(2,1)S(1)} collective-permute-done((bf16[128,2688]{1,0:T(8,128)(2,1)S(1)}, bf16[128,2688]{1,0:T(8,128)(2,1)S(1)}, u32[]{:S(2)}, u32[]{:S(2)}) %collective-permute-start.60) | collective-permute-done | bytes 688160 | tf_op jit(solution)/shard_map/ppermute | solution.py:714
  507.1 5.3 all-to-all-start.3
  524.7 20.4 %collective-permute-done.63.moving_ref = bf16[128,3072]{1,0:T(8,128)(2,1)S(1)} collective-permute-done((bf16[128,3072]{1,0:T(8,128)(2,1)S(1)}, bf16[128,3072]{1,0:T(8,128)(2,1)S(1)}, u32[]{:S(2)}, u32[]{:S(2)}) %collective-permute-start.63) | collective-permute-done | bytes 786464 | tf_op jit(solution)/shard_map/ppermute | solution.py:714
  553.5 5.4 collective-permute-done.64
  (481 shorter events, 251.7 us)
Async XLA Ops:
  13.9 18.2 %collective-permute-start.2 = (bf16[128,4224]{1,0:T(8,128)(2,1)S(1)}, bf16[128,4224]{1,0:T(8,128)(2,1)}, u32[]{:S(2)}, u32[]{:S(2)}) collective-permute-start(bf16[128,4224]{1,0:T(8,128)(2,1)S(1)} %pad_maximum_fusion), channel_id=1, source_target_pairs={{0,4},{1,3},{4,8},{5,1},{8,12},{9,5},{12,14},{13,9},{14,10},{15,13... | collective-permute-start | bytes 3244040 | tf_op jit(solution)/shard_map/ppermute | solution.py:714
  21.6 20.9 %collective-permute-start.12 = (bf16[128,2688]{1,0:T(8,128)(2,1)}, bf16[128,2688]{1,0:T(8,128)(2,1)S(1)}, u32[]{:S(2)}, u32[]{:S(2)}) collective-permute-start(bf16[128,2688]{1,0:T(8,128)(2,1)} %collective-permute-done.3), channel_id=1, source_target_pairs={{0,4},{1,3},{4,8},{5,1},{8,12},{9,5},{12,14},{13,9},{14,10},{15,13... | collective-permute-start | bytes 2064392 | tf_op jit(solution)/shard_map/ppermute | solution.py:714
  21.9 21.7 %collective-permute-start.23 = (bf16[128,2688]{1,0:T(8,128)(2,1)}, bf16[128,2688]{1,0:T(8,128)(2,1)}, u32[]{:S(2)}, u32[]{:S(2)}) collective-permute-start(bf16[128,2688]{1,0:T(8,128)(2,1)} %collective-permute-done.3), channel_id=1, source_target_pairs={{0,1},{1,0},{2,3},{3,2},{4,5},{5,4},{6,7},{7,6},{8,9},{9,8},{10,11... | collective-permute-start | bytes 2064392 | tf_op jit(solution)/shard_map/ppermute | solution.py:711
  32.0 57.5 %all-to-all-start.1 = ((bf16[8,64,1024]{2,1,0:T(8,128)(2,1)}), bf16[8,64,1024]{2,1,0:T(8,128)(2,1)S(1)}, u32[]{:S(2)}, u32[]{:S(2)}) async-start(bf16[8,64,1024]{2,1,0:T(8,128)(2,1)} %bitcast.9), calls=%async_computation.1 | async-start | bytes 2097152 | tf_op jit(solution)/shard_map/all_to_all | solution.py:728
  39.6 45.0 %collective-permute-start.4 = (bf16[128,4224]{1,0:T(8,128)(2,1)}, bf16[128,4224]{1,0:T(8,128)(2,1)S(1)}, u32[]{:S(2)}, u32[]{:S(2)}) collective-permute-start(bf16[128,4224]{1,0:T(8,128)(2,1)} %collective-permute-done.2), channel_id=1, source_target_pairs={{0,1},{1,0},{2,3},{3,2},{4,5},{5,4},{6,7},{7,6},{8,9},{9,8},{10,11... | collective-permute-start | bytes 3244040 | tf_op jit(solution)/shard_map/ppermute | solution.py:711
  42.4 41.6 %collective-permute-start.5 = (bf16[128,4224]{1,0:T(8,128)(2,1)}, bf16[128,4224]{1,0:T(8,128)(2,1)}, u32[]{:S(2)}, u32[]{:S(2)}) collective-permute-start(bf16[128,4224]{1,0:T(8,128)(2,1)} %collective-permute-done.2), channel_id=1, source_target_pairs={{0,4},{1,3},{4,8},{5,1},{8,12},{9,5},{12,14},{13,9},{14,10},{15,13... | collective-permute-start | bytes 3244040 | tf_op jit(solution)/shard_map/ppermute | solution.py:714
  43.6 36.3 %collective-permute-start.13 = (bf16[128,2688]{1,0:T(8,128)(2,1)S(1)}, bf16[128,2688]{1,0:T(8,128)(2,1)S(1)}, u32[]{:S(2)}, u32[]{:S(2)}) collective-permute-start(bf16[128,2688]{1,0:T(8,128)(2,1)S(1)} %collective-permute-done.12), channel_id=1, source_target_pairs={{0,4},{1,3},{4,8},{5,1},{8,12},{9,5},{12,14},{13,9},{14,10},{15,13... | collective-permute-start | bytes 2064392 | tf_op jit(solution)/shard_map/ppermute | solution.py:714
  47.8 34.4 %collective-permute-start.24 = (bf16[128,2688]{1,0:T(8,128)(2,1)S(1)}, bf16[128,2688]{1,0:T(8,128)(2,1)S(1)}, u32[]{:S(2)}, u32[]{:S(2)}) collective-permute-start(bf16[128,2688]{1,0:T(8,128)(2,1)S(1)} %collective-permute-done.12), channel_id=1, source_target_pairs={{0,1},{1,0},{2,3},{3,2},{4,5},{5,4},{6,7},{7,6},{8,9},{9,8},{10,11... | collective-permute-start | bytes 2064392 | tf_op jit(solution)/shard_map/ppermute | solution.py:711
  110.8 24.3 %collective-permute-start.18 = (bf16[128,2688]{1,0:T(8,128)(2,1)}, bf16[128,2688]{1,0:T(8,128)(2,1)S(1)}, u32[]{:S(2)}, u32[]{:S(2)}) collective-permute-start(bf16[128,2688]{1,0:T(8,128)(2,1)} %pad_maximum_fusion.3), channel_id=1, source_target_pairs={{0,4},{1,3},{4,8},{5,1},{8,12},{9,5},{12,14},{13,9},{14,10},{15,13... | collective-permute-start | bytes 2064392 | tf_op jit(solution)/shard_map/ppermute | solution.py:714
  117.3 19.9 %collective-permute-start.19 = (bf16[128,2688]{1,0:T(8,128)(2,1)S(1)}, bf16[128,2688]{1,0:T(8,128)(2,1)S(1)}, u32[]{:S(2)}, u32[]{:S(2)}) collective-permute-start(bf16[128,2688]{1,0:T(8,128)(2,1)S(1)} %collective-permute-done.15), channel_id=1, source_target_pairs={{0,4},{1,3},{4,8},{5,1},{8,12},{9,5},{12,14},{13,9},{14,10},{15,13... | collective-permute-start | bytes 2064392 | tf_op jit(solution)/shard_map/ppermute | solution.py:714
  119.1 19.1 %collective-permute-start.27 = (bf16[128,2688]{1,0:T(8,128)(2,1)S(1)}, bf16[128,2688]{1,0:T(8,128)(2,1)S(1)}, u32[]{:S(2)}, u32[]{:S(2)}) collective-permute-start(bf16[128,2688]{1,0:T(8,128)(2,1)S(1)} %collective-permute-done.15), channel_id=1, source_target_pairs={{0,1},{1,0},{2,3},{3,2},{4,5},{5,4},{6,7},{7,6},{8,9},{9,8},{10,11... | collective-permute-start | bytes 2064392 | tf_op jit(solution)/shard_map/ppermute | solution.py:711
  135.1 19.2 %collective-permute-start.21 = (bf16[128,2688]{1,0:T(8,128)(2,1)S(1)}, bf16[128,2688]{1,0:T(8,128)(2,1)S(1)}, u32[]{:S(2)}, u32[]{:S(2)}) collective-permute-start(bf16[128,2688]{1,0:T(8,128)(2,1)S(1)} %collective-permute-done.18), channel_id=1, source_target_pairs={{0,4},{1,3},{4,8},{5,1},{8,12},{9,5},{12,14},{13,9},{14,10},{15,13... | collective-permute-start | bytes 2064392 | tf_op jit(solution)/shard_map/ppermute | solution.py:714
  153.9 17.2 %collective-permute-start.29 = (bf16[128,2688]{1,0:T(8,128)(2,1)S(1)}, bf16[128,2688]{1,0:T(8,128)(2,1)S(1)}, u32[]{:S(2)}, u32[]{:S(2)}) collective-permute-start(bf16[128,2688]{1,0:T(8,128)(2,1)S(1)} %collective-permute-done.22), channel_id=1, source_target_pairs={{0,1},{1,0},{2,3},{3,2},{4,5},{5,4},{6,7},{7,6},{8,9},{9,8},{10,11... | collective-permute-start | bytes 2064392 | tf_op jit(solution)/shard_map/ppermute | solution.py:711
  190.2 25.7 %collective-permute-start.38 = (bf16[512,1024]{1,0:T(8,128)(2,1)S(1)}, bf16[512,1024]{1,0:T(8,128)(2,1)}, u32[]{:S(2)}, u32[]{:S(2)}) collective-permute-start(bf16[512,1024]{1,0:T(8,128)(2,1)S(1)} %ffn_out.2), channel_id=1, source_target_pairs={{0,16},{1,17},{2,18},{3,19},{4,20},{5,21},{6,22},{7,23},{8,24},{9,... | collective-permute-start | bytes 3145736 | tf_op jit(solution)/shard_map/ppermute | solution.py:1026
  313.5 28.0 %collective-permute-start.41 = (bf16[512,1024]{1,0:T(8,128)(2,1)S(1)}, bf16[512,1024]{1,0:T(8,128)(2,1)}, u32[]{:S(2)}, u32[]{:S(2)}) collective-permute-start(bf16[512,1024]{1,0:T(8,128)(2,1)S(1)} %get-tuple-element.134), channel_id=1, source_target_pairs={{16,0},{17,1},{18,2},{19,3},{20,4},{21,5},{22,6},{23,7},{24,8},{25... | collective-permute-start | bytes 3145736 | tf_op jit(solution)/shard_map/ppermute | solution.py:1026
  372.4 19.9 %collective-permute-start.45 = (bf16[64,5376]{1,0:T(8,128)(2,1)S(1)}, bf16[64,5376]{1,0:T(8,128)(2,1)S(1)}, u32[]{:S(2)}, u32[]{:S(2)}) collective-permute-start(bf16[64,5376]{1,0:T(8,128)(2,1)S(1)} %get-tuple-element.142), channel_id=1, source_target_pairs={{0,4},{1,3},{4,8},{5,1},{8,12},{9,5},{12,14},{13,9},{14,10},{15,13... | collective-permute-start | bytes 2064392 | tf_op jit(solution)/shard_map/ppermute | solution.py:714
  393.6 23.5 %collective-permute-start.49 = (bf16[128,5376]{1,0:T(8,128)(2,1)S(1)}, bf16[128,5376]{1,0:T(8,128)(2,1)S(1)}, u32[]{:S(2)}, u32[]{:S(2)}) collective-permute-start(bf16[128,5376]{1,0:T(8,128)(2,1)S(1)} %ring_add.12), channel_id=1, source_target_pairs={{0,4},{1,3},{4,8},{5,1},{8,12},{9,5},{12,14},{13,9},{14,10},{15,13... | collective-permute-start | bytes 4128776 | tf_op jit(solution)/shard_map/ppermute | solution.py:714
  397.4 21.1 %collective-permute-start.48 = (bf16[128,2688]{1,0:T(8,128)(2,1)S(1)}, bf16[128,2688]{1,0:T(8,128)(2,1)S(1)}, u32[]{:S(2)}, u32[]{:S(2)}) collective-permute-start(bf16[128,2688]{1,0:T(8,128)(2,1)S(1)} %ring_add.13), channel_id=1, source_target_pairs={{0,4},{1,3},{4,8},{5,1},{8,12},{9,5},{12,14},{13,9},{14,10},{15,13... | collective-permute-start | bytes 2064392 | tf_op jit(solution)/shard_map/ppermute | solution.py:714
  406.3 32.2 %collective-permute-start.53 = (bf16[512,512]{1,0:T(8,128)(2,1)S(1)}, bf16[512,512]{1,0:T(8,128)(2,1)S(1)}, u32[]{:S(2)}, u32[]{:S(2)}) collective-permute-start(bf16[512,512]{1,0:T(8,128)(2,1)S(1)} %get-tuple-element.169), channel_id=1, source_target_pairs={{0,1},{1,0},{2,3},{3,2},{4,5},{5,4},{6,7},{7,6},{8,9},{9,8},{10,11... | collective-permute-start | bytes 1572872 | tf_op jit(solution)/shard_map/ppermute | solution.py:760
  416.6 22.4 %collective-permute-start.54 = (bf16[512,512]{1,0:T(8,128)(2,1)S(1)}, bf16[512,512]{1,0:T(8,128)(2,1)S(1)}, u32[]{:S(2)}, u32[]{:S(2)}) collective-permute-start(bf16[512,512]{1,0:T(8,128)(2,1)S(1)} %get-tuple-element.171), channel_id=1, source_target_pairs={{0,1},{1,0},{2,3},{3,2},{4,5},{5,4},{6,7},{7,6},{8,9},{9,8},{10,11... | collective-permute-start | bytes 1572872 | tf_op jit(solution)/shard_map/ppermute | solution.py:760
  438.0 17.8 %collective-permute-start.52 = (bf16[128,5376]{1,0:T(8,128)(2,1)}, bf16[128,5376]{1,0:T(8,128)(2,1)}, u32[]{:S(2)}, u32[]{:S(2)}) collective-permute-start(bf16[128,5376]{1,0:T(8,128)(2,1)} %ring_add.14), channel_id=1, source_target_pairs={{0,4},{1,3},{4,8},{5,1},{8,12},{9,5},{12,14},{13,9},{14,10},{15,13... | collective-permute-start | bytes 4128776 | tf_op jit(solution)/shard_map/ppermute | solution.py:714
  444.5 48.0 %collective-permute-start.57 = (bf16[448,3072]{1,0:T(8,128)(2,1)}, bf16[448,3072]{1,0:T(8,128)(2,1)}, u32[]{:S(2)}, u32[]{:S(2)}) collective-permute-start(bf16[448,3072]{1,0:T(8,128)(2,1)} %weight_rows.14), channel_id=1, source_target_pairs={{0,1},{1,0},{2,3},{3,2},{4,5},{5,4},{6,7},{7,6},{8,9},{9,8},{10,11... | collective-permute-start | bytes 8257544 | tf_op jit(solution)/shard_map/ppermute | solution.py:711
  445.3 17.8 %collective-permute-start.51 = (bf16[128,2688]{1,0:T(8,128)(2,1)}, bf16[128,2688]{1,0:T(8,128)(2,1)S(1)}, u32[]{:S(2)}, u32[]{:S(2)}) collective-permute-start(bf16[128,2688]{1,0:T(8,128)(2,1)} %ring_add.15), channel_id=1, source_target_pairs={{0,4},{1,3},{4,8},{5,1},{8,12},{9,5},{12,14},{13,9},{14,10},{15,13... | collective-permute-start | bytes 2064392 | tf_op jit(solution)/shard_map/ppermute | solution.py:714
  446.3 19.7 %collective-permute-start.50 = (bf16[128,1024]{1,0:T(8,128)(2,1)}, bf16[128,1024]{1,0:T(8,128)(2,1)}, u32[]{:S(2)}, u32[]{:S(2)}) collective-permute-start(bf16[128,1024]{1,0:T(8,128)(2,1)} %ring_add.16), channel_id=1, source_target_pairs={{0,4},{1,3},{4,8},{5,1},{8,12},{9,5},{12,14},{13,9},{14,10},{15,13... | collective-permute-start | bytes 786440 | tf_op jit(solution)/shard_map/ppermute | solution.py:714
  460.1 36.9 %collective-permute-start.59 = (bf16[128,5376]{1,0:T(8,128)(2,1)S(1)}, bf16[128,5376]{1,0:T(8,128)(2,1)S(1)}, u32[]{:S(2)}, u32[]{:S(2)}) collective-permute-start(bf16[128,5376]{1,0:T(8,128)(2,1)S(1)} %ring_add.17), channel_id=1, source_target_pairs={{0,4},{1,3},{4,8},{5,1},{8,12},{9,5},{12,14},{13,9},{14,10},{15,13... | collective-permute-start | bytes 4128776 | tf_op jit(solution)/shard_map/ppermute | solution.py:714
  463.3 24.7 %collective-permute-start.60 = (bf16[128,2688]{1,0:T(8,128)(2,1)S(1)}, bf16[128,2688]{1,0:T(8,128)(2,1)S(1)}, u32[]{:S(2)}, u32[]{:S(2)}) collective-permute-start(bf16[128,2688]{1,0:T(8,128)(2,1)S(1)} %ring_add.18), channel_id=1, source_target_pairs={{0,4},{1,3},{4,8},{5,1},{8,12},{9,5},{12,14},{13,9},{14,10},{15,13... | collective-permute-start | bytes 2064392 | tf_op jit(solution)/shard_map/ppermute | solution.py:714
  467.7 47.1 %collective-permute-start.62 = (bf16[128,1024]{1,0:T(8,128)(2,1)}, bf16[128,1024]{1,0:T(8,128)(2,1)}, u32[]{:S(2)}, u32[]{:S(2)}) collective-permute-start(bf16[128,1024]{1,0:T(8,128)(2,1)} %ring_add.19), channel_id=1, source_target_pairs={{0,4},{1,3},{4,8},{5,1},{8,12},{9,5},{12,14},{13,9},{14,10},{15,13... | collective-permute-start | bytes 786440 | tf_op jit(solution)/shard_map/ppermute | solution.py:714
  491.2 21.5 %collective-permute-start.69 = (bf16[64,2688]{1,0:T(8,128)(2,1)}, bf16[64,2688]{1,0:T(8,128)(2,1)}, u32[]{:S(2)}, u32[]{:S(2)}) collective-permute-start(bf16[64,2688]{1,0:T(8,128)(2,1)} %dynamic-slice_convert_fusion.2), channel_id=1, source_target_pairs={{0,1},{1,0},{2,3},{3,2},{4,5},{5,4},{6,7},{7,6},{8,9},{9,8},{10,11... | collective-permute-start | bytes 1032200 | tf_op jit(solution)/shard_map/ppermute | solution.py:711
  507.1 38.8 %all-to-all-start.3 = ((bf16[8,64,1024]{2,1,0:T(8,128)(2,1)}), bf16[8,64,1024]{2,1,0:T(8,128)(2,1)}, u32[]{:S(2)}, u32[]{:S(2)}) async-start(bf16[8,64,1024]{2,1,0:T(8,128)(2,1)} %bitcast.180), calls=%async_computation.3 | async-start | bytes 2097152 | tf_op jit(solution)/shard_map/all_to_all | solution.py:731
  518.8 26.2 %collective-permute-start.63 = (bf16[128,3072]{1,0:T(8,128)(2,1)S(1)}, bf16[128,3072]{1,0:T(8,128)(2,1)S(1)}, u32[]{:S(2)}, u32[]{:S(2)}) collective-permute-start(bf16[128,3072]{1,0:T(8,128)(2,1)S(1)} %ring_add.22), channel_id=1, source_target_pairs={{0,4},{1,3},{4,8},{5,1},{8,12},{9,5},{12,14},{13,9},{14,10},{15,13... | collective-permute-start | bytes 2359304 | tf_op jit(solution)/shard_map/ppermute | solution.py:714
  522.4 27.3 %collective-permute-start.66 = (bf16[128,1024]{1,0:T(8,128)(2,1)S(1)}, bf16[128,1024]{1,0:T(8,128)(2,1)}, u32[]{:S(2)}, u32[]{:S(2)}) collective-permute-start(bf16[128,1024]{1,0:T(8,128)(2,1)S(1)} %ring_add.21), channel_id=1, source_target_pairs={{0,4},{1,3},{4,8},{5,1},{8,12},{9,5},{12,14},{13,9},{14,10},{15,13... | collective-permute-start | bytes 786440 | tf_op jit(solution)/shard_map/ppermute | solution.py:714
  523.6 26.0 %collective-permute-start.72 = (f32[2,1024]{1,0:T(2,128)S(1)}, f32[2,1024]{1,0:T(2,128)S(1)}, u32[]{:S(2)}, u32[]{:S(2)}) collective-permute-start(f32[2,1024]{1,0:T(2,128)S(1)} %add.327), channel_id=1, source_target_pairs={{0,4},{1,5},{2,6},{3,7},{4,0},{5,1},{6,2},{7,3},{8,12},{9,13},{10,... | collective-permute-start | bytes 24584 | tf_op jit(solution)/shard_map/ppermute | solution.py:742
  (137 other events, 1794.7 us)
